TPU v7x, 32 devices: a whole 2x2x4 slice. The times are simulated.
32 devices in a mesh: dp: 8 (over y, x, core), fsdp: 4 (over z).
Axes of the slice: x: 2, y: 2, z: 4, core: 2. Of those that a mesh axis runs over, the one named last changes fastest.
Arguments:
- tokens: bfloat16 [256, 128, 768], P(('dp', 'fsdp')), may hold values from -6 to 6
- cotangent: float32 [256, 128, 768], P(('dp', 'fsdp')), may hold values from -6 to 6
- placement: int32 [256], replicated, may hold values from 0 to 255, as said below
- project_weight: bfloat16 [2, 768, 2304], P(None, None, ('dp', 'fsdp')), may hold values from -0.3125 to 0.3125
- project_bias: bfloat16 [2, 1536], P(None, ('dp', 'fsdp')), may hold values from -4 to 4
- output_weight: bfloat16 [2, 768, 768], P(None, None, ('dp', 'fsdp')), may hold values from -0.875 to 0.875
- output_bias: bfloat16 [2, 768], P(None, ('dp', 'fsdp')), may hold values from -4 to 4
- up_weight: bfloat16 [2, 768, 3072], P(None, None, ('dp', 'fsdp')), may hold values from -0.21875 to 0.21875
- up_bias: bfloat16 [2, 3072], P(None, ('dp', 'fsdp')), may hold values from -4 to 4
- down_weight: bfloat16 [2, 3072, 768], P(None, ('dp', 'fsdp')), may hold values from -0.109375 to 0.109375
- down_bias: bfloat16 [2, 768], P(None, ('dp', 'fsdp')), may hold values from -4 to 4
- norm_gain: bfloat16 [2, 2, 768], P(None, None, ('dp', 'fsdp')), may hold values from 0.5 to 1.5
- norm_bias: bfloat16 [2, 2, 768], P(None, None, ('dp', 'fsdp')), may hold values from -4 to 4
- position_table: bfloat16 [64, 768], P(None, ('dp', 'fsdp')), may hold values from -6 to 6
Outputs:
- layer_output: bfloat16 [256, 128, 768], P(('dp', 'fsdp'))
- token_gradient: float32 [256, 128, 768], P(('dp', 'fsdp'))
- project_weight_gradient: float32 [2, 768, 2304], P(None, None, ('dp', 'fsdp'))
- project_bias_gradient: float32 [2, 1536], P(None, ('dp', 'fsdp'))
- output_weight_gradient: float32 [2, 768, 768], P(None, None, ('dp', 'fsdp'))
- output_bias_gradient: float32 [2, 768], P(None, ('dp', 'fsdp'))
- up_weight_gradient: float32 [2, 768, 3072], P(None, None, ('dp', 'fsdp'))
- up_bias_gradient: float32 [2, 3072], P(None, ('dp', 'fsdp'))
- down_weight_gradient: float32 [2, 3072, 768], P(None, ('dp', 'fsdp'))
- down_bias_gradient: float32 [2, 768], P(None, ('dp', 'fsdp'))
- norm_gain_gradient: float32 [2, 2, 768], P(None, None, ('dp', 'fsdp'))
- norm_bias_gradient: float32 [2, 2, 768], P(None, None, ('dp', 'fsdp'))
- position_table_gradient: float32 [64, 768], P(None, ('dp', 'fsdp'))
Inputs may be any that keep to these rules, and one draw needn't show every extreme that they name: placement is a permutation: slot s holds segment placement[s] of the documents laid end to end, first 2 documents of 64 segments, then 8 of 16; slot 0 holds the first segment of a long document and slot 255 the last segment of the same document.
All inputs are finite; a program needn't handle non-finite values.
Results may differ from a plain program's by a relative error of at most 0.03.
Values may be sent and summed in bfloat16 or wider, within the bound.
A program may use at most 320 MiB of HBM per device.

v0:
```python
import jax
import jax.numpy as jnp
from jax import lax
from jax.sharding import PartitionSpec as P

HEADS = 12
HEAD_DIM = 64
SEG_LEN = 128
LONG_SEGS = 64
SHORT_SEGS = 16


highest = lax.Precision.HIGHEST
epsilon = 1e-06
masked_score = -1e30


def document_table(placement):
    long_total = placement.shape[0] // 2
    long_docs = long_total // LONG_SEGS
    is_long = placement < long_total
    remainder = placement - long_total
    doc_ids = jnp.where(is_long, placement // LONG_SEGS, long_docs + remainder // SHORT_SEGS)
    places = jnp.where(is_long, placement % LONG_SEGS, remainder % SHORT_SEGS)
    return (doc_ids, places)


def layer_norm(value, gain, shift):
    centre = jnp.mean(value, -1, keepdims=True)
    offset = value - centre
    spread = jnp.mean(offset * offset, -1, keepdims=True)
    return offset * lax.rsqrt(spread + epsilon) * gain + shift


def gelu_exact(value):
    return jax.nn.gelu(value, approximate=False)


def softmax_rows(scores):
    row_peak = jnp.max(scores, -1, keepdims=True)
    raised = jnp.exp(scores - row_peak)
    return raised / jnp.sum(raised, -1, keepdims=True)


def row_grad(left, right):
    return lax.dot_general(
        left, right, (((0,), (0,)), ((), ())), preferred_element_type=jnp.float32
    )


def back_product(left, right):
    return lax.dot_general(
        left, right, (((1,), (1,)), ((), ())), preferred_element_type=jnp.float32
    )


def column_sums(grad_low):
    return jnp.sum(grad_low.astype(jnp.float32), 0)


def split_heads(matrix):
    return matrix.reshape(matrix.shape[0], HEADS, HEAD_DIM)


def block_params(weights, layer_id):
    (
        project_weight,
        project_bias,
        output_weight,
        output_bias,
        up_weight,
        up_bias,
        down_weight,
        down_bias,
        norm_gain,
        norm_bias,
        position_table,
    ) = weights
    model_width = output_weight.shape[1]
    bias_pair = project_bias[layer_id].astype(jnp.float32)
    full_bias = jnp.concatenate(
        [bias_pair[:model_width], jnp.zeros((model_width,), jnp.float32), bias_pair[model_width:]]
    )
    return (
        project_weight[layer_id],
        full_bias,
        output_weight[layer_id],
        output_bias[layer_id].astype(jnp.float32),
        up_weight[layer_id],
        up_bias[layer_id].astype(jnp.float32),
        down_weight[layer_id],
        down_bias[layer_id].astype(jnp.float32),
        norm_gain[layer_id].astype(jnp.float32),
        norm_bias[layer_id].astype(jnp.float32),
    )


def run_forward(inputs, params, attend):
    (
        project_weight,
        full_bias,
        output_weight,
        output_bias,
        up_weight,
        up_bias,
        down_weight,
        down_bias,
        gains,
        shifts,
    ) = params
    inputs_low = inputs.astype(jnp.bfloat16)
    projected = (
        jnp.dot(inputs_low, project_weight, preferred_element_type=jnp.float32) + full_bias
    ).astype(jnp.bfloat16)
    attended, kept_state = attend(projected)
    attended_low = attended.astype(jnp.bfloat16)
    first_sum = inputs + (
        jnp.dot(attended_low, output_weight, preferred_element_type=jnp.float32) + output_bias
    )
    normed = layer_norm(first_sum, gains[0], shifts[0])
    normed_low = normed.astype(jnp.bfloat16)
    pre_act = jnp.dot(normed_low, up_weight, preferred_element_type=jnp.float32) + up_bias
    hidden_low = gelu_exact(pre_act).astype(jnp.bfloat16)
    second = normed + (
        jnp.dot(hidden_low, down_weight, preferred_element_type=jnp.float32) + down_bias
    )
    output = layer_norm(second, gains[1], shifts[1])
    return (
        output,
        (
            inputs_low,
            projected,
            attended_low,
            first_sum,
            normed_low,
            pre_act,
            hidden_low,
            second,
            kept_state,
        ),
    )


def run_backward(grad_out, kept_values, params, attend_back):
    (
        project_weight,
        full_bias,
        output_weight,
        output_bias,
        up_weight,
        up_bias,
        down_weight,
        down_bias,
        gains,
        shifts,
    ) = params
    (
        inputs_low,
        projected,
        attended_low,
        first_sum,
        normed_low,
        pre_act,
        hidden_low,
        second,
        kept_state,
    ) = kept_values
    model_width = output_weight.shape[1]
    norm_pull = jax.vjp(layer_norm, second, gains[1], shifts[1])[1]
    grad_second, gain_two, shift_two = norm_pull(grad_out)
    down_low = grad_second.astype(jnp.bfloat16)
    grad_down = row_grad(hidden_low, down_low)
    gelu_pull = jax.vjp(gelu_exact, pre_act)[1]
    up_low = gelu_pull(back_product(down_low, down_weight))[0].astype(jnp.bfloat16)
    grad_up = row_grad(normed_low, up_low)
    grad_normed = grad_second + back_product(up_low, up_weight)
    norm_pull = jax.vjp(layer_norm, first_sum, gains[0], shifts[0])[1]
    grad_first, gain_one, shift_one = norm_pull(grad_normed)
    branch_low = grad_first.astype(jnp.bfloat16)
    grad_output = row_grad(attended_low, branch_low)
    mixed_low = back_product(branch_low, output_weight).astype(jnp.bfloat16)
    project_low = attend_back(mixed_low, projected, kept_state).astype(jnp.bfloat16)
    grad_project = row_grad(inputs_low, project_low)
    sums_project = column_sums(project_low)
    grad_pair = jnp.concatenate([sums_project[:model_width], sums_project[2 * model_width :]])
    grad_inputs = grad_first + back_product(project_low, project_weight)
    gradients = (
        grad_project,
        grad_pair,
        grad_output,
        column_sums(branch_low),
        grad_up,
        column_sums(up_low),
        grad_down,
        column_sums(down_low),
        jnp.stack([gain_one, gain_two]),
        jnp.stack([shift_one, shift_two]),
    )
    return (grad_inputs, gradients)


def segment_parts(projected):
    grid = projected.reshape(projected.shape[0] // SEG_LEN, SEG_LEN, 3, HEADS, HEAD_DIM)
    return (grid[:, :, 0], grid[:, :, 1], grid[:, :, 2])


def segment_shares(queries, key_rows):
    scores = jnp.einsum(
        "glhd,gmhd->ghlm", queries, key_rows, preferred_element_type=jnp.float32
    ) * HEAD_DIM ** (-0.5)
    return softmax_rows(scores)


def segment_attend(projected):
    queries, key_rows, values = segment_parts(projected)
    shares = segment_shares(queries, key_rows)
    attended = jnp.einsum(
        "ghlm,gmhd->glhd", shares.astype(jnp.bfloat16), values, preferred_element_type=jnp.float32
    )
    return (attended.reshape(projected.shape[0], -1), None)


def segment_back(mixed_low, projected, kept_state):
    queries, key_rows, values = segment_parts(projected)
    shares = segment_shares(queries, key_rows)
    grad_low = mixed_low.reshape(queries.shape)
    grad_shares = jnp.einsum(
        "glhd,gmhd->ghlm", grad_low, values, preferred_element_type=jnp.float32
    )
    row_dot = jnp.sum(shares * grad_shares, -1, keepdims=True)
    score_low = (shares * (grad_shares - row_dot)).astype(jnp.bfloat16)
    grad_queries = jnp.einsum(
        "ghlm,gmhd->glhd", score_low, key_rows, preferred_element_type=jnp.float32
    ) * HEAD_DIM ** (-0.5)
    grad_keys = jnp.einsum(
        "ghlm,glhd->gmhd", score_low, queries, preferred_element_type=jnp.float32
    ) * HEAD_DIM ** (-0.5)
    grad_values = jnp.einsum(
        "ghlm,glhd->gmhd", shares.astype(jnp.bfloat16), grad_low, preferred_element_type=jnp.float32
    )
    return jnp.stack([grad_queries, grad_keys, grad_values], 2).reshape(projected.shape)


def cross_shares(queries, key_rows, same_doc):
    scores = jnp.einsum(
        "rhd,shd->hrs", queries, key_rows, preferred_element_type=jnp.float32
    ) * HEAD_DIM ** (-0.5)
    scores = jnp.where(same_doc[None], scores, masked_score)
    row_peak = jnp.max(scores, -1, keepdims=True)
    raised = jnp.exp(scores - row_peak)
    total = jnp.sum(raised, -1, keepdims=True)
    return (raised / total, row_peak + jnp.log(total))


def shards(
    tokens,
    cotangent,
    placement,
    project_weight,
    project_bias,
    output_weight,
    output_bias,
    up_weight,
    up_bias,
    down_weight,
    down_bias,
    norm_gain,
    norm_bias,
    position_table,
):
    gathered = (
        lax.all_gather(project_weight, ("dp", "fsdp"), axis=2, tiled=True),
        lax.all_gather(project_bias, ("dp", "fsdp"), axis=1, tiled=True),
        lax.all_gather(output_weight, ("dp", "fsdp"), axis=2, tiled=True),
        lax.all_gather(output_bias, ("dp", "fsdp"), axis=1, tiled=True),
        lax.all_gather(up_weight, ("dp", "fsdp"), axis=2, tiled=True),
        lax.all_gather(up_bias, ("dp", "fsdp"), axis=1, tiled=True),
        lax.all_gather(down_weight, ("dp", "fsdp"), axis=1, tiled=True),
        lax.all_gather(down_bias, ("dp", "fsdp"), axis=1, tiled=True),
        lax.all_gather(norm_gain, ("dp", "fsdp"), axis=2, tiled=True),
        lax.all_gather(norm_bias, ("dp", "fsdp"), axis=2, tiled=True),
        lax.all_gather(position_table, ("dp", "fsdp"), axis=1, tiled=True),
    )
    seg_count, seg_len, model_width = tokens.shape
    inputs = tokens.reshape(seg_count * seg_len, model_width).astype(jnp.float32)
    doc_ids, places = document_table(placement)
    first_slot = lax.axis_index(("dp", "fsdp")) * seg_count
    my_docs = lax.dynamic_slice_in_dim(doc_ids, first_slot, seg_count)
    my_places = lax.dynamic_slice_in_dim(places, first_slot, seg_count)
    same_doc = my_docs[:, None] == doc_ids[None, :]
    picker = my_places[:, None] == jnp.arange(position_table.shape[0], dtype=jnp.int32)[None, :]

    def cross_attend(projected):
        queries = split_heads(projected[:, :model_width])
        key_rows, values = (
            lax.all_gather(
                projected[:, model_width : 2 * model_width], ("dp", "fsdp"), axis=0, tiled=True
            ),
            lax.all_gather(projected[:, 2 * model_width :], ("dp", "fsdp"), axis=0, tiled=True),
        )
        shares, log_total = cross_shares(queries, split_heads(key_rows), same_doc)
        attended = jnp.einsum(
            "hrs,shd->rhd",
            shares.astype(jnp.bfloat16),
            split_heads(values),
            preferred_element_type=jnp.float32,
        )
        return (attended.reshape(projected.shape[0], model_width), (key_rows, values, log_total))

    def cross_back(mixed_low, projected, kept_state):
        key_rows, values, log_total = kept_state
        queries = split_heads(projected[:, :model_width])
        grad_heads = split_heads(mixed_low)
        shares, unused = cross_shares(queries, split_heads(key_rows), same_doc)
        grad_shares = jnp.einsum(
            "rhd,shd->hrs", grad_heads, split_heads(values), preferred_element_type=jnp.float32
        )
        row_dot = jnp.sum(shares * grad_shares, -1, keepdims=True)
        score_low = (shares * (grad_shares - row_dot)).astype(jnp.bfloat16)
        grad_queries = jnp.einsum(
            "hrs,shd->rhd", score_low, split_heads(key_rows), preferred_element_type=jnp.float32
        ) * HEAD_DIM ** (-0.5)
        grad_keys_all = jnp.einsum(
            "hrs,rhd->shd", score_low, queries, preferred_element_type=jnp.float32
        ) * HEAD_DIM ** (-0.5)
        grad_values_all = jnp.einsum(
            "hrs,rhd->shd",
            shares.astype(jnp.bfloat16),
            grad_heads,
            preferred_element_type=jnp.float32,
        )
        grad_keys, grad_values = (
            lax.psum_scatter(
                grad_keys_all.reshape(-1, model_width),
                ("dp", "fsdp"),
                scatter_dimension=0,
                tiled=True,
            ),
            lax.psum_scatter(
                grad_values_all.reshape(-1, model_width),
                ("dp", "fsdp"),
                scatter_dimension=0,
                tiled=True,
            ),
        )
        return jnp.concatenate([grad_queries.reshape(-1, model_width), grad_keys, grad_values], 1)

    seg_out, unused_kept = run_forward(inputs, block_params(gathered, 0), segment_attend)
    seg_grid = seg_out.reshape(seg_count, seg_len, model_width)
    position_rows = jnp.dot(
        picker.astype(jnp.bfloat16), gathered[10], preferred_element_type=jnp.float32
    )
    cls_in = seg_grid[:, 0, :] + position_rows
    cross_out, cross_kept = run_forward(cls_in, block_params(gathered, 1), cross_attend)
    layer_output = seg_grid.at[:, 0, :].set(cross_out).astype(jnp.bfloat16)
    weights_back = (
        lax.all_gather(project_weight, ("dp", "fsdp"), axis=2, tiled=True),
        lax.all_gather(project_bias, ("dp", "fsdp"), axis=1, tiled=True),
        lax.all_gather(output_weight, ("dp", "fsdp"), axis=2, tiled=True),
        lax.all_gather(output_bias, ("dp", "fsdp"), axis=1, tiled=True),
        lax.all_gather(up_weight, ("dp", "fsdp"), axis=2, tiled=True),
        lax.all_gather(up_bias, ("dp", "fsdp"), axis=1, tiled=True),
        lax.all_gather(down_weight, ("dp", "fsdp"), axis=1, tiled=True),
        lax.all_gather(down_bias, ("dp", "fsdp"), axis=1, tiled=True),
        lax.all_gather(norm_gain, ("dp", "fsdp"), axis=2, tiled=True),
        lax.all_gather(norm_bias, ("dp", "fsdp"), axis=2, tiled=True),
        lax.all_gather(position_table, ("dp", "fsdp"), axis=1, tiled=True),
    )
    grad_cls, cross_gradients = run_backward(
        cotangent[:, 0, :], cross_kept, block_params(weights_back, 1), cross_back
    )
    position_gradient = lax.dot_general(
        picker.astype(jnp.float32), grad_cls, (((0,), (0,)), ((), ())), precision=highest
    )
    grad_rows = cotangent.at[:, 0, :].set(grad_cls).reshape(-1, model_width)
    seg_params = block_params(weights_back, 0)
    unused_out, seg_kept = run_forward(inputs, seg_params, segment_attend)
    grad_inputs, seg_gradients = run_backward(grad_rows, seg_kept, seg_params, segment_back)
    stacked = [
        jnp.stack([seg_grad, cross_grad])
        for seg_grad, cross_grad in zip(seg_gradients, cross_gradients)
    ]
    owned = (
        lax.psum_scatter(stacked[0], ("dp", "fsdp"), scatter_dimension=2, tiled=True),
        lax.psum_scatter(stacked[1], ("dp", "fsdp"), scatter_dimension=1, tiled=True),
        lax.psum_scatter(stacked[2], ("dp", "fsdp"), scatter_dimension=2, tiled=True),
        lax.psum_scatter(stacked[3], ("dp", "fsdp"), scatter_dimension=1, tiled=True),
        lax.psum_scatter(stacked[4], ("dp", "fsdp"), scatter_dimension=2, tiled=True),
        lax.psum_scatter(stacked[5], ("dp", "fsdp"), scatter_dimension=1, tiled=True),
        lax.psum_scatter(stacked[6], ("dp", "fsdp"), scatter_dimension=1, tiled=True),
        lax.psum_scatter(stacked[7], ("dp", "fsdp"), scatter_dimension=1, tiled=True),
        lax.psum_scatter(stacked[8], ("dp", "fsdp"), scatter_dimension=2, tiled=True),
        lax.psum_scatter(stacked[9], ("dp", "fsdp"), scatter_dimension=2, tiled=True),
        lax.psum_scatter(position_gradient, ("dp", "fsdp"), scatter_dimension=1, tiled=True),
    )
    return (layer_output, grad_inputs.reshape(tokens.shape)) + tuple(owned)


def solution(mesh):
    placed = (
        P(("dp", "fsdp"), None, None),
        P(("dp", "fsdp"), None, None),
        P(),
        P(None, None, ("dp", "fsdp")),
        P(None, ("dp", "fsdp")),
        P(None, None, ("dp", "fsdp")),
        P(None, ("dp", "fsdp")),
        P(None, None, ("dp", "fsdp")),
        P(None, ("dp", "fsdp")),
        P(None, ("dp", "fsdp"), None),
        P(None, ("dp", "fsdp")),
        P(None, None, ("dp", "fsdp")),
        P(None, None, ("dp", "fsdp")),
        P(None, ("dp", "fsdp")),
    )
    return jax.shard_map(
        shards,
        mesh=mesh,
        in_specs=placed,
        out_specs=(
            P(("dp", "fsdp"), None, None),
            P(("dp", "fsdp"), None, None),
            P(None, None, ("dp", "fsdp")),
            P(None, ("dp", "fsdp")),
            P(None, None, ("dp", "fsdp")),
            P(None, ("dp", "fsdp")),
            P(None, None, ("dp", "fsdp")),
            P(None, ("dp", "fsdp")),
            P(None, ("dp", "fsdp"), None),
            P(None, ("dp", "fsdp")),
            P(None, None, ("dp", "fsdp")),
            P(None, None, ("dp", "fsdp")),
            P(None, ("dp", "fsdp")),
        ),
        check_vma=False,
    )
```

profile of v0, /device:TPU:0, one launch (start us, length us, event | category | flops | bytes accessed | tf_op | source)
XLA Modules:
  0.0 2087.6 jit_solution(4171634446820557824)
XLA Ops:
  11.8 69.6 %all-gather = bf16[32,48,2]{1,2,0:T(2,128)(2,1)S(1)} all-gather(bf16[1,48,2]{1,2,0:T(2,128)(2,1)S(1)} %bitcast.303), channel_id=1, replica_groups=mesh['dp'=8,'fsdp'=4] {'dp','fsdp'}, dimensions={0}, use_global_device_ids=true | all-gather | bytes 6336 | tf_op jit(solution)/shard_map/all_gather | solution.py:273
  81.5 63.1 %all-gather.1 = bf16[32,24,2]{1,2,0:T(2,128)(2,1)S(1)} all-gather(bf16[1,24,2]{1,2,0:T(2,128)(2,1)S(1)} %bitcast.304), channel_id=1, replica_groups=mesh['dp'=8,'fsdp'=4] {'dp','fsdp'}, dimensions={0}, use_global_device_ids=true | all-gather | bytes 3168 | tf_op jit(solution)/shard_map/all_gather | solution.py:275
  144.8 65.7 %all-gather.2 = bf16[32,96,2]{1,2,0:T(2,128)(2,1)S(1)} all-gather(bf16[1,96,2]{1,2,0:T(2,128)(2,1)S(1)} %bitcast.305), channel_id=1, replica_groups=mesh['dp'=8,'fsdp'=4] {'dp','fsdp'}, dimensions={0}, use_global_device_ids=true | all-gather | bytes 12672 | tf_op jit(solution)/shard_map/all_gather | solution.py:277
  210.5 63.3 %all-gather.3 = bf16[32,24,2]{1,2,0:T(2,128)(2,1)S(1)} all-gather(bf16[1,24,2]{1,2,0:T(2,128)(2,1)S(1)} %bitcast.306), channel_id=1, replica_groups=mesh['dp'=8,'fsdp'=4] {'dp','fsdp'}, dimensions={0}, use_global_device_ids=true | all-gather | bytes 3168 | tf_op jit(solution)/shard_map/all_gather | solution.py:279
  273.9 71.6 %all_gather.54 = bf16[2,2,768]{1,0,2:T(2,128)(2,1)S(1)} all-gather(bf16[2,2,24]{1,0,2:T(2,128)(2,1)S(1)} %copy.132), channel_id=1, replica_groups=mesh['dp'=8,'fsdp'=4] {'dp','fsdp'}, dimensions={2}, use_global_device_ids=true | all-gather | bytes 6336 | tf_op jit(solution)/shard_map/all_gather | solution.py:281
  345.5 66.8 %all_gather.53 = bf16[2,2,768]{1,0,2:T(2,128)(2,1)S(1)} all-gather(bf16[2,2,24]{1,0,2:T(2,128)(2,1)S(1)} %copy.131), channel_id=1, replica_groups=mesh['dp'=8,'fsdp'=4] {'dp','fsdp'}, dimensions={2}, use_global_device_ids=true | all-gather | bytes 6336 | tf_op jit(solution)/shard_map/all_gather | solution.py:280
  412.3 66.7 %all_gather.59 = bf16[64,768]{0,1:T(8,128)(2,1)S(1)} all-gather(bf16[64,24]{0,1:T(8,128)(2,1)S(1)} %copy-done.47), channel_id=1, replica_groups=mesh['dp'=8,'fsdp'=4] {'dp','fsdp'}, dimensions={1}, use_global_device_ids=true | all-gather | bytes 101376 | tf_op jit(solution)/shard_map/all_gather | solution.py:282
  482.1 9.5 slice_reduce_fusion.1
  491.5 9.9 slice_reduce_fusion
  501.6 8.5 add_convert_fusion.1
  510.0 6.7 copy.124
  516.7 3.6 copy.184
  523.4 5.9 fusion.107
  534.4 3.8 fusion.108
  538.8 36.9 %multiply_convert_fusion = (bf16[1024,3072]{1,0:T(8,128)(2,1)}, f32[1024,3072]{1,0:T(8,128)}, f32[1024,3072]{1,0:T(8,128)}) fusion(f32[3072]{0:T(1024)S(1)} %bitcast.299, bf16[2,768,3072]{1,2,0:T(8,128)(2,1)} %all-gather.13.cloned.1.call-done, f32[1024,768]{1,0:T(8,128)S(1)} %get-tuple-element.169, f32[768]{0:T(1024)S(1)} %get-tuple-element.191, ...), kind=kOutput, calls=%fused_computation.9 | convolution fusion | flops 5043388416 | bytes 39348224 | tf_op jit(solution)/shard_map/dot_general | solution.py:122
  575.8 9.0 fusion.109
  591.6 67.0 %all_gather.61 = bf16[256,768]{1,0:T(8,128)(2,1)S(1)} all-gather(bf16[8,768]{1,0:T(8,128)(2,1)S(1)} %get-tuple-element.151), channel_id=1, replica_groups=mesh['dp'=8,'fsdp'=4] {'dp','fsdp'}, dimensions={0}, use_global_device_ids=true | all-gather | bytes 405504 | tf_op jit(solution)/shard_map/all_gather | solution.py:296
  661.1 68.5 %all_gather.60 = bf16[256,768]{1,0:T(8,128)(2,1)S(1)} all-gather(bf16[8,768]{1,0:T(8,128)(2,1)S(1)} %get-tuple-element.152), channel_id=1, replica_groups=mesh['dp'=8,'fsdp'=4] {'dp','fsdp'}, dimensions={0}, use_global_device_ids=true | all-gather | bytes 405504 | tf_op jit(solution)/shard_map/all_gather | solution.py:299
  732.2 3.8 fusion.23
  736.1 3.5 fusion.112
  741.9 3.8 convert_reduce_fusion.4
  754.3 5.2 convolution_bitcast_fusion.2
  759.5 82.2 %reduce-scatter.20.cloned.1.call-done = f32[8,768]{1,0:T(8,128)} async-done(((f32[256,768]{1,0:T(8,128)}), f32[8,768]{1,0:T(8,128)}) %reduce-scatter.20.cloned.1.call-update) | async-done | bytes 24592 | tf_op jit(solution)/shard_map/reduce_scatter | solution.py:339
  842.5 98.7 %reduce-scatter.18.cloned.1.call-done = f32[8,768]{1,0:T(8,128)} async-done(((f32[256,768]{1,0:T(8,128)}), f32[8,768]{1,0:T(8,128)}) %reduce-scatter.18.cloned.1.call-update) | async-done | bytes 24592 | tf_op jit(solution)/shard_map/reduce_scatter | solution.py:333
  944.8 5.2 fusion.25
  953.7 16.9 convert_reduce_fusion
  970.6 10.8 convolution_bitcast_fusion.3
  981.4 8.2 multiply_reduce_fusion.2
  1003.9 5.2 fusion.40
  1009.2 4.1 multiply_reduce_fusion
  1013.3 5.0 multiply_convert_fusion.1
  1028.0 14.4 pad_maximum_fusion
  1044.7 8.2 copy.157
  1053.0 28.3 %copy.158 = f32[2,768,3072]{1,0,2:T(2,128)} copy(f32[2,768,3072]{2,1,0:T(8,128)} %pad_maximum_fusion) | data formatting | bytes 37748736 | tf_op jit(solution)/shard_map/stack | solution.py:380
  1081.3 13.9 copy.155
  1095.2 4.0 convolution_bitcast_fusion.4
  1100.5 8.5 convolution_bitcast_fusion.5
  1109.0 10.9 pad_maximum_fusion.2
  1122.3 7.3 convolution_bitcast_fusion.1
  1129.6 6.7 pad_maximum_fusion.1
  1139.0 3.2 convert_element_type.202
  1142.7 40.8 %all-reduce.7 = (f32[2,768]{1,0:T(2,128)S(1)}, f32[2,768]{1,0:T(2,128)S(1)}, f32[2,2,768]{2,1,0:T(2,128)S(1)}, f32[2,2,768]{2,1,0:T(2,128)S(1)}) all-reduce(f32[2,768]{1,0:T(2,128)S(1)} %pad_maximum_fusion.14, f32[2,768]{1,0:T(2,128)S(1)} %pad_maximum_fusion.15, ...), channel_id=7, replica_groups=mesh['dp'=8,'fsdp'=4] {'dp','fsdp'}, use_global_device_ids=true, to_apply=%region_31.32.clone | all-reduce | flops 9216 | bytes 73728
  1186.1 9.9 add_add_fusion.4
  1197.5 24.9 %reduce-scatter.28.cloned.1.call-done = f32[96,2]{1,0:T(8,128)} async-done(((f32[3072,2]{1,0:T(8,128)}), f32[96,2]{1,0:T(8,128)}) %reduce-scatter.28.cloned.1.call-update) | async-done | bytes 784
  1223.8 375.8 %all-reduce.11.cloned.1.call-done = (f32[2,768,768]{1,0,2:T(2,128)}, f32[2,768,3072]{1,0,2:T(2,128)}) async-done(((f32[2,768,768]{1,0,2:T(2,128)}, f32[2,768,3072]{1,0,2:T(2,128)}), (f32[2,768,768]{1,0,2:T(2,128)}, f32[2,768,3072]{1,0,2:T(2,128)})) %all-reduce.11.cloned.1.call-update) | async-done | bytes 23592976
  1603.1 96.0 %reduce-scatter.30.cloned.1.call-done = f32[64,24]{0,1:T(8,128)} async-done(((f32[64,768]{0,1:T(8,128)}), f32[64,24]{0,1:T(8,128)}) %reduce-scatter.30.cloned.1.call-update) | async-done | bytes 6160
  1699.1 169.6 %reduce-scatter.22.cloned.1.call-done = f32[2,768,72]{1,2,0:T(8,128)} async-done(((f32[2,768,2304]{1,2,0:T(8,128)}), f32[2,768,72]{1,2,0:T(8,128)}) %reduce-scatter.22.cloned.1.call-update) | async-done | bytes 442384 | tf_op jit(solution)/shard_map/reduce_scatter | solution.py:384
  1868.8 211.8 %reduce-scatter.24.cloned.1.call-done = f32[2,96,768]{2,1,0:T(8,128)} async-done(((f32[2,3072,768]{2,1,0:T(8,128)}), f32[2,96,768]{2,1,0:T(8,128)}) %reduce-scatter.24.cloned.1.call-update) | async-done | bytes 589840 | tf_op jit(solution)/shard_map/reduce_scatter | solution.py:390
  (301 shorter events, 89.2 us)
Async XLA Ops:
  7.2 74.3 %copy-start.53 = (bf16[2,24]{1,0:T(2,128)(2,1)S(1)}, bf16[2,24]{1,0:T(2,128)(2,1)}, u32[]{:S(2)}) copy-start(bf16[2,24]{1,0:T(2,128)(2,1)} %param.24) | copy-start | bytes 292
  7.2 137.6 %copy-start.54 = (bf16[2,96]{1,0:T(2,128)(2,1)S(1)}, bf16[2,96]{1,0:T(2,128)(2,1)}, u32[]{:S(2)}) copy-start(bf16[2,96]{1,0:T(2,128)(2,1)} %param.26) | copy-start | bytes 1156
  7.2 203.3 %copy-start.55 = (bf16[2,24]{1,0:T(2,128)(2,1)S(1)}, bf16[2,24]{1,0:T(2,128)(2,1)}, u32[]{:S(2)}) copy-start(bf16[2,24]{1,0:T(2,128)(2,1)} %param.28) | copy-start | bytes 292
  7.3 405.0 %copy-start.47 = (bf16[64,24]{0,1:T(8,128)(2,1)S(1)}, bf16[64,24]{0,1:T(8,128)(2,1)}, u32[]{:S(2)}) copy-start(bf16[64,24]{0,1:T(8,128)(2,1)} %param.31) | copy-start | bytes 9220
  7.3 494.3 %all-gather.9.cloned.1.call-start = ((), (), s32[]{:S(2)}) async-start(), calls=%async_computation.7 | async-start | bytes 7299072 | tf_op jit(solution)/shard_map/all_gather | solution.py:272
  9.2 500.8 %copy-start = (f32[8,128,768]{2,1,0:T(8,128)}, f32[8,128,768]{2,1,0:T(8,128)S(1)}, u32[]{:S(2)}) copy-start(f32[8,128,768]{2,1,0:T(8,128)S(1)} %copy.253) | copy-start | bytes 9437188
  9.2 525.2 %all-gather.11.cloned.1.call-start = ((), (), s32[]{:S(2)}) async-start(), calls=%async_computation.8 | async-start | bytes 2433024 | tf_op jit(solution)/shard_map/all_gather | solution.py:274
  10.0 528.9 %all-gather.13.cloned.1.call-start = ((), (), s32[]{:S(2)}) async-start(), calls=%async_computation.9 | async-start | bytes 9732096 | tf_op jit(solution)/shard_map/all_gather | solution.py:276
  10.7 565.1 %all-gather.15.cloned.1.call-start = ((), (), s32[]{:S(2)}) async-start(), calls=%async_computation.10 | async-start | bytes 9732096 | tf_op jit(solution)/shard_map/all_gather | solution.py:278
  11.3 830.5 %reduce-scatter.20.cloned.1.call-start = ((), (), s32[]{:S(2)}) async-start(), calls=%async_computation.12 | async-start | bytes 811008 | tf_op jit(solution)/shard_map/reduce_scatter | solution.py:339
  520.7 8.7 copy-start.22
  538.3 37.5 %copy-start.6 = (f32[1024,768]{1,0:T(8,128)}, f32[1024,768]{1,0:T(8,128)S(1)}, u32[]{:S(2)}) copy-start(f32[1024,768]{1,0:T(8,128)S(1)} %get-tuple-element.169) | copy-start | bytes 9437188
  538.8 37.0 %copy-start.36 = (f32[1024]{0:T(1024)}, f32[1024]{0:T(1024)S(1)}, u32[]{:S(2)}) copy-start(f32[1024]{0:T(1024)S(1)} %multiply_reduce_fusion.6) | copy-start | bytes 12292
  588.3 157.5 %slice-start.2 = ((s8[9437184]{0:T(1024)(128)(4,1)}), s8[1048576]{0:T(1024)(128)(4,1)S(1)}, s32[]{:S(2)}) async-start(s8[9437184]{0:T(1024)(128)(4,1)} %bitcast.274), calls=%async_computation.21 | async-start | bytes 2097152
  658.6 77.5 %copy-start.48 = (f32[768]{0:T(1024)S(1)}, f32[768]{0:T(1024)}, u32[]{:S(2)}) copy-start(f32[768]{0:T(1024)} %get-tuple-element.111) | copy-start | bytes 9220
  732.2 7.6 copy-start.31
  732.2 7.6 copy-start.35
  732.2 8.2 copy-start.41
  732.2 13.6 slice-start.3
  736.0 9.7 copy-start.27
  736.0 9.8 slice-start.4
  741.9 5.3 copy-start.33
  741.9 6.2 copy-start.19
  750.1 191.1 %reduce-scatter.18.cloned.1.call-start = ((), (), s32[]{:S(2)}) async-start(), calls=%async_computation.11 | async-start | bytes 811008 | tf_op jit(solution)/shard_map/reduce_scatter | solution.py:333
  752.0 444.0 %reduce-scatter.26.cloned.1.call-start = ((), (), s32[]{:S(2)}) async-start(), calls=%async_computation.15 | async-start | bytes 811008
  754.3 190.3 %copy-start.1 = (f32[8,128,768]{2,1,0:T(8,128)S(1)}, f32[8,128,768]{2,1,0:T(8,128)}, u32[]{:S(2)}) copy-start(f32[8,128,768]{2,1,0:T(8,128)} %copy-done) | copy-start | bytes 9437188
  944.8 7.2 copy-start.2
  953.2 17.3 copy-start.25
  953.7 16.9 copy-start.7
  970.6 10.9 copy-start.16
  970.6 10.9 copy-start.18
  981.4 8.2 copy-start.37
  991.3 5.4 copy-start.14
  999.3 9.8 slice-start
  1026.1 196.2 %reduce-scatter.28.cloned.1.call-start = ((), (), s32[]{:S(2)}) async-start(), calls=%async_computation.16 | async-start | bytes 1622016
  1027.9 14.4 copy-start.17
  1027.9 571.7 %all-reduce.11.cloned.1.call-start = ((), (), s32[]{:S(2)}) async-start(), calls=%async_computation.18 | async-start | bytes 47185920
  1027.9 14.4 copy-start.21
  1081.2 617.9 %reduce-scatter.30.cloned.1.call-start = ((), (), s32[]{:S(2)}) async-start(), calls=%async_computation.17 | async-start | bytes 405504
  1095.2 5.3 copy-start.56
  1109.0 759.8 %reduce-scatter.22.cloned.1.call-start = ((), (), s32[]{:S(2)}) async-start(), calls=%async_computation.13 | async-start | bytes 14598144 | tf_op jit(solution)/shard_map/reduce_scatter | solution.py:384
  1120.0 960.6 %reduce-scatter.24.cloned.1.call-start = ((), (), s32[]{:S(2)}) async-start(), calls=%async_computation.14 | async-start | bytes 19464192 | tf_op jit(solution)/shard_map/reduce_scatter | solution.py:390
  1136.3 5.9 copy-start.39
  1136.3 5.9 copy-start.38
  1136.3 5.9 copy-start.45
  1136.3 6.0 copy-start.3
  1136.3 6.2 copy-start.46
  1136.3 6.2 copy-start.40
  (26 other events, 70.5 us)
Sparse Core Ops, SparseCore 0:
  11.2 75.3 all-gather.8
  89.6 55.9 all-gather.10
  148.7 80.9 all-gather.12
  232.6 82.4 all-gather.14
  750.2 91.4 reduce-scatter.19
  846.7 94.4 reduce-scatter.17
  1026.2 94.5 reduce-scatter.25
  1126.0 96.2 reduce-scatter.27
  1228.8 370.7 all-reduce.10
  1604.9 94.1 reduce-scatter.29
  1706.7 161.9 reduce-scatter.21
  1876.7 203.7 reduce-scatter.23
where the time goes:
time: 2100 us; the launch traced here: 2090 us
  waiting for transfers between devices  1060 us (50%)
  blocking collectives  643 us (31%)
  matrix products  176 us (8%)
  local copies, waits for them, and re-layouts  117 us (6%)
  other arithmetic  74.2 us (4%)
    unnamed x16, waiting for transfers between devices  499 us
    reduce_scatter x1, waiting for transfers between devices, shards(): lax.psum_scatter(stacked[6], ('dp', 'fsdp'), scatter_dimension=1, tiled=T...  212 us
    reduce_scatter x1, waiting for transfers between devices, shards(): lax.psum_scatter(stacked[0], ('dp', 'fsdp'), scatter_dimension=2, tiled=T...  170 us
    reduce_scatter x1, waiting for transfers between devices, cross_back(): lax.psum_scatter(grad_keys_all.reshape(-1, model_width), ('dp', 'fsdp'),...  98.7 us
    reduce_scatter x1, waiting for transfers between devices, cross_back(): lax.psum_scatter(grad_values_all.reshape(-1, model_width), ('dp', 'fsdp')...  82.2 us
    all_gather x1, blocking collectives, shards(): lax.all_gather(norm_bias, ('dp', 'fsdp'), axis=2, tiled=True)  71.6 us
    all_gather x1, blocking collectives, shards(): lax.all_gather(project_bias, ('dp', 'fsdp'), axis=1, tiled=True)  69.6 us
    all_gather x1, blocking collectives, cross_attend(): lax.all_gather(projected[:, 2 * model_width:], ('dp', 'fsdp'), axis=0, ti...  68.5 us
  transfers between devices with their start and end apart: 12, of which 7 were waited for; matrix products, arithmetic and copies ran while one was open for 11% of the time, Pallas kernels for 0%

commit v1 on v0

v1 whole, which is shorter than its diff:
```python
import functools
import math

import jax
import jax.numpy as jnp
from jax import lax
from jax.experimental import pallas as pl
from jax.experimental.pallas import tpu as pltpu
from jax.sharding import PartitionSpec as P

HEADS = 12
HEAD_DIM = 64
SEG_LEN = 128
LONG_SEGS = 64
SHORT_SEGS = 16
MESH = pl.DeviceIdType.MESH
AXES = ("dp", "fsdp")

highest = lax.Precision.HIGHEST
epsilon = 1e-06
masked_score = -1e30


class Grid:
    def __init__(self, mesh):
        self.dp, self.fsdp = mesh.shape["dp"], mesh.shape["fsdp"]
        twos = int(math.log2(self.dp))
        self.dims = (2,) * twos + (self.fsdp,)
        self.n = self.dp * self.fsdp
        self.last = len(self.dims) - 1

    def coords(self):
        dp, fs = lax.axis_index("dp"), lax.axis_index("fsdp")
        twos = self.last
        return tuple((dp // 2 ** (twos - 1 - i)) % 2 for i in range(twos)) + (fs,)

    def peer(self, coords, dim, step):
        other = list(coords)
        other[dim] = lax.rem(coords[dim] + step, self.dims[dim])
        dp = 0
        for value in other[:-1]:
            dp = dp * 2 + value
        return (dp, other[-1]), other[dim]

    def greet(self, coords):
        barrier = pltpu.get_barrier_semaphore()
        count = 0
        for dim, size in enumerate(self.dims):
            for step in range(1, size):
                where, unused = self.peer(coords, dim, step)
                pl.semaphore_signal(barrier, inc=1, device_id=where, device_id_type=MESH)
                count += 1
        pl.semaphore_wait(barrier, count)

    def orders(self):
        middle = list(range(self.last - 1))
        return (
            [self.last] + middle[::-1] + [self.last - 1],
            [self.last] + middle + [self.last - 1],
        )


def index_of(coords, free, ndims):
    return tuple(slice(None) if d in free else coords[d] for d in range(ndims))


def chunks_of(shapes, dtypes):
    out = []
    colour = 0
    for a, (rows, dtype) in enumerate(zip(shapes, dtypes)):
        tile = 16 if dtype == jnp.bfloat16 else 8
        if rows % (2 * tile) == 0:
            out.append([(a, 0, rows // 2, 0), (a, rows // 2, rows // 2, 1)])
        else:
            out.append([(a, 0, rows, colour)])
            colour = 1 - colour
    return out


def gather_all(grid, parts, cid):
    shapes = [p.shape[0] for p in parts]
    groups = chunks_of(shapes, [p.dtype for p in parts])
    flat = [c for g in groups for c in g]
    ndims = len(grid.dims)
    most = max(grid.dims) - 1
    orders = grid.orders()
    nparts = len(parts)

    def kernel(*refs):
        sources, dests = refs[:nparts], refs[nparts : 2 * nparts]
        send_sem, recv_sem, own_sem = refs[2 * nparts :]
        coords = grid.coords()
        own = [
            pltpu.make_async_copy(sources[a], dests[a].at[coords], own_sem.at[a])
            for a in range(nparts)
        ]
        for copy in own:
            copy.start()
        grid.greet(coords)

        def copies(k, stage):
            a, first, rows, colour = flat[k]
            order = orders[colour]
            dim = order[stage]
            where = index_of(coords, order[:stage], ndims) + (pl.ds(first, rows),)
            made = []
            for step in range(1, grid.dims[dim]):
                target, unused = grid.peer(coords, dim, step)
                source = sources[a].at[pl.ds(first, rows)] if stage == 0 else dests[a].at[where]
                made.append(
                    pltpu.make_async_remote_copy(
                        source,
                        dests[a].at[where],
                        send_sem.at[k, stage, step - 1],
                        recv_sem.at[k, stage, step - 1],
                        device_id=target,
                        device_id_type=MESH,
                    )
                )
            return made

        first_of = []
        k = 0
        for g in groups:
            first_of.append(list(range(k, k + len(g))))
            k += len(g)
        for tick in range(len(groups) + ndims - 1):
            for g in range(len(groups)):
                stage = tick - g
                if not 0 <= stage < ndims:
                    continue
                for k in first_of[g]:
                    if stage == 1:
                        pass
                    if stage >= 1:
                        for copy in copies(k, stage - 1):
                            copy.wait_recv()
                    if stage == 1 and k == first_of[g][0]:
                        own[flat[k][0]].wait()
                    for copy in copies(k, stage):
                        copy.start()
        for k in range(len(flat)):
            for copy in copies(k, ndims - 1):
                copy.wait_recv()
        for k in range(len(flat)):
            for stage in range(ndims):
                for copy in copies(k, stage):
                    copy.wait_send()

    out = pl.pallas_call(
        kernel,
        out_shape=[
            jax.ShapeDtypeStruct(tuple(grid.dims) + p.shape, p.dtype) for p in parts
        ],
        in_specs=[pl.BlockSpec(memory_space=pl.ANY)] * nparts,
        out_specs=[pl.BlockSpec(memory_space=pl.ANY)] * nparts,
        scratch_shapes=[
            pltpu.SemaphoreType.DMA((len(flat), ndims, most)),
            pltpu.SemaphoreType.DMA((len(flat), ndims, most)),
            pltpu.SemaphoreType.DMA((nparts,)),
        ],
        compiler_params=pltpu.CompilerParams(collective_id=cid, has_side_effects=True),
    )(*parts)
    return [o.reshape((grid.n,) + p.shape) for o, p in zip(out, parts)]


def scatter_sum(grid, parts, cid):
    shapes = [p.shape[1] for p in parts]
    groups = chunks_of(shapes, [p.dtype for p in parts])
    flat = [c for g in groups for c in g]
    ndims = len(grid.dims)
    most = max(grid.dims) - 1
    orders = [o[::-1] for o in grid.orders()]
    nparts = len(parts)
    landing = []
    for a, first, rows, colour in flat:
        order = orders[colour]
        for stage in range(ndims):
            left = [grid.dims[d] for d in range(ndims) if d in order[stage + 1 :]]
            landing.append((grid.dims[order[stage]] - 1,) + tuple(left) + (rows, parts[a].shape[2]))

    def kernel(*refs):
        sources, outs = refs[:nparts], refs[nparts : 2 * nparts]
        lands = refs[2 * nparts : -2]
        send_sem, recv_sem = refs[-2:]
        coords = grid.coords()
        grid.greet(coords)

        def copies(k, stage):
            a, first, rows, colour = flat[k]
            order = orders[colour]
            dim = order[stage]
            made = []
            for step in range(1, grid.dims[dim]):
                target, value = grid.peer(coords, dim, step)
                there = list(coords)
                there[dim] = value
                where = index_of(there, order[stage + 1 :], ndims) + (pl.ds(first, rows),)
                made.append(
                    pltpu.make_async_remote_copy(
                        sources[a].at[where],
                        lands[k * ndims + stage].at[step - 1],
                        send_sem.at[k, stage, step - 1],
                        recv_sem.at[k, stage, step - 1],
                        device_id=target,
                        device_id_type=MESH,
                    )
                )
            return made

        def add(k, stage):
            a, first, rows, colour = flat[k]
            order = orders[colour]
            free = [d for d in range(ndims) if d in order[stage + 1 :]]
            land = lands[k * ndims + stage]
            count = grid.dims[order[stage]] - 1
            sizes = [grid.dims[d] for d in free]

            def body(i, unused):
                there = list(coords)
                rest = i
                inner = [None] * len(free)
                for pos in range(len(free) - 1, -1, -1):
                    inner[pos] = rest % sizes[pos]
                    rest = rest // sizes[pos]
                    there[free[pos]] = inner[pos]
                where = tuple(there) + (pl.ds(first, rows),)
                total = sources[a][where].astype(jnp.float32)
                for step in range(count):
                    total += land[(step,) + tuple(inner)].astype(jnp.float32)
                if stage == ndims - 1:
                    outs[a][pl.ds(first, rows)] = total
                else:
                    sources[a][where] = total.astype(sources[a].dtype)
                return unused

            lax.fori_loop(0, math.prod(sizes), body, 0)

        first_of = []
        k = 0
        for g in groups:
            first_of.append(list(range(k, k + len(g))))
            k += len(g)
        for tick in range(len(groups) + ndims):
            for g in range(len(groups)):
                stage = tick - g
                if not 0 <= stage <= ndims:
                    continue
                for k in first_of[g]:
                    if stage >= 1:
                        for copy in copies(k, stage - 1):
                            copy.wait_recv()
                        add(k, stage - 1)
                    if stage < ndims:
                        for copy in copies(k, stage):
                            copy.start()
        for k in range(len(flat)):
            for stage in range(ndims):
                for copy in copies(k, stage):
                    copy.wait_send()

    def outer(*refs):
        given, outs = refs[:nparts], refs[nparts : 2 * nparts]
        held = refs[2 * nparts : 3 * nparts]
        load_sem = refs[-1]
        loads = [
            pltpu.make_async_copy(given[a], held[a], load_sem.at[a]) for a in range(nparts)
        ]
        for load in loads:
            load.start()
        for load in loads:
            load.wait()
        kernel(*held, *outs, *refs[3 * nparts : -1])

    shaped = [p.reshape(tuple(grid.dims) + p.shape[1:]) for p in parts]
    return pl.pallas_call(
        outer,
        out_shape=[jax.ShapeDtypeStruct(p.shape[1:], jnp.float32) for p in parts],
        in_specs=[pl.BlockSpec(memory_space=pl.ANY)] * nparts,
        out_specs=[pl.BlockSpec(memory_space=pltpu.VMEM)] * nparts,
        scratch_shapes=[pltpu.VMEM(s.shape, s.dtype) for s in shaped]
        + [
            pltpu.VMEM(landing[k * ndims + s], parts[flat[k][0]].dtype)
            for k in range(len(flat))
            for s in range(ndims)
        ]
        + [
            pltpu.SemaphoreType.DMA((len(flat), ndims, most)),
            pltpu.SemaphoreType.DMA((len(flat), ndims, most)),
            pltpu.SemaphoreType.DMA((nparts,)),
        ],
        compiler_params=pltpu.CompilerParams(
            collective_id=cid, has_side_effects=True, vmem_limit_bytes=56 * 2**20
        ),
    )(*shaped)


def document_table(placement):
    long_total = placement.shape[0] // 2
    long_docs = long_total // LONG_SEGS
    is_long = placement < long_total
    remainder = placement - long_total
    doc_ids = jnp.where(is_long, placement // LONG_SEGS, long_docs + remainder // SHORT_SEGS)
    places = jnp.where(is_long, placement % LONG_SEGS, remainder % SHORT_SEGS)
    return (doc_ids, places)


def layer_norm(value, gain, shift):
    centre = jnp.mean(value, -1, keepdims=True)
    offset = value - centre
    spread = jnp.mean(offset * offset, -1, keepdims=True)
    return offset * lax.rsqrt(spread + epsilon) * gain + shift


def gelu_exact(value):
    return jax.nn.gelu(value, approximate=False)


def softmax_rows(scores):
    row_peak = jnp.max(scores, -1, keepdims=True)
    raised = jnp.exp(scores - row_peak)
    return raised / jnp.sum(raised, -1, keepdims=True)


def dot_nt(left, right):
    return lax.dot_general(
        left, right, (((1,), (1,)), ((), ())), preferred_element_type=jnp.float32
    )


def dot_nn(left, right):
    return jnp.dot(left, right, preferred_element_type=jnp.float32)


def dot_tn(left, right):
    return lax.dot_general(
        left, right, (((0,), (0,)), ((), ())), preferred_element_type=jnp.float32
    )


def column_sums(grad_low):
    return jnp.sum(grad_low.astype(jnp.float32), 0)


def split_heads(matrix):
    return matrix.reshape(matrix.shape[0], HEADS, HEAD_DIM)


def run_forward(inputs, params, attend):
    project_t, full_bias, output_t, output_bias, up_t, up_bias, down, down_bias, gains, shifts = params
    inputs_low = inputs.astype(jnp.bfloat16)
    projected = (dot_nt(inputs_low, project_t) + full_bias).astype(jnp.bfloat16)
    attended_low, kept_state = attend(projected)
    first_sum = inputs + (dot_nt(attended_low, output_t) + output_bias)
    normed = layer_norm(first_sum, gains[0], shifts[0])
    normed_low = normed.astype(jnp.bfloat16)
    pre_act = dot_nt(normed_low, up_t) + up_bias
    hidden_low = gelu_exact(pre_act).astype(jnp.bfloat16)
    second = normed + (dot_nn(hidden_low, down) + down_bias)
    output = layer_norm(second, gains[1], shifts[1])
    return (
        output,
        (inputs_low, projected, attended_low, first_sum, normed_low, pre_act, hidden_low, second, kept_state),
    )


def run_backward(grad_out, kept_values, params, attend_back, mine):
    project_t, full_bias, output_t, output_bias, up_t, up_bias, down, down_bias, gains, shifts = params
    inputs_low, projected, attended_low, first_sum, normed_low, pre_act, hidden_low, second, kept_state = kept_values
    width = output_t.shape[1]
    norm_pull = jax.vjp(layer_norm, second, gains[1], shifts[1])[1]
    grad_second, gain_two, shift_two = norm_pull(grad_out)
    down_low = grad_second.astype(jnp.bfloat16)
    grad_down = dot_tn(mine(hidden_low), down_low)
    gelu_pull = jax.vjp(gelu_exact, pre_act)[1]
    up_low = gelu_pull(dot_nt(down_low, down))[0].astype(jnp.bfloat16)
    grad_up = dot_tn(mine(up_low), normed_low)
    grad_normed = grad_second + dot_nn(up_low, up_t)
    norm_pull = jax.vjp(layer_norm, first_sum, gains[0], shifts[0])[1]
    grad_first, gain_one, shift_one = norm_pull(grad_normed)
    branch_low = grad_first.astype(jnp.bfloat16)
    grad_output = dot_tn(mine(branch_low), attended_low)
    mixed_low = dot_nn(branch_low, output_t).astype(jnp.bfloat16)
    project_low = attend_back(mixed_low, projected, kept_state).astype(jnp.bfloat16)
    grad_project = dot_tn(mine(project_low), inputs_low)
    sums_project = column_sums(project_low)
    grad_pair = jnp.concatenate([sums_project[:width], sums_project[2 * width :]])
    grad_inputs = grad_first + dot_nn(project_low, project_t)
    small = (
        grad_pair,
        column_sums(branch_low),
        column_sums(up_low),
        column_sums(down_low),
        jnp.stack([gain_one, gain_two]),
        jnp.stack([shift_one, shift_two]),
    )
    return (grad_inputs, (grad_project, grad_output, grad_up, grad_down), small)


def segment_parts(projected):
    grid = projected.reshape(projected.shape[0] // SEG_LEN, SEG_LEN, 3, HEADS, HEAD_DIM)
    return (grid[:, :, 0], grid[:, :, 1], grid[:, :, 2])


def segment_shares(queries, key_rows):
    scores = jnp.einsum(
        "glhd,gmhd->ghlm", queries, key_rows, preferred_element_type=jnp.float32
    ) * HEAD_DIM ** (-0.5)
    return softmax_rows(scores)


def segment_attend(projected):
    queries, key_rows, values = segment_parts(projected)
    shares = segment_shares(queries, key_rows)
    attended = jnp.einsum(
        "ghlm,gmhd->glhd", shares.astype(jnp.bfloat16), values, preferred_element_type=jnp.float32
    )
    return (attended.reshape(projected.shape[0], -1).astype(jnp.bfloat16), shares)


def segment_back(mixed_low, projected, shares):
    queries, key_rows, values = segment_parts(projected)
    grad_low = mixed_low.reshape(queries.shape)
    grad_shares = jnp.einsum(
        "glhd,gmhd->ghlm", grad_low, values, preferred_element_type=jnp.float32
    )
    row_dot = jnp.sum(shares * grad_shares, -1, keepdims=True)
    score_low = (shares * (grad_shares - row_dot)).astype(jnp.bfloat16)
    grad_queries = jnp.einsum(
        "ghlm,gmhd->glhd", score_low, key_rows, preferred_element_type=jnp.float32
    ) * HEAD_DIM ** (-0.5)
    grad_keys = jnp.einsum(
        "ghlm,glhd->gmhd", score_low, queries, preferred_element_type=jnp.float32
    ) * HEAD_DIM ** (-0.5)
    grad_values = jnp.einsum(
        "ghlm,glhd->gmhd", shares.astype(jnp.bfloat16), grad_low, preferred_element_type=jnp.float32
    )
    return jnp.stack([grad_queries, grad_keys, grad_values], 2).reshape(projected.shape)


def cross_shares(queries, key_rows, same_doc):
    scores = jnp.einsum(
        "rhd,shd->hrs", queries, key_rows, preferred_element_type=jnp.float32
    ) * HEAD_DIM ** (-0.5)
    return softmax_rows(jnp.where(same_doc[None], scores, masked_score))


def cross_parts(projected):
    width = projected.shape[1] // 3
    return [split_heads(projected[:, i * width : (i + 1) * width]) for i in range(3)]


def cross_attend_with(same_doc):
    def attend(projected):
        queries, key_rows, values = cross_parts(projected)
        shares = cross_shares(queries, key_rows, same_doc)
        attended = jnp.einsum(
            "hrs,shd->rhd", shares.astype(jnp.bfloat16), values, preferred_element_type=jnp.float32
        )
        return (attended.reshape(projected.shape[0], -1).astype(jnp.bfloat16), shares)

    return attend


def cross_back(mixed_low, projected, shares):
    queries, key_rows, values = cross_parts(projected)
    grad_heads = split_heads(mixed_low)
    grad_shares = jnp.einsum(
        "rhd,shd->hrs", grad_heads, values, preferred_element_type=jnp.float32
    )
    row_dot = jnp.sum(shares * grad_shares, -1, keepdims=True)
    score_low = (shares * (grad_shares - row_dot)).astype(jnp.bfloat16)
    grad_queries = jnp.einsum(
        "hrs,shd->rhd", score_low, key_rows, preferred_element_type=jnp.float32
    ) * HEAD_DIM ** (-0.5)
    grad_keys = jnp.einsum(
        "hrs,rhd->shd", score_low, queries, preferred_element_type=jnp.float32
    ) * HEAD_DIM ** (-0.5)
    grad_values = jnp.einsum(
        "hrs,rhd->shd", shares.astype(jnp.bfloat16), grad_heads, preferred_element_type=jnp.float32
    )
    rows = projected.shape[0]
    return jnp.concatenate([g.reshape(rows, -1) for g in (grad_queries, grad_keys, grad_values)], 1)


def shards(
    grid,
    tokens,
    cotangent,
    placement,
    project_weight,
    project_bias,
    output_weight,
    output_bias,
    up_weight,
    up_bias,
    down_weight,
    down_bias,
    norm_gain,
    norm_bias,
    position_table,
):
    n = grid.n
    seg_count, seg_len, width = tokens.shape
    slots, rows = placement.shape[0], seg_count * seg_len
    per_project, per_output = project_weight.shape[2], output_weight.shape[2]
    per_pair, per_up = project_bias.shape[1], up_bias.shape[1]
    places_n = position_table.shape[0]
    me = lax.axis_index(AXES)

    mixed_part = [
        jnp.concatenate([project_weight[b].T, output_weight[b].T], 0) for b in range(2)
    ]
    up_part = [up_weight[b].T for b in range(2)]
    down_part = [down_weight[b] for b in range(2)]
    small = [
        jnp.concatenate(
            [
                project_bias[b], output_bias[b], up_bias[b], down_bias[b],
                norm_gain[b].reshape(-1), norm_bias[b].reshape(-1),
            ]
        )
        for b in range(2)
    ]
    small_size = small[0].shape[0]
    table_rows = -(-position_table.size // width)
    flat_table = jnp.pad(position_table.reshape(-1), (0, table_rows * width - position_table.size))
    misc = jnp.concatenate(
        [jnp.pad(s, (0, width - small_size))[None] for s in small]
        + [flat_table.reshape(table_rows, width)],
        0,
    )
    misc = jnp.pad(misc, ((0, 16 - misc.shape[0]), (0, 0)))

    misc_all, mixed0, up0, down0, mixed1, up1, down1 = gather_all(
        grid,
        [misc, mixed_part[0], up_part[0], down_part[0], mixed_part[1], up_part[1], down_part[1]],
        0,
    )

    def params_of(b, mixed_all, up_all, down_all):
        project_t = mixed_all[:, :per_project].reshape(n * per_project, width)
        output_t = mixed_all[:, per_project:].reshape(n * per_output, width)
        values = misc_all[:, b, :small_size].astype(jnp.float32)
        cuts, at = [], 0
        for size in (per_pair, per_output, per_up, per_output):
            cuts.append(values[:, at : at + size].reshape(-1))
            at += size
        norms = []
        for unused in range(2):
            pair = values[:, at : at + 2 * per_output].reshape(n, 2, per_output)
            norms.append(pair.transpose(1, 0, 2).reshape(2, width))
            at += 2 * per_output
        pair_bias, out_bias, up_b, down_b = cuts
        full_bias = jnp.concatenate(
            [pair_bias[:width], jnp.zeros((width,), jnp.float32), pair_bias[width:]]
        )
        return (
            project_t, full_bias, output_t, out_bias, up_all.reshape(n * per_up, width), up_b,
            down_all.reshape(n * per_up, width), down_b, norms[0], norms[1],
        )

    seg_params = params_of(0, mixed0, up0, down0)
    cross_params = params_of(1, mixed1, up1, down1)
    table = (
        misc_all[:, 2 : 2 + table_rows]
        .reshape(n, -1)[:, : position_table.size]
        .reshape(n, places_n, per_output)
        .transpose(1, 0, 2)
        .reshape(places_n, width)
    )

    doc_ids, places = document_table(placement)
    same_doc = doc_ids[:, None] == doc_ids[None, :]
    picker = places[:, None] == jnp.arange(places_n, dtype=jnp.int32)[None, :]

    inputs = tokens.reshape(rows, width).astype(jnp.float32)
    seg_out, seg_kept = run_forward(inputs, seg_params, segment_attend)
    seg_grid = seg_out.reshape(seg_count, seg_len, width)

    cls_rows, cot_rows = gather_all(grid, [seg_grid[:, 0, :], cotangent[:, 0, :]], 1)
    cls_in = cls_rows.reshape(slots, width) + dot_nn(picker.astype(jnp.bfloat16), table)
    cross_out, cross_kept = run_forward(cls_in, cross_params, cross_attend_with(same_doc))

    def own_columns(matrix):
        size = matrix.shape[1] // n
        return lax.dynamic_slice_in_dim(matrix, me * size, size, 1)

    grad_cls_all, cross_big, cross_small = run_backward(
        cot_rows.reshape(slots, width), cross_kept, cross_params, cross_back, own_columns
    )
    position_gradient = lax.dot_general(
        picker.astype(jnp.float32), own_columns(grad_cls_all), (((0,), (0,)), ((), ())), precision=highest
    )
    my_cross = lax.dynamic_slice_in_dim(cross_out, me * seg_count, seg_count, 0)
    grad_cls = lax.dynamic_slice_in_dim(grad_cls_all, me * seg_count, seg_count, 0)
    layer_output = seg_grid.at[:, 0, :].set(my_cross).astype(jnp.bfloat16)

    grad_rows = cotangent.at[:, 0, :].set(grad_cls).reshape(rows, width)
    grad_inputs, seg_big, seg_small = run_backward(
        grad_rows, seg_kept, seg_params, segment_back, lambda matrix: matrix
    )

    def small_slots(pair, out_b, up_b, down_b, gains, shifts):
        def per_device(vector):
            return vector.reshape(vector.shape[:-1] + (n, -1))

        return jnp.concatenate(
            [
                per_device(pair), per_device(out_b), per_device(up_b), per_device(down_b),
                per_device(gains).transpose(1, 0, 2).reshape(n, -1),
                per_device(shifts).transpose(1, 0, 2).reshape(n, -1),
            ],
            1,
        )

    grad_project, grad_output, grad_up, grad_down = [
        g.astype(jnp.bfloat16).reshape(n, -1, width) for g in seg_big
    ]
    seg_small_slots = small_slots(*seg_small)
    seg_small_slots = jnp.pad(seg_small_slots[:, None], ((0, 0), (0, 7), (0, width - small_size)))
    down_sum, up_sum, mixed_sum, small_sum = scatter_sum(
        grid,
        [grad_down, grad_up, jnp.concatenate([grad_project, grad_output], 1), seg_small_slots],
        2,
    )
    my_small = [
        small_sum[0, :small_size],
        lax.dynamic_slice_in_dim(small_slots(*cross_small), me, 1, 0)[0],
    ]
    small_pair = jnp.stack(my_small)
    cuts, at = [], 0
    for size in (per_pair, per_output, per_up, per_output, 2 * per_output, 2 * per_output):
        cuts.append(small_pair[:, at : at + size])
        at += size
    pair_g, out_g, up_g, down_g, gain_g, shift_g = cuts
    return (
        layer_output,
        grad_inputs.reshape(tokens.shape),
        jnp.stack([mixed_sum[:per_project].T, cross_big[0].T]),
        pair_g,
        jnp.stack([mixed_sum[per_project:].T, cross_big[1].T]),
        out_g,
        jnp.stack([up_sum.T, cross_big[2].T]),
        up_g,
        jnp.stack([down_sum, cross_big[3]]),
        down_g,
        gain_g.reshape(2, 2, per_output),
        shift_g.reshape(2, 2, per_output),
        position_gradient,
    )


def solution(mesh):
    grid = Grid(mesh)
    rows, cols, last = P(AXES, None, None), P(None, AXES), P(None, None, AXES)
    middle = P(None, AXES, None)
    return jax.shard_map(
        functools.partial(shards, grid),
        mesh=mesh,
        in_specs=(
            rows, rows, P(), last, cols, last, cols, last, cols, middle, cols, last, last, cols,
        ),
        out_specs=(rows, rows, last, cols, last, cols, last, cols, middle, cols, last, last, cols),
        check_vma=False,
    )
```

time: 2100 us -> 618 us (0.29)
  waiting for transfers between devices: 1060 us -> 0 us
  blocking collectives: 643 us -> 0 us
  Pallas kernels: 0 us -> 264 us
    all_gather x9 -> x0, blocking collectives: 602 us -> none  [the longest x1 71.6 us: shards(): lax.all_gather(norm_bias, ('dp', 'fsdp'), axis=2, tiled=True)]
    reduce_scatter x4 -> x0, waiting for transfers between devices: 562 us -> none  [the longest x1 212 us: shards(): lax.psum_scatter(stacked[6], ('dp', 'fsdp'), scatter_dimension=1, tiled=T...]
    unnamed x16 -> x0, waiting for transfers between devices: 499 us -> none
    pallas_call x0 -> x3, Pallas kernels: none -> 264 us  [the longest x2 168 us: gather_all(): pl.pallas_call(kernel, out_shape=[jax.ShapeDtypeStruct(tuple(grid.dims) +...]
    unnamed x1 -> x0, blocking collectives: 40.8 us -> none
    another operation x16 -> x7, other arithmetic: 35.9 us -> 7.05 us  [the longest x1 1.91 us: shards(): jnp.stack([down_sum, cross_big[3]])]
    another operation x11 -> x19, local copies, waits for them, and re-layouts: 36.6 us -> 8.98 us  [the longest x4 1.7 us: run_backward(): jnp.stack([gain_one, gain_two])]
    slice x7 -> x45, local copies, waits for them, and re-layouts: 0.2 us -> 26.2 us  [the longest x4 6.16 us: cross_parts(): projected[:, i * width:(i + 1) * width]]
  transfers between devices with their start and end apart: 12 -> 0, of which waited for: 7 -> 0; matrix products, arithmetic and copies ran while one was open for 11% -> 0% of each run, Pallas kernels for 0% -> 0%
where the time goes in v1:
time: 618 us; the launch traced here: 608 us
  Pallas kernels  264 us (43%)
  matrix products  186 us (30%)
  local copies, waits for them, and re-layouts  99.4 us (16%)
  other arithmetic  54.8 us (9%)
    pallas_call x2, Pallas kernels, gather_all(): pl.pallas_call(kernel, out_shape=[jax.ShapeDtypeStruct(tuple(grid.dims) +...  168 us
    pallas_call x1, Pallas kernels, scatter_sum(): pl.pallas_call(outer, out_shape=[jax.ShapeDtypeStruct(p.shape[1:], jnp.fl...  95.9 us
    dot_general x8, matrix products, dot_nt(): lax.dot_general(left, right, (((1,), (1,)), ((), ())), preferred_element_...  86.9 us
    dot_general x9, matrix products, dot_nn(): return jnp.dot(left, right, preferred_element_type=jnp.float32)  47.9 us
    unnamed x248, local copies, waits for them, and re-layouts  27.5 us
    dot_general x8, matrix products, dot_tn(): lax.dot_general(left, right, (((0,), (0,)), ((), ())), preferred_element_...  24.9 us

profile of v1, /device:TPU:0, one launch (start us, length us, event | category | flops | bytes accessed | tf_op | source)
XLA Modules:
  0.0 607.7 jit_solution(15501659032322163621)
XLA Ops:
  0.7 1.9 copy.214
  14.8 142.8 %shard_map.237 = (bf16[2,2,2,4,16,768]{5,4,3,2,1,0:T(8,128)(2,1)}, bf16[2,2,2,4,96,768]{5,4,3,2,1,0:T(8,128)(2,1)}, bf16[2,2,2,4,96,768]{5,4,3,2,1,0:T(8,128)(2,...) custom-call(bf16[16,768]{1,0:T(8,128)(2,1)} %fusion.79.refs_0_, ...), custom_call_target="tpu_custom_call" | custom-call | tf_op jit(solution)/shard_map/pallas_call | solution.py:150
  160.5 2.4 slice.384
  162.9 1.8 copy-done.23
  164.6 4.3 fusion.27
  173.2 5.9 fusion.130
  181.9 2.4 copy.106
  185.8 3.9 fusion.131
  193.1 37.0 %multiply_convert_fusion = (bf16[1024,3072]{1,0:T(8,128)(2,1)}, f32[1024,3072]{1,0:T(8,128)}, f32[1024,3072]{1,0:T(8,128)}) fusion(f32[3072]{0:T(1024)S(1)} %add.250, bf16[3072,768]{1,0:T(8,128)(2,1)} %bitcast.334, f32[1024,768]{1,0:T(8,128)} %copy-done.9, f32[768]{0:T(1024)S(1)} %add.247, f32[768]{0:T(1024)S(1)} %mul.375, f32[1024]{0:T(1024)S(1)} %fusion.83, ...), kind=kOutput, calls=%fused_computation.6 | convolution fusion | flops 5043388416 | bytes 39348224 | tf_op jit(solution)/shard_map/dot_general | solution.py:326
  230.3 9.7 %fusion.132 = (f32[1024]{0:T(1024)S(1)}, f32[1024,768]{1,0:T(8,128)S(1)}) fusion(f32[768]{0:T(1024)S(1)} %add.253, bf16[1024,3072]{1,0:T(8,128)(2,1)} %get-tuple-element.112, bf16[3072,768]{1,0:T(8,128)(2,1)} %bitcast.336, f32[768]{0:T(1024)S(1)} %add.247, f32[768]{0:T(1024)S(1)} %mul.375, f32[1024]{0:T(1024)S(1)} %fusion.83, f32[1024,768]{1,0:T(8,128)} %copy-done.9, ...), kind=kOutput, calls=%fused_computation.300 | convolution fusion | flops 4837342208 | bytes 17323008 | tf_op jit(solution)/shard_map/dot_general | solution.py:332
  243.2 2.4 multiply_add_fusion
  248.5 25.6 %shard_map.238 = (f32[2,2,2,4,8,768]{5,4,3,2,1,0:T(8,128)}, f32[2,2,2,4,8,768]{5,4,3,2,1,0:T(8,128)}) custom-call(f32[8,768]{1,0:T(8,128)} %bitcast.322, f32[8,768]{1,0:T(8,128)} %bitcast.323), custom_call_target="tpu_custom_call" | custom-call | tf_op jit(solution)/shard_map/pallas_call | solution.py:150
  279.5 2.5 slice.403
  286.0 2.1 copy.122
  288.8 4.6 fusion.133
  293.4 1.9 copy.120
  295.3 2.3 convolution_convert_fusion.8
  302.6 2.2 fusion.134
  309.2 12.5 %multiply_convert_fusion.5 = (bf16[256,3072]{1,0:T(8,128)(2,1)}, f32[256,3072]{1,0:T(8,128)}, f32[256,3072]{1,0:T(8,128)}) fusion(f32[3072]{0:T(1024)S(1)} %add.276, bf16[3072,768]{1,0:T(8,128)(2,1)} %bitcast.338, f32[256,768]{1,0:T(8,128)} %copy-done.14, f32[768]{0:T(1024)S(1)} %add.273, f32[768]{0:T(1024)S(1)} %mul.392, f32[256]{0:T(256)} %fusion.97, ...), kind=kOutput, calls=%fused_computation.58 | convolution fusion | flops 1260847104 | bytes 13389824 | tf_op jit(solution)/shard_map/dot_general | solution.py:326
  321.9 5.3 fusion.135
  329.1 3.2 fusion.110
  334.0 1.9 convolution_bitcast_fusion
  335.9 7.0 %convert_reduce_fusion.2 = (f32[3072]{0:T(1024)}, bf16[256,3072]{1,0:T(8,128)(2,1)S(1)}) fusion(f32[256,3072]{1,0:T(8,128)} %get-tuple-element.111, f32[256,3072]{1,0:T(8,128)} %get-tuple-element.190, bf16[256,768]{1,0:T(8,128)(2,1)S(1)} %get-tuple-element.89, bf16[3072,768]{1,0:T(8,128)(2,1)} %bitcast.341), kind=kOutput, calls=%fused_computation.47 | convolution fusion | flops 1220539392 | bytes 12988416 | tf_op jit(solution)/shard_map/dot_general | solution.py:326
  342.9 5.1 multiply_reduce_fusion.8
  351.3 1.9 copy.131
  353.2 2.9 multiply_reduce_fusion.5
  360.9 2.1 convolution_add_fusion.4
  365.2 4.0 fusion.18
  369.3 1.8 fusion.108
  371.2 2.3 convert_reduce_fusion.3
  373.5 18.9 %convert_reduce_fusion = (f32[3072]{0:T(1024)}, bf16[1024,3072]{1,0:T(8,128)(2,1)}) fusion(f32[1024,3072]{1,0:T(8,128)} %get-tuple-element.113, bf16[1024,768]{1,0:T(8,128)(2,1)} %get-tuple-element.97, bf16[3072,768]{1,0:T(8,128)(2,1)} %bitcast.337, f32[1024,3072]{1,0:T(8,128)} %get-tuple-element.183, f32[3072]{0:T(1024)S(1)} %copy-done.87), kind=kOutput, calls=%fused_computation.4 | convolution fusion | flops 4885312512 | bytes 37773312 | tf_op jit(solution)/shard_map/dot_general | solution.py:326
  392.4 11.5 %multiply_reduce_fusion.2 = (f32[768]{0:T(1024)}, f32[1024]{0:T(1024)}, f32[768]{0:T(1024)}, f32[1024,768]{1,0:T(8,128)}) fusion(f32[1024,768]{1,0:T(8,128)S(1)} %copy-done.10, f32[1024]{0:T(1024)S(1)} %copy-done.78, f32[1024]{0:T(1024)S(1)} %copy-done.62, f32[768]{0:T(1024)S(1)} %copy-done.70, bf16[1024,3072]{1,0:T(8,128)(2,1)} %get-tuple-element.200, ...), kind=kOutput, calls=%fused_computation.48 | convolution fusion | flops 4839699456 | bytes 20472832 | tf_op jit(solution)/shard_map/dot_general | solution.py:332
  410.1 3.6 fusion.107
  421.5 5.8 multiply_reduce_fusion
  427.4 3.1 multiply_convert_fusion.1
  431.9 2.3 fusion.42
  434.2 2.3 fusion.46
  436.5 3.2 convert_reduce_fusion.1
  452.2 9.2 %copy.142 = bf16[8,128,3,12,64]{1,0,4,3,2:T(8,128)(2,1)S(1)} copy(bf16[8,128,3,12,64]{1,4,3,0,2:T(8,128)(2,1)S(1)} %bitcast.277) | data formatting | bytes 9437184 | tf_op jit(solution)/shard_map/stack | solution.py:438
  461.5 4.3 convolution_convert_fusion.2
  465.8 3.0 pad_maximum_fusion.1.refs_2_
  468.9 7.8 %convolution_convert_fusion = bf16[3072,768]{1,0:T(8,128)(2,1)} fusion(bf16[1024,3072]{1,0:T(8,128)(2,1)S(1)} %bitcast.347, f32[1024,768]{1,0:T(8,128)S(1)} %copy-done.11, f32[768]{0:T(1024)S(1)} %copy-done.98, f32[768]{0:T(1024)S(1)} %copy-done.71, f32[1024]{0:T(1024)S(1)} %copy-done.79, f32[1024]{0:T(1024)S(1)} %copy-done.63), kind=kOutput, calls=%fused_computation.27 | convolution fusion | flops 4838129664 | bytes 14170112 | tf_op jit(solution)/shard_map/dot_general | solution.py:336
  476.7 7.0 %convolution_convert_fusion.1 = bf16[3072,768]{1,0:T(8,128)(2,1)} fusion(bf16[1024,3072]{1,0:T(8,128)(2,1)S(1)} %bitcast.349, bf16[1024,768]{1,0:T(8,128)(2,1)S(1)} %copy-done.39), kind=kOutput, calls=%fused_computation.28 | convolution fusion | flops 4834197504 | bytes 12582912 | tf_op jit(solution)/shard_map/dot_general | solution.py:336
  483.8 95.9 %shard_map.239 = (f32[96,768]{1,0:T(8,128)}, f32[96,768]{1,0:T(8,128)}, f32[96,768]{1,0:T(8,128)}, f32[8,768]{1,0:T(8,128)}) custom-call(bf16[2,2,2,4,96,768]{5,4,3,2,1,0:T(8,128)(2,1)} %bitcast.284, bf16[2,2,2,4,96,768]{5,4,3,2,1,0:T(8,128)(2,1)} %bitcast.283, bf16[2,2,2,4,96,768]{5,4,3,2,1,0:T(8,128)(2,1)} %pad_maximum_fusion.1.refs_2_, ...), custom_call_target="tpu_custom_call" | custom-call | tf_op jit(solution)/shard_map/pallas_call | solution.py:276
  579.8 1.9 pad_maximum_fusion.4
  585.7 1.8 pad_maximum_fusion.3
  592.9 10.1 %add_add_fusion.4 = f32[1024,768]{1,0:T(8,128)} fusion(f32[1024,768]{1,0:T(8,128)} %copy-done.12, bf16[2304,768]{1,0:T(8,128)(2,1)} %bitcast.292, bf16[288,8,8,128]{3,2,1,0:T(8,128)(2,1)} %bitcast.290, f32[1024]{0:T(1024)S(1)} %copy-done.81), kind=kOutput, calls=%fused_computation.82 | convolution fusion | flops 3625451520 | bytes 14553088 | tf_op jit(solution)/shard_map/dot_general | solution.py:332
  602.9 1.9 fusion.67
  (435 shorter events, 105.4 us)
Async XLA Ops:
  0.7 11.0 %copy-start.54 = (bf16[2,768,24]{1,2,0:T(8,128)(2,1)S(1)}, bf16[2,768,24]{1,2,0:T(8,128)(2,1)}, u32[]{:S(2)}) copy-start(bf16[2,768,24]{1,2,0:T(8,128)(2,1)} %param.23) | copy-start | bytes 221188
  0.7 11.7 %copy-start.51 = (bf16[2,96,768]{2,1,0:T(8,128)(2,1)S(1)}, bf16[2,96,768]{2,1,0:T(8,128)(2,1)}, u32[]{:S(2)}) copy-start(bf16[2,96,768]{2,1,0:T(8,128)(2,1)} %param.27) | copy-start | bytes 884740
  0.7 9.1 %copy-start.96 = (bf16[64,24]{0,1:T(8,128)(2,1)S(1)}, bf16[64,24]{0,1:T(8,128)(2,1)}, u32[]{:S(2)}) copy-start(bf16[64,24]{0,1:T(8,128)(2,1)} %param.31) | copy-start | bytes 9220
  170.5 8.6 %copy-start.31 = (bf16[8,128,1,12,64]{1,0,4,3,2:T(8,128)(2,1)}, bf16[8,128,1,12,64]{1,0,4,3,2:T(8,128)(2,1)S(1)}, u32[]{:S(2)}) copy-start(bf16[8,128,1,12,64]{1,0,4,3,2:T(8,128)(2,1)S(1)} %get-tuple-element.116) | copy-start | bytes 4718596
  189.8 40.5 %copy-start.61 = (f32[1024]{0:T(1024)}, f32[1024]{0:T(1024)S(1)}, u32[]{:S(2)}) copy-start(f32[1024]{0:T(1024)S(1)} %broadcast_multiply_fusion.1) | copy-start | bytes 12292
  192.0 38.3 %copy-start.77 = (f32[1024]{0:T(1024)}, f32[1024]{0:T(1024)S(1)}, u32[]{:S(2)}) copy-start(f32[1024]{0:T(1024)S(1)} %fusion.83) | copy-start | bytes 12292
  192.7 37.6 %copy-start.69 = (f32[768]{0:T(1024)}, f32[768]{0:T(1024)S(1)}, u32[]{:S(2)}) copy-start(f32[768]{0:T(1024)S(1)} %mul.375) | copy-start | bytes 9220
  192.9 37.4 %copy-start.97 = (f32[768]{0:T(1024)}, f32[768]{0:T(1024)S(1)}, u32[]{:S(2)}) copy-start(f32[768]{0:T(1024)S(1)} %add.247) | copy-start | bytes 9220
  193.1 37.0 %copy-start.86 = (f32[3072]{0:T(1024)}, f32[3072]{0:T(1024)S(1)}, u32[]{:S(2)}) copy-start(f32[3072]{0:T(1024)S(1)} %add.250) | copy-start | bytes 36868
  243.2 34.8 %copy-start.108 = (s32[256]{0:T(256)S(1)}, s32[256]{0:T(256)}, u32[]{:S(2)}) copy-start(s32[256]{0:T(256)} %param.20) | copy-start | bytes 3076
  297.6 8.3 %copy-start.42 = (bf16[12,64,256]{2,1,0:T(8,128)(2,1)}, bf16[12,64,256]{2,1,0:T(8,128)(2,1)S(1)}, u32[]{:S(2)}) copy-start(bf16[12,64,256]{2,1,0:T(8,128)(2,1)S(1)} %convolution_convert_fusion.8) | copy-start | bytes 1179652
  307.5 40.6 %copy-start.59 = (f32[768]{0:T(1024)}, f32[768]{0:T(1024)S(1)}, u32[]{:S(2)}) copy-start(f32[768]{0:T(1024)S(1)} %mul.392) | copy-start | bytes 9220
  308.3 13.7 %copy-start.72 = (f32[768]{0:T(1024)}, f32[768]{0:T(1024)S(1)}, u32[]{:S(2)}) copy-start(f32[768]{0:T(1024)S(1)} %add.273) | copy-start | bytes 9220
  309.2 12.5 %copy-start.58 = (f32[32,24]{0,1:T(8,128)S(1)}, f32[32,24]{0,1:T(8,128)}, u32[]{:S(2)}) copy-start(f32[32,24]{0,1:T(8,128)} %get-tuple-element.130) | copy-start | bytes 9220
  309.2 12.7 %copy-start.83 = (f32[256]{0:T(256)S(1)}, f32[256]{0:T(256)}, u32[]{:S(2)}) copy-start(f32[256]{0:T(256)} %copy-done.82) | copy-start | bytes 3076
  309.2 12.7 %copy-start.93 = (f32[256]{0:T(256)S(1)}, f32[256]{0:T(256)}, u32[]{:S(2)}) copy-start(f32[256]{0:T(256)} %fusion.97) | copy-start | bytes 3076
  373.5 18.9 %copy-start.10 = (f32[1024,768]{1,0:T(8,128)S(1)}, f32[1024,768]{1,0:T(8,128)}, u32[]{:S(2)}) copy-start(f32[1024,768]{1,0:T(8,128)} %copy-done.9) | copy-start | bytes 9437188
  373.5 18.9 %copy-start.62 = (f32[1024]{0:T(1024)S(1)}, f32[1024]{0:T(1024)}, u32[]{:S(2)}) copy-start(f32[1024]{0:T(1024)} %copy-done.61) | copy-start | bytes 12292
  373.5 18.9 %copy-start.70 = (f32[768]{0:T(1024)S(1)}, f32[768]{0:T(1024)}, u32[]{:S(2)}) copy-start(f32[768]{0:T(1024)} %copy-done.69) | copy-start | bytes 9220
  373.5 18.9 %copy-start.78 = (f32[1024]{0:T(1024)S(1)}, f32[1024]{0:T(1024)}, u32[]{:S(2)}) copy-start(f32[1024]{0:T(1024)} %copy-done.77) | copy-start | bytes 12292
  436.4 13.5 %copy-start.33 = (bf16[8,128,12,64]{1,0,3,2:T(8,128)(2,1)S(1)}, bf16[8,128,12,64]{1,0,3,2:T(8,128)(2,1)}, u32[]{:S(2)}) copy-start(bf16[8,128,12,64]{1,0,3,2:T(8,128)(2,1)} %copy.106) | copy-start | bytes 4718596
  436.4 13.5 %copy-start.41 = (bf16[1024,768]{1,0:T(8,128)(2,1)S(1)}, bf16[1024,768]{1,0:T(8,128)(2,1)}, u32[]{:S(2)}) copy-start(bf16[1024,768]{1,0:T(8,128)(2,1)} %copy-done.40) | copy-start | bytes 4718596
  452.2 9.3 %copy-start.111 = (bf16[8,128,768]{2,1,0:T(8,128)(2,1)S(1)}, bf16[8,128,768]{2,1,0:T(8,128)(2,1)}, u32[]{:S(2)}) copy-start(bf16[8,128,768]{2,1,0:T(8,128)(2,1)} %param.18) | copy-start | bytes 4718596
  452.2 16.6 %slice-start.4 = ((s8[6291456]{0:T(1024)(128)(4,1)}), s8[4194304]{0:T(1024)(128)(4,1)S(1)}, s32[]{:S(2)}) async-start(s8[6291456]{0:T(1024)(128)(4,1)} %bitcast.346), calls=%async_computation.4 | async-start | bytes 8388608
  465.8 10.9 %slice-start.6 = ((s8[6291456]{0:T(1024)(128)(4,1)}), s8[4194304]{0:T(1024)(128)(4,1)S(1)}, s32[]{:S(2)}) async-start(s8[6291456]{0:T(1024)(128)(4,1)} %bitcast.348), calls=%async_computation.6 | async-start | bytes 8388608
  468.9 7.8 %copy-start.39 = (bf16[1024,768]{1,0:T(8,128)(2,1)S(1)}, bf16[1024,768]{1,0:T(8,128)(2,1)}, u32[]{:S(2)}) copy-start(bf16[1024,768]{1,0:T(8,128)(2,1)} %get-tuple-element.97) | copy-start | bytes 4718596
  468.9 7.8 %slice-start.7 = ((s8[6291456]{0:T(1024)(128)(4,1)}), s8[2097152]{0:T(1024)(128)(4,1)S(1)}, s32[]{:S(2)}) async-start(s8[6291456]{0:T(1024)(128)(4,1)} %bitcast.348), calls=%async_computation.7 | async-start | bytes 4194304
  483.7 96.0 %copy-start.47 = (f32[1,96,768]{2,1,0:T(8,128)S(1)}, f32[1,96,768]{2,1,0:T(8,128)}, u32[]{:S(2)}) copy-start(f32[1,96,768]{2,1,0:T(8,128)} %convolution_bitcast_fusion) | copy-start | bytes 884740
  483.7 98.0 %copy-start.100 = (f32[768]{0:T(1024)S(1)}, f32[768]{0:T(1024)}, u32[]{:S(2)}) copy-start(f32[768]{0:T(1024)} %get-tuple-element.85) | copy-start | bytes 9220
  483.7 98.1 %copy-start.21 = (f32[2,2,2,4,8,768]{5,4,3,2,1,0:T(8,128)S(1)}, f32[2,2,2,4,8,768]{5,4,3,2,1,0:T(8,128)}, u32[]{:S(2)}) copy-start(f32[2,2,2,4,8,768]{5,4,3,2,1,0:T(8,128)} %get-tuple-element.58) | copy-start | bytes 2359300
  483.7 98.4 %copy-start.99 = (f32[768]{0:T(1024)S(1)}, f32[768]{0:T(1024)}, u32[]{:S(2)}) copy-start(f32[768]{0:T(1024)} %get-tuple-element.81) | copy-start | bytes 9220
  483.7 98.5 %copy-start.75 = (f32[768]{0:T(1024)S(1)}, f32[768]{0:T(1024)}, u32[]{:S(2)}) copy-start(f32[768]{0:T(1024)} %get-tuple-element.117) | copy-start | bytes 9220
  483.7 98.7 %copy-start.67 = (f32[2304]{0:T(1024)S(1)}, f32[2304]{0:T(1024)}, u32[]{:S(2)}) copy-start(f32[2304]{0:T(1024)} %get-tuple-element.94) | copy-start | bytes 27652
  483.7 98.9 %copy-start.76 = (f32[768]{0:T(1024)S(1)}, f32[768]{0:T(1024)}, u32[]{:S(2)}) copy-start(f32[768]{0:T(1024)} %get-tuple-element.92) | copy-start | bytes 9220
  483.8 99.0 %copy-start.88 = (f32[3072]{0:T(1024)S(1)}, f32[3072]{0:T(1024)}, u32[]{:S(2)}) copy-start(f32[3072]{0:T(1024)} %get-tuple-element.90) | copy-start | bytes 36868
  483.8 99.1 %copy-start.74 = (f32[768]{0:T(1024)S(1)}, f32[768]{0:T(1024)}, u32[]{:S(2)}) copy-start(f32[768]{0:T(1024)} %get-tuple-element.88) | copy-start | bytes 9220
  483.8 100.6 %copy-start.16 = (f32[256,768]{1,0:T(8,128)S(1)}, f32[256,768]{1,0:T(8,128)}, u32[]{:S(2)}) copy-start(f32[256,768]{1,0:T(8,128)} %copy-done.14) | copy-start | bytes 2359300
  483.8 100.6 %copy-start.60 = (f32[768]{0:T(1024)S(1)}, f32[768]{0:T(1024)}, u32[]{:S(2)}) copy-start(f32[768]{0:T(1024)} %copy-done.59) | copy-start | bytes 9220
  483.8 100.6 %copy-start.73 = (f32[768]{0:T(1024)S(1)}, f32[768]{0:T(1024)}, u32[]{:S(2)}) copy-start(f32[768]{0:T(1024)} %copy-done.72) | copy-start | bytes 9220
  483.8 100.6 %copy-start.85 = (f32[256]{0:T(256)S(1)}, f32[256]{0:T(256)}, u32[]{:S(2)}) copy-start(f32[256]{0:T(256)} %copy-done.82) | copy-start | bytes 3076
  483.8 100.6 %copy-start.95 = (f32[256]{0:T(256)S(1)}, f32[256]{0:T(256)}, u32[]{:S(2)}) copy-start(f32[256]{0:T(256)} %fusion.97) | copy-start | bytes 3076
  579.7 8.4 %copy-start.43 = (bf16[12,64,256]{2,1,0:T(8,128)(2,1)S(1)}, bf16[12,64,256]{2,1,0:T(8,128)(2,1)}, u32[]{:S(2)}) copy-start(bf16[12,64,256]{2,1,0:T(8,128)(2,1)} %copy-done.42) | copy-start | bytes 1179652
  579.8 11.3 %copy-start.20 = (f32[256,768]{1,0:T(8,128)S(1)}, f32[256,768]{1,0:T(8,128)}, u32[]{:S(2)}) copy-start(f32[256,768]{1,0:T(8,128)} %copy-done.19) | copy-start | bytes 2359300
  582.0 10.8 %copy-start.81 = (f32[1024]{0:T(1024)S(1)}, f32[1024]{0:T(1024)}, u32[]{:S(2)}) copy-start(f32[1024]{0:T(1024)} %copy-done.80) | copy-start | bytes 12292
  592.8 10.1 %copy-start.90 = (s32[256]{0:T(256)S(1)}, s32[256]{0:T(256)}, u32[]{:S(2)}) copy-start(s32[256]{0:T(256)} %copy-done.89) | copy-start | bytes 3076
  592.8 12.0 %copy-start.57 = (f32[1,32,24]{1,2,0:T(8,128)S(1)}, f32[1,32,24]{1,2,0:T(8,128)}, u32[]{:S(2)}) copy-start(f32[1,32,24]{1,2,0:T(8,128)} %get-tuple-element.146) | copy-start | bytes 9220
  592.8 12.2 %copy-start.56 = (f32[768]{0:T(1024)S(1)}, f32[768]{0:T(1024)}, u32[]{:S(2)}) copy-start(f32[768]{0:T(1024)} %copy-done.55) | copy-start | bytes 9220
  592.9 12.9 %copy-start.8 = (f32[1024,768]{1,0:T(8,128)S(1)}, f32[1024,768]{1,0:T(8,128)}, u32[]{:S(2)}) copy-start(f32[1024,768]{1,0:T(8,128)} %copy-done.7) | copy-start | bytes 9437188
  (72 other events, 226.6 us)

commit v2 on v0

v2 whole, which is shorter than its diff:
```python
import functools
import math

import jax
import jax.numpy as jnp
from jax import lax
from jax.experimental import pallas as pl
from jax.experimental.pallas import tpu as pltpu
from jax.sharding import PartitionSpec as P

HEADS = 12
HEAD_DIM = 64
SEG_LEN = 128
LONG_SEGS = 64
SHORT_SEGS = 16
MESH = pl.DeviceIdType.MESH
AXES = ("dp", "fsdp")

highest = lax.Precision.HIGHEST
epsilon = 1e-06
masked_score = -1e30


class Grid:
    def __init__(self, mesh):
        self.dp, self.fsdp = mesh.shape["dp"], mesh.shape["fsdp"]
        twos = int(math.log2(self.dp))
        self.dims = (2,) * twos + (self.fsdp,)
        self.n = self.dp * self.fsdp
        self.last = len(self.dims) - 1
        self.most = max(self.dims) - 1
        middle = list(range(self.last - 1))
        self.orders = (
            [self.last] + middle[::-1] + [self.last - 1],
            [self.last] + middle + [self.last - 1],
        )

    def coords(self):
        dp, fs = lax.axis_index("dp"), lax.axis_index("fsdp")
        twos = self.last
        return tuple((dp // 2 ** (twos - 1 - i)) % 2 for i in range(twos)) + (fs,)

    def flat(self):
        return lax.axis_index("dp") * self.fsdp + lax.axis_index("fsdp")

    def peer(self, coords, dim, step):
        other = list(coords)
        other[dim] = lax.rem(coords[dim] + step, self.dims[dim])
        dp = 0
        for value in other[:-1]:
            dp = dp * 2 + value
        return (dp, other[-1]), other[dim]

    def greet(self, coords):
        barrier = pltpu.get_barrier_semaphore()
        count = 0
        for dim, size in enumerate(self.dims):
            for step in range(1, size):
                where, unused = self.peer(coords, dim, step)
                pl.semaphore_signal(barrier, inc=1, device_id=where, device_id_type=MESH)
                count += 1
        pl.semaphore_wait(barrier, count)

    def sems(self, chunks):
        shape = (chunks, len(self.dims), self.most)
        return [pltpu.SemaphoreType.DMA(shape), pltpu.SemaphoreType.DMA(shape)]


def index_of(coords, free, ndims):
    return tuple(slice(None) if d in free else coords[d] for d in range(ndims))


def halves(rows, dtype):
    tile = 16 if dtype == jnp.bfloat16 else 8
    if rows % (2 * tile) == 0:
        return [(0, rows // 2, 0), (rows // 2, rows // 2, 1)]
    return [(0, rows, 0)]


class Gather:
    def __init__(self, grid, coords, chunks, send_sem, recv_sem, base=0):
        self.grid, self.coords, self.chunks = grid, coords, chunks
        self.send_sem, self.recv_sem, self.base = send_sem, recv_sem, base
        self.stages = len(grid.dims)

    def copies(self, k, stage):
        own, line, dest, first, rows, colour = self.chunks[k]
        grid, coords = self.grid, self.coords
        order = grid.orders[colour]
        dim = order[stage]
        cut = (pl.ds(first, rows),)
        if stage == 0:
            source = own.at[cut]
            target_ref = dest.at[coords + cut] if line is None else line.at[(coords[-1],) + cut]
        else:
            target_ref = dest.at[index_of(coords, order[:stage], len(grid.dims)) + cut]
            source = line.at[(slice(None),) + cut] if line is not None and stage == 1 else target_ref
        made = []
        for step in range(1, grid.dims[dim]):
            target, unused = grid.peer(coords, dim, step)
            made.append(
                pltpu.make_async_remote_copy(
                    source,
                    target_ref,
                    self.send_sem.at[self.base + k, stage, step - 1],
                    self.recv_sem.at[self.base + k, stage, step - 1],
                    device_id=target,
                    device_id_type=MESH,
                )
            )
        return made

    def start(self, k, stage):
        for copy in self.copies(k, stage):
            copy.start()

    def landed(self, k, stage):
        for copy in self.copies(k, stage):
            copy.wait_recv()

    def sent(self, k, first_stage, last_stage):
        for stage in range(first_stage, last_stage):
            for copy in self.copies(k, stage):
                copy.wait_send()


class Scatter:
    def __init__(self, grid, coords, chunks, send_sem, recv_sem, base=0):
        self.grid, self.coords, self.chunks = grid, coords, chunks
        self.send_sem, self.recv_sem, self.base = send_sem, recv_sem, base
        self.stages = len(grid.dims)

    @staticmethod
    def landing(grid, rows, width, dtype, colour):
        order = grid.orders[colour][::-1]
        made = []
        for stage, dim in enumerate(order):
            left = [grid.dims[d] for d in range(len(order)) if d in order[stage + 1 :]]
            made.append(pltpu.VMEM((grid.dims[dim] - 1, *left, rows, width), dtype))
        return made

    def copies(self, k, stage):
        held, lands, out, first, rows, colour = self.chunks[k]
        grid, coords = self.grid, self.coords
        order = grid.orders[colour][::-1]
        dim = order[stage]
        made = []
        for step in range(1, grid.dims[dim]):
            target, value = grid.peer(coords, dim, step)
            there = list(coords)
            there[dim] = value
            where = index_of(there, order[stage + 1 :], len(order)) + (pl.ds(first, rows),)
            made.append(
                pltpu.make_async_remote_copy(
                    held.at[where],
                    lands[stage].at[step - 1],
                    self.send_sem.at[self.base + k, stage, step - 1],
                    self.recv_sem.at[self.base + k, stage, step - 1],
                    device_id=target,
                    device_id_type=MESH,
                )
            )
        return made

    def start(self, k, stage):
        for copy in self.copies(k, stage):
            copy.start()

    def add(self, k, stage):
        for copy in self.copies(k, stage):
            copy.wait_recv()
        held, lands, out, first, rows, colour = self.chunks[k]
        grid, coords = self.grid, self.coords
        order = grid.orders[colour][::-1]
        free = [d for d in range(len(order)) if d in order[stage + 1 :]]
        sizes = [grid.dims[d] for d in free]
        final = stage == self.stages - 1
        land = lands[stage]

        def body(i, unused):
            there = list(coords)
            rest = i
            inner = [None] * len(free)
            for pos in range(len(free) - 1, -1, -1):
                inner[pos] = rest % sizes[pos]
                rest = rest // sizes[pos]
                there[free[pos]] = inner[pos]
            where = tuple(there) + (pl.ds(first, rows),)
            total = held[where]
            if final:
                total = total.astype(jnp.float32)
            for step in range(grid.dims[order[stage]] - 1):
                total += land[(step,) + tuple(inner)].astype(total.dtype)
            if final:
                out[pl.ds(first, rows)] = total
            else:
                held[where] = total
            return unused

        if free:
            lax.fori_loop(0, math.prod(sizes), body, 0)
        else:
            body(0, 0)

    def sent(self, k):
        for stage in range(self.stages):
            for copy in self.copies(k, stage):
                copy.wait_send()


def dot_nt(left, right):
    return lax.dot_general(
        left, right, (((1,), (1,)), ((), ())), preferred_element_type=jnp.float32
    )


def dot_nn(left, right):
    return lax.dot_general(
        left, right, (((1,), (0,)), ((), ())), preferred_element_type=jnp.float32
    )


def dot_tn(left, right):
    return lax.dot_general(
        left, right, (((0,), (0,)), ((), ())), preferred_element_type=jnp.float32
    )


def normalise(value):
    offset = value - jnp.mean(value, -1, keepdims=True)
    scale = lax.rsqrt(jnp.mean(offset * offset, -1, keepdims=True) + epsilon)
    return offset * scale, scale


def norm_back(grad, unit, scale, gain):
    pulled = grad * gain
    along = jnp.mean(pulled * unit, -1, keepdims=True)
    return scale * (pulled - jnp.mean(pulled, -1, keepdims=True) - unit * along)


def gelu_pair(x):
    bell = jnp.exp(-0.5 * x * x)
    t = 1.0 / (1.0 + (0.3275911 * 0.5**0.5) * jnp.abs(x))
    tail = t * (0.5 * 0.254829592 + t * (0.5 * -0.284496736 + t * (
        0.5 * 1.421413741 + t * (0.5 * -1.453152027 + t * (0.5 * 1.061405429)))))
    tail = tail * bell
    below = jnp.where(x < 0, tail, 1.0 - tail)
    return x * below, below + (x * 0.3989422804014327) * bell


def first_lanes():
    return lax.broadcasted_iota(jnp.int32, (1, 2 * HEAD_DIM), 1) < HEAD_DIM


def stack_heads(pair):
    zero = jnp.zeros_like(pair)
    left = first_lanes()
    return jnp.concatenate([jnp.where(left, pair, zero), jnp.where(left, zero, pair)], 0)


def unstack_heads(stacked):
    rows = stacked.shape[0] // 2
    return jnp.where(first_lanes(), stacked[:rows], stacked[rows:])


def pair_shares(query_stack, key_pair, allowed):
    scores = dot_nt(query_stack, key_pair)
    if allowed is not None:
        scores = jnp.where(allowed, scores, masked_score)
    raised = jnp.exp(scores - jnp.max(scores, -1, keepdims=True))
    return raised * (1.0 / jnp.sum(raised, -1, keepdims=True))


def attend_rows(qkv, mixed, rows, span, width, allowed):
    for start in range(0, rows, span):
        here = pl.ds(start, span)
        for p in range(width // (2 * HEAD_DIM)):
            at = p * 2 * HEAD_DIM
            query = stack_heads(qkv[here, pl.ds(at, 2 * HEAD_DIM)] * jnp.bfloat16(HEAD_DIM**-0.5))
            key = qkv[here, pl.ds(width + at, 2 * HEAD_DIM)]
            value = qkv[here, pl.ds(2 * width + at, 2 * HEAD_DIM)]
            shares = pair_shares(query, key, allowed)
            both = dot_nn(shares.astype(jnp.bfloat16), value)
            mixed[here, pl.ds(at, 2 * HEAD_DIM)] = unstack_heads(both).astype(jnp.bfloat16)


def attend_back(qkv, d_mixed, d_qkv, rows, span, width, allowed):
    scale = HEAD_DIM**-0.5
    for start in range(0, rows, span):
        here = pl.ds(start, span)
        for p in range(width // (2 * HEAD_DIM)):
            at = p * 2 * HEAD_DIM
            query = stack_heads(qkv[here, pl.ds(at, 2 * HEAD_DIM)] * jnp.bfloat16(scale))
            key = qkv[here, pl.ds(width + at, 2 * HEAD_DIM)]
            value = qkv[here, pl.ds(2 * width + at, 2 * HEAD_DIM)]
            grad = stack_heads(d_mixed[here, pl.ds(at, 2 * HEAD_DIM)])
            shares = pair_shares(query, key, allowed)
            d_shares = dot_nt(grad, value)
            delta = jnp.sum(shares * d_shares, -1, keepdims=True)
            d_scores = (shares * (d_shares - delta)).astype(jnp.bfloat16)
            d_query = unstack_heads(dot_nn(d_scores, key)) * scale
            d_key = dot_tn(d_scores, query)
            d_value = dot_tn(shares.astype(jnp.bfloat16), grad)
            d_qkv[here, pl.ds(at, 2 * HEAD_DIM)] = d_query.astype(jnp.bfloat16)
            d_qkv[here, pl.ds(width + at, 2 * HEAD_DIM)] = d_key.astype(jnp.bfloat16)
            d_qkv[here, pl.ds(2 * width + at, 2 * HEAD_DIM)] = d_value.astype(jnp.bfloat16)


def row_sums(value):
    return jnp.sum(value.astype(jnp.float32), 0, keepdims=True)


def whole(shape):
    return pl.BlockSpec(shape, lambda *i: (0,) * len(shape), pipeline_mode=pl.Buffered(1))


def select(rows, columns, first):
    row = lax.broadcasted_iota(jnp.int32, (rows, columns), 0)
    column = lax.broadcasted_iota(jnp.int32, (rows, columns), 1)
    return jnp.where(row == first + column, 1.0, 0.0).astype(jnp.bfloat16)


def spread_slots(rows_of_slots, n, per, size):
    columns = n * size
    step = min(columns, 768)
    out = []
    lane = lax.broadcasted_iota(jnp.int32, (128, 1), 0)
    slot = lax.broadcasted_iota(jnp.int32, (n * per, 1), 0) // per
    for c in range(0, columns, step):
        column = lax.broadcasted_iota(jnp.int32, (1, step), 1) + c
        ones = jnp.where(column % size == lane, 1.0, 0.0).astype(jnp.bfloat16)
        laid = dot_nn(rows_of_slots, ones)
        kept = jnp.where(slot == column // size, laid, 0.0)
        out.append(jnp.sum(kept.reshape(n, per, step), 0))
    return out[0] if len(out) == 1 else jnp.concatenate(out, 1)


SMALL_ROWS = 16


def weights_kernel(grid, sizes, *refs):
    width, per_project, per_output, per_up, per_pair, places_n = sizes
    n, ndims = grid.n, len(grid.dims)
    pw, ow, uw, dw, pb, ob, ub, db, ng, nb, pt, cot = refs[:12]
    mixed0, up0, down0, mixed1, up1, cot1, own_down1, vec, vec_pair, vec_up, table = refs[12:23]
    own_mixed, own_up, own_down, own_misc, misc_f, misc_all, own_cot, cot_head = refs[23:31]
    send_sem, recv_sem, local_sem = refs[31:]
    coords = grid.coords()
    me_line = coords[-1]
    cot_copy = pltpu.make_async_copy(cot.at[:, pl.ds(0, 8)], cot_head, local_sem.at[0])
    cot_copy.start()

    misc_f[...] = jnp.zeros_like(misc_f)
    at = 0
    for ref, size in ((pb, per_pair), (ob, per_output), (ub, per_up), (db, per_output)):
        misc_f[pl.ds(at, 2), pl.ds(0, size)] = ref[...].astype(jnp.float32)
        at += 2
    for ref in (ng, nb):
        for b in range(2):
            misc_f[pl.ds(at, 2), pl.ds(0, per_output)] = ref[b].astype(jnp.float32)
            at += 2
    misc_f[pl.ds(SMALL_ROWS, places_n), pl.ds(0, per_output)] = pt[...].astype(jnp.float32)
    own_misc[...] = misc_f[...].astype(jnp.bfloat16)

    def pack(b):
        rows = per_project + per_output
        own_mixed[b] = (
            dot_nt(place_rows(rows, per_project, 0), pw[b]) + dot_nt(place_rows(rows, per_output, per_project), ow[b])
        ).astype(jnp.bfloat16)

    def place_rows(rows, size, first):
        row = lax.broadcasted_iota(jnp.int32, (rows, size), 0)
        column = lax.broadcasted_iota(jnp.int32, (rows, size), 1)
        return jnp.where(row == first + column, 1.0, 0.0).astype(jnp.bfloat16)

    pack(0)
    grid.greet(coords)

    units, chunks = [], []

    def add(own, line, dest, cuts):
        for cut in cuts:
            chunks.append((own, line, dest, *cut))
        return list(range(len(chunks) - len(cuts), len(chunks)))

    mixed_rows = per_project + per_output
    units += [add(own_mixed.at[0], None, mixed0, u) for u in pairs(mixed_rows)]
    units[0] += add(own_misc, None, misc_all, [(0, SMALL_ROWS + places_n, 0)])
    up_units = len(units)
    units += [add(own_up.at[0], None, up0, u) for u in pairs(per_up)]
    down_units = len(units)
    units += [add(own_down.at[0], None, down0, u) for u in pairs(per_up)]
    line_units = [add(own_mixed.at[1], mixed1, None, [h]) for h in halves(mixed_rows, jnp.bfloat16)]
    line_units += [add(own_up.at[1], up1, None, [h]) for h in halves(per_up, jnp.bfloat16)]
    line_units[0] += add(own_cot, cot1, None, [(0, own_cot.shape[0], 0)])
    gather = Gather(grid, coords, chunks, send_sem, recv_sem)

    def start(unit, stage):
        for k in unit:
            gather.start(k, stage)

    start(units[0], 0)
    own_up[0] = dot_nt(place_rows(per_up, per_up, 0), uw[0]).astype(jnp.bfloat16)
    own_down[0] = dw[0]
    pack(1)
    own_up[1] = dot_nt(place_rows(per_up, per_up, 0), uw[1]).astype(jnp.bfloat16)
    own_down[1] = dw[1]
    cot_copy.wait()
    for s in range(own_cot.shape[0]):
        own_cot[pl.ds(s, 1), :] = cot_head[s, 0:1, :]
    locals_ = [
        pltpu.make_async_copy(own_mixed.at[0], mixed0.at[coords], local_sem.at[0]),
        pltpu.make_async_copy(own_up.at[0], up0.at[coords], local_sem.at[1]),
        pltpu.make_async_copy(own_down.at[0], down0.at[coords], local_sem.at[2]),
        pltpu.make_async_copy(own_mixed.at[1], mixed1.at[me_line], local_sem.at[3]),
        pltpu.make_async_copy(own_up.at[1], up1.at[me_line], local_sem.at[4]),
        pltpu.make_async_copy(own_down.at[1], own_down1, local_sem.at[5]),
        pltpu.make_async_copy(own_cot, cot1.at[me_line], local_sem.at[6]),
    ]
    for copy in locals_:
        copy.start()
    misc_all[coords] = own_misc[...]
    for copy in locals_:
        copy.wait()

    def vectors():
        small = misc_all[..., 0:SMALL_ROWS, :].reshape(n * SMALL_ROWS, 128)
        singles = spread_slots(small, n, SMALL_ROWS, per_output)
        pairs = spread_slots(small, n, SMALL_ROWS, per_pair)
        ups = spread_slots(small, n, SMALL_ROWS, per_up)
        for b in range(2):
            vec[b, 0:1, :] = singles[2 + b : 3 + b]
            vec[b, 1:2, :] = singles[6 + b : 7 + b]
            vec[b, 2:4, :] = singles[8 + 2 * b : 10 + 2 * b]
            vec[b, 4:6, :] = singles[12 + 2 * b : 14 + 2 * b]
            vec[b, 6:8, :] = jnp.zeros((2, width), jnp.float32)
            vec_pair[b, :, 0:width] = pairs[b : b + 1, :width]
            vec_pair[b, :, width : 2 * width] = jnp.zeros((1, width), jnp.float32)
            vec_pair[b, :, 2 * width : 3 * width] = pairs[b : b + 1, width:]
            vec_up[b] = ups[4 + b : 5 + b]
        lead = grid.dims[0]
        total = jnp.zeros((places_n, width), jnp.float32)
        per = n // lead
        lane = lax.broadcasted_iota(jnp.int32, (128, 1), 0)
        column = lax.broadcasted_iota(jnp.int32, (1, width), 1)
        ones = jnp.where(column % per_output == lane, 1.0, 0.0).astype(jnp.bfloat16)
        owner = column // per_output
        for i in range(lead):
            rows = misc_all[i, ..., SMALL_ROWS : SMALL_ROWS + places_n, :].reshape(per * places_n, 128)
            laid = dot_nn(rows, ones)
            slot = lax.broadcasted_iota(jnp.int32, (per * places_n, 1), 0) // places_n + i * per
            kept = jnp.where(slot == owner, laid, 0.0)
            total += jnp.sum(kept.reshape(per, places_n, width), 0)
        table[...] = total.astype(jnp.bfloat16)

    count = len(units)
    line_ticks = {count - 6: line_units[:1], count - 4: line_units[1:2], count - 1: line_units[2:]} if count >= 7 else {0: line_units}
    for tick in range(1, count + ndims):
        for stage in range(1, ndims + 1):
            u = tick - stage
            if not 0 <= u < count:
                continue
            for k in units[u]:
                gather.landed(k, stage - 1)
                if stage < ndims:
                    gather.start(k, stage)
            if stage == 1:
                if u + 1 < count:
                    start(units[u + 1], 0)
                for unit in line_ticks.get(u, []):
                    start(unit, 0)
            if stage == ndims and u == 0:
                vectors()
    for unit in line_units:
        for k in unit:
            gather.landed(k, 0)
            gather.sent(k, 0, 1)
    for unit in units:
        for k in unit:
            gather.sent(k, 0, ndims)


def pairs(rows):
    if rows % 32:
        return [[(0, rows, 0)]]
    return [[(r, 16, 0), (r + 16, 16, 1)] for r in range(0, rows, 32)]


def gather_weights(grid, arrays, cid):
    project_weight, output_weight, up_weight, down_weight, project_bias = arrays[:5]
    width = project_weight.shape[1]
    per_project, per_output, per_up = project_weight.shape[2], output_weight.shape[2], up_weight.shape[2]
    per_pair = project_bias.shape[1]
    places_n = arrays[10].shape[0]
    segs = arrays[11].shape[0]
    n = grid.n
    low, full = jnp.bfloat16, jnp.float32
    mixed_rows = per_project + per_output
    misc_rows = SMALL_ROWS + places_n
    fs = grid.fsdp
    count = 2 + sum(len(u) for r in (mixed_rows, per_up, per_up) for u in pairs(r)) + sum(len(halves(r, low)) for r in (mixed_rows, per_up))
    vmem, anywhere = pl.BlockSpec(memory_space=pltpu.VMEM), pl.BlockSpec(memory_space=pl.ANY)

    def shape(s, d):
        return jax.ShapeDtypeStruct(s, d)

    return pl.pallas_call(
        functools.partial(weights_kernel, grid, (width, per_project, per_output, per_up, per_pair, places_n)),
        in_specs=[vmem] * 11 + [anywhere],
        out_specs=[anywhere] * 7 + [vmem] * 4,
        out_shape=[
            shape((*grid.dims, mixed_rows, width), low), shape((*grid.dims, per_up, width), low), shape((*grid.dims, per_up, width), low),
            shape((fs, mixed_rows, width), low), shape((fs, per_up, width), low), shape((fs, segs, width), full), shape((per_up, width), low),
            shape((2, 8, width), full), shape((2, 1, 3 * width), full), shape((2, 1, n * per_up), full), shape((places_n, width), low),
        ],
        scratch_shapes=[
            pltpu.VMEM((2, mixed_rows, width), low), pltpu.VMEM((2, per_up, width), low), pltpu.VMEM((2, per_up, width), low),
            pltpu.VMEM((misc_rows, 128), low), pltpu.VMEM((misc_rows, 128), full), pltpu.VMEM((*grid.dims, misc_rows, 128), low),
            pltpu.VMEM((segs, width), full), pltpu.VMEM((segs, 8, width), full),
        ]
        + grid.sems(count)
        + [pltpu.SemaphoreType.DMA((7,))],
        compiler_params=pltpu.CompilerParams(collective_id=cid, has_side_effects=True, vmem_limit_bytes=56 * 2**20),
        name="gather_weights",
    )(*arrays)


def forward_rows(x_low, x, w, r, rows, span, allowed, hook=lambda name: None):
    width = x.shape[1]
    step = width
    hook("project")
    for c in range(0, 3 * width, step):
        cut = pl.ds(c, step)
        r["qkv"][:, cut] = (dot_nt(x_low, w["project"][cut, :]) + w["project_b"][:, cut]).astype(jnp.bfloat16)
    attend_rows(r["qkv"], r["mixed"], rows, span, width, allowed)
    first = x + (dot_nt(r["mixed"][...], w["output"][...]) + w["output_b"])
    if "first" in r:
        r["first"](first)
    hook("first")
    unit_one, scale_one, unit_two, scale_two = feed_forward(first, w, r, hook)
    return unit_one, scale_one, unit_two, scale_two


def feed_forward(first, w, r, hook=lambda name: None):
    unit_one, scale_one = normalise(first)
    normed = unit_one * w["gains"][0:1, :] + w["shifts"][0:1, :]
    normed_low = normed.astype(jnp.bfloat16)
    r["normed"][...] = normed_low
    hidden_units = w["up"].shape[0]
    step = normed.shape[1]
    for c in range(0, hidden_units, step):
        cut = pl.ds(c, step)
        inner = dot_nt(normed_low, w["up"][cut, :]) + w["up_b"][:, cut]
        value, slope = gelu_pair(inner)
        r["hidden"][:, cut] = value.astype(jnp.bfloat16)
        r["slope"][:, cut] = slope.astype(r["slope"].dtype)
    hook("down")
    second = normed + (dot_nn(r["hidden"][...], w["down"][...]) + w["down_b"])
    unit_two, scale_two = normalise(second)
    return unit_one, scale_one, unit_two, scale_two


def mlp_back(grad, unit_one, scale_one, unit_two, scale_two, w, r, hook=lambda name: None):
    d_second = norm_back(grad, unit_two, scale_two, w["gains"][1:2, :])
    d_down = d_second.astype(jnp.bfloat16)
    r["d_down"][...] = d_down
    hidden_units = w["up"].shape[0]
    step = grad.shape[1]
    for c in range(0, hidden_units, step):
        cut = pl.ds(c, step)
        d_hidden = dot_nt(d_down, w["down"][cut, :])
        r["d_inner"][:, cut] = (d_hidden * r["slope"][:, cut].astype(jnp.float32)).astype(jnp.bfloat16)
    hook("up")
    d_normed = d_second + dot_nn(r["d_inner"][...], w["up"][...])
    d_first = norm_back(d_normed, unit_one, scale_one, w["gains"][0:1, :])
    sums = (
        row_sums(d_normed * unit_one), row_sums(grad * unit_two), row_sums(d_normed), row_sums(grad),
        row_sums(d_down), row_sums(r["d_inner"][...]),
    )
    return d_first, sums


def small_of(vec, vec_pair, vec_up, b):
    return {
        "project_b": vec_pair.at[b], "output_b": vec[b, 0:1, :], "up_b": vec_up.at[b], "down_b": vec[b, 1:2, :],
        "gains": vec[b, 2:4, :], "shifts": vec[b, 4:6, :],
    }


def unpack_mixed(grid, mixed, project, output, per_project):
    rows, width = mixed.shape[-2:]
    per_output = rows - per_project
    for d in range(grid.n):
        where, rest = [], d
        for size in grid.dims[::-1]:
            where.append(rest % size)
            rest //= size
        part = mixed[tuple(where[::-1])]
        project[pl.ds(d * per_project, per_project), :] = part[:per_project]
        output[pl.ds(d * per_output, per_output), :] = part[per_project:]


def spread(events, points):
    return [events[len(events) * p // points : len(events) * (p + 1) // points] for p in range(points)]


def segment_forward_kernel(grid, tile, steps, per_project, *refs):
    (tokens, grads, mixed0, up0, down0, vec, vec_pair, vec_up, line_mixed, line_up, line_cot, own_down) = refs[:12]
    names = ("qkv", "mixed", "normed", "hidden", "d_down", "d_inner", "d_first", "seg_low", "norm_sums", "up_sums")
    r = dict(zip(names, refs[12:22]))
    project_out, output_out, all_first, mixed1, up1, down1, all_cot = refs[22:29]
    r["slope"], held_mixed, project, output, up, down, own_first = refs[29:36]
    send_sem, recv_sem, local_sem = refs[36:]
    w = small_of(vec, vec_pair, vec_up, 0)
    w.update(project=project, output=output, up=up, down=down)
    width = tokens.shape[1]
    step = pl.program_id(0)
    last = steps - 1
    ndims = len(grid.dims)
    coords = grid.coords()
    loads = [pltpu.make_async_copy(*p, local_sem.at[i]) for i, p in enumerate(
        ((mixed0, held_mixed), (up0, up), (down0, down)))]
    stores = [pltpu.make_async_copy(*p, local_sem.at[3 + i]) for i, p in enumerate(
        ((project, project_out), (output, output_out)))]
    here = (coords[:-1]) + (slice(None),)
    lines = [pltpu.make_async_copy(a, b.at[here], local_sem.at[5 + i]) for i, (a, b) in enumerate(
        ((line_mixed, mixed1), (line_up, up1), (line_cot, all_cot)))]
    lines.append(pltpu.make_async_copy(own_down, down1.at[coords], local_sem.at[8]))
    keep_first = pltpu.make_async_copy(own_first, all_first.at[coords], local_sem.at[9])

    chunks, groups = [], []
    for own, line, dest, rows in (
        (None, line_mixed, mixed1, line_mixed.shape[1]), (None, line_up, up1, line_up.shape[1]), (own_down, None, down1, own_down.shape[0])
    ):
        cuts = halves(rows, jnp.bfloat16)
        groups.append(list(range(len(chunks), len(chunks) + len(cuts))))
        chunks += [(own, line, dest, *cut) for cut in cuts]
    groups[0].append(len(chunks))
    chunks.append((None, line_cot, all_cot, 0, line_cot.shape[1], 1))
    first_chunk = len(chunks)
    chunks.append((own_first, None, all_first, 0, own_first.shape[0], 0))
    gather = Gather(grid, coords, chunks, send_sem, recv_sem)

    ticks = ndims - 1 + len(groups)

    def go(tick):
        if tick == 1:
            for copy in lines:
                copy.wait()
        for g in range(len(groups) - 1, -1, -1):
            stage = tick - g + 1
            late = chunks[groups[g][0]][1] is None
            for k in groups[g]:
                if late and tick == 0:
                    gather.start(k, 0)
                if (late and stage == 1) or 1 < stage <= ndims:
                    gather.landed(k, stage - 1)
                if 1 <= stage < ndims:
                    gather.start(k, stage)

    plan = {}
    for tick in range(1, ticks - 1):
        at = min(2 * steps - 1, round(2 * steps * (tick - 0.65) / (ticks - 3)) - 1)
        plan.setdefault(at, []).append(tick)

    def at_point(which):
        for at, some in plan.items():
            if at % 2 == which:

                @pl.when(step == at // 2)
                def _(some=some):
                    for tick in some:
                        go(tick)

    first_points = ["first", "down", "back", "up"]
    first_events = [[] for unused in first_points]
    stages = list(range(ndims))
    for i, stage in enumerate(stages):
        first_events[min(i, len(first_points) - 1)].append(stage)

    def first_point(name):
        @pl.when(step == last)
        def _():
            for stage in first_events[first_points.index(name)]:
                if stage == 0:
                    keep_first.start()
                else:
                    gather.landed(first_chunk, stage - 1)
                    if stage == 1:
                        keep_first.wait()
                gather.start(first_chunk, stage)

    @pl.when(step == 0)
    def _():
        for copy in loads:
            copy.start()
        grid.greet(coords)
        go(0)
        for copy in lines:
            copy.start()
        loads[0].wait()
        unpack_mixed(grid, held_mixed, project, output, per_project)
        for copy in stores:
            copy.start()

    def hook(name):
        if name == "first":
            first_point("first")

            @pl.when(step == 0)
            def _():
                for copy in loads[1:]:
                    copy.wait()

            at_point(0)
        if name == "down":
            first_point("down")
        if name == "up":
            first_point("up")

    def take_first(first):
        for s in range(tile // SEG_LEN):
            own_first[pl.ds(step * (tile // SEG_LEN) + s, 1), :] = first[s * SEG_LEN : s * SEG_LEN + 1]

    r["first"] = take_first
    x_low = tokens[...]
    x = x_low.astype(jnp.float32)
    unit_one, scale_one, unit_two, scale_two = forward_rows(x_low, x, w, r, tile, SEG_LEN, None, hook)
    seg_out = unit_two * w["gains"][1:2, :] + w["shifts"][1:2, :]
    r["seg_low"][...] = seg_out.astype(jnp.bfloat16)
    first_point("back")
    place = lax.broadcasted_iota(jnp.int32, (tile, 1), 0) % SEG_LEN
    grad = jnp.where(place == 0, 0.0, grads[...])
    d_first, sums = mlp_back(grad, unit_one, scale_one, unit_two, scale_two, w, r, hook)
    r["d_first"][...] = d_first
    gathered = jnp.concatenate(list(sums[:5]) + [jnp.zeros((3, width), jnp.float32)], 0)

    @pl.when(step == 0)
    def _():
        r["norm_sums"][...] = jnp.zeros_like(r["norm_sums"])
        r["up_sums"][...] = jnp.zeros_like(r["up_sums"])

    r["norm_sums"][...] += gathered
    r["up_sums"][...] += jnp.broadcast_to(sums[5], r["up_sums"].shape)

    at_point(1)

    @pl.when(step == last)
    def _():
        go(ticks - 1)
        for g in range(len(groups)):
            for k in groups[g]:
                gather.sent(k, 1 if chunks[k][1] is not None else 0, ndims)
        gather.landed(first_chunk, ndims - 1)
        gather.sent(first_chunk, 0, ndims)
        for copy in stores:
            copy.wait()


def segment_forward(grid, tokens, grads, mixed0, up0, down0, smalls, lines, per_project, cid):
    rows, width = tokens.shape
    per_up = up0.shape[-2]
    mixed_rows = mixed0.shape[-2]
    hidden_units = per_up * grid.n
    tile = 2 * SEG_LEN
    steps = rows // tile
    segs = rows // SEG_LEN
    low, full = jnp.bfloat16, jnp.float32
    up0, down0 = up0.reshape(hidden_units, width), down0.reshape(hidden_units, width)
    count = 2 + sum(len(halves(r, low)) for r in (mixed_rows, per_up, per_up))
    vmem, anywhere = pl.BlockSpec(memory_space=pltpu.VMEM), pl.BlockSpec(memory_space=pl.ANY)

    def cut(columns):
        return pl.BlockSpec((tile, columns), lambda i: (i, 0))

    def shape(columns, dtype):
        return jax.ShapeDtypeStruct((rows, columns), dtype)

    return pl.pallas_call(
        functools.partial(segment_forward_kernel, grid, tile, steps, per_project),
        grid=(steps,),
        in_specs=[cut(width), cut(width)] + [anywhere] * 3 + [whole(s.shape) for s in (*smalls, *lines)],
        out_specs=[
            cut(3 * width), cut(width), cut(width), cut(hidden_units), cut(width), cut(hidden_units), cut(width), cut(width),
            pl.BlockSpec((8, width), lambda i: (0, 0)), pl.BlockSpec((8, hidden_units), lambda i: (0, 0)),
        ]
        + [anywhere] * 7,
        out_shape=[
            shape(3 * width, low), shape(width, low), shape(width, low), shape(hidden_units, low), shape(width, low),
            shape(hidden_units, low), shape(width, full), shape(width, low),
            jax.ShapeDtypeStruct((8, width), full), jax.ShapeDtypeStruct((8, hidden_units), full),
            jax.ShapeDtypeStruct((3 * width, width), low), jax.ShapeDtypeStruct((width, width), low),
            jax.ShapeDtypeStruct((*grid.dims, segs, width), full),
            jax.ShapeDtypeStruct((*grid.dims, mixed_rows, width), low),
            jax.ShapeDtypeStruct((*grid.dims, per_up, width), low), jax.ShapeDtypeStruct((*grid.dims, per_up, width), low),
            jax.ShapeDtypeStruct((*grid.dims, segs, width), full),
        ],
        scratch_shapes=[
            pltpu.VMEM((tile, hidden_units), low), pltpu.VMEM((*grid.dims, mixed_rows, width), low),
            pltpu.VMEM((3 * width, width), low), pltpu.VMEM((width, width), low),
            pltpu.VMEM((hidden_units, width), low), pltpu.VMEM((hidden_units, width), low), pltpu.VMEM((segs, width), full),
        ]
        + grid.sems(count)
        + [pltpu.SemaphoreType.DMA((10,))],
        compiler_params=pltpu.CompilerParams(collective_id=cid, has_side_effects=True, vmem_limit_bytes=60 * 2**20),
        name="segment_forward",
    )(tokens, grads, mixed0, up0, down0, *smalls, *lines)


def own_columns(value, first, size):
    return dot_nn(value, select(value.shape[1], size, first)).astype(jnp.bfloat16)


def own_sums(value, first, size):
    row = lax.broadcasted_iota(jnp.int32, (value.shape[1], size), 0)
    column = lax.broadcasted_iota(jnp.int32, (value.shape[1], size), 1)
    ones = jnp.where(row == first + column, 1.0, 0.0)
    return jnp.dot(value, ones, precision=highest, preferred_element_type=jnp.float32)


def document_of(placed, long_total):
    long_docs = long_total // LONG_SEGS
    is_long = placed < long_total
    rest = placed - long_total
    doc = jnp.where(is_long, placed // LONG_SEGS, long_docs + rest // SHORT_SEGS)
    return doc, jnp.where(is_long, placed % LONG_SEGS, rest % SHORT_SEGS)


def cross_kernel(grid, sizes, *refs):
    per_project, per_output, per_up, per_pair = sizes
    (firsts, grads, placed_row, placed_col, mixed1, up1, down1, up0, down0, vec, vec_pair, vec_up, table) = refs[:13]
    g_project, g_output, g_up, g_down, z_up, z_down, smalls, g_table, cross_own, d_first_own = refs[13:23]
    names = ("qkv", "slope", "d_mixed", "mixed", "normed", "hidden", "d_down", "d_inner", "d_qkv")
    r = dict(zip(names, refs[23:32]))
    held_mixed, project, output, up, down, z_up_w, z_down_w, z_slope, z_normed, z_hidden, z_d_down, z_d_inner, rows_f = refs[32:45]
    local_sem = refs[45]
    loads = [pltpu.make_async_copy(*p, local_sem.at[i]) for i, p in enumerate(
        ((up0, z_up_w), (down0, z_down_w), (mixed1, held_mixed), (up1, up), (down1, down)))]
    for copy in loads:
        copy.start()
    slots, width = firsts.shape
    places_n = table.shape[0]
    me = grid.flat()
    per_slots = slots // grid.n

    w0 = small_of(vec, vec_pair, vec_up, 0)
    w0.update(up=z_up_w, down=z_down_w)
    r0 = {"normed": z_normed, "hidden": z_hidden, "slope": z_slope, "d_down": z_d_down, "d_inner": z_d_inner}

    def hook0(name):
        if name == "down":
            loads[1].wait()

    loads[0].wait()
    kept0 = feed_forward(firsts[...], w0, r0, hook0)
    seg_first = kept0[2] * w0["gains"][1:2, :] + w0["shifts"][1:2, :]
    doc_row, unused = document_of(placed_row[...], slots // 2)
    doc_col, place_col = document_of(placed_col[...], slots // 2)
    picker = place_col == lax.broadcasted_iota(jnp.int32, (slots, places_n), 1)
    picker_f = jnp.where(picker, 1.0, 0.0)
    x = seg_first + dot_nn(picker_f.astype(jnp.bfloat16), table[...])

    w = small_of(vec, vec_pair, vec_up, 1)
    w.update(project=project, output=output, up=up, down=down)
    loads[2].wait()
    unpack_mixed(grid, held_mixed, project, output, per_project)
    x_low = x.astype(jnp.bfloat16)
    allowed = doc_col == doc_row
    allowed = jnp.concatenate([allowed, allowed], 0)

    def hook(name):
        if name == "first":
            loads[3].wait()
        if name == "down":
            loads[4].wait()

    kept = forward_rows(x_low, x, w, r, slots, slots, allowed, hook)
    mine = pl.ds(pl.multiple_of(me * per_slots, per_slots), per_slots)
    rows_f[...] = kept[2] * w["gains"][1:2, :] + w["shifts"][1:2, :]
    cross_own[...] = rows_f[mine, :]
    d_first, sums = mlp_back(grads[...], *kept, w, r)
    branch = d_first.astype(jnp.bfloat16)
    r["d_mixed"][...] = dot_nn(branch, output[...]).astype(jnp.bfloat16)
    attend_back(r["qkv"], r["d_mixed"], r["d_qkv"], slots, slots, width, allowed)
    d_x = d_first + dot_nn(r["d_qkv"][...], project[...])

    g_project[...] = dot_tn(x_low, own_columns(r["d_qkv"][...], me * per_project, per_project))
    g_output[...] = dot_tn(r["mixed"][...], own_columns(branch, me * per_output, per_output))
    g_up[...] = dot_tn(r["normed"][...], own_columns(r["d_inner"][...], me * per_up, per_up))
    g_down[...] = dot_tn(own_columns(r["hidden"][...], me * per_up, per_up), r["d_down"][...])
    smalls[...] = jnp.zeros_like(smalls)
    norm_rows = jnp.concatenate(list(sums[:5]) + [row_sums(branch), jnp.zeros((2, width), jnp.float32)], 0)
    smalls[0:8, 0:per_output] = own_sums(norm_rows, me * per_output, per_output)
    smalls[8:16, 0:per_up] = own_sums(jnp.broadcast_to(sums[5], (8, sums[5].shape[1])), me * per_up, per_up)
    qkv_sums = row_sums(r["d_qkv"][...])
    pair = jnp.concatenate([qkv_sums[:, :width], qkv_sums[:, 2 * width :]], 1)
    smalls[16:24, 0:per_pair] = own_sums(jnp.broadcast_to(pair, (8, 2 * width)), me * per_pair, per_pair)
    g_table[...] = lax.dot_general(
        picker_f, own_sums(d_x, me * per_output, per_output), (((0,), (0,)), ((), ())),
        precision=highest, preferred_element_type=jnp.float32,
    )

    d_first0, sums = mlp_back(d_x, *kept0, w0, r0)
    rows_f[...] = d_first0
    d_first_own[...] = rows_f[mine, :]
    z_up[...] = dot_tn(own_columns(z_d_inner[...], me * per_up, per_up), z_normed[...])
    z_down[...] = dot_tn(own_columns(z_hidden[...], me * per_up, per_up), z_d_down[...])
    norm_rows = jnp.concatenate(list(sums[:5]) + [jnp.zeros((3, width), jnp.float32)], 0)
    smalls[24:32, 0:per_output] = own_sums(norm_rows, me * per_output, per_output)
    smalls[32:40, 0:per_up] = own_sums(jnp.broadcast_to(sums[5], (8, sums[5].shape[1])), me * per_up, per_up)


def cross_block(grid, firsts, grads, placement, mixed1, up1, down1, up0, down0, smalls, table, sizes):
    slots, width = firsts.shape
    per_project, per_output, per_up, per_pair = sizes
    hidden_units = per_up * grid.n
    low, full = jnp.bfloat16, jnp.float32
    per_slots = slots // grid.n
    flat = lambda ref: ref.reshape(hidden_units, width)
    vmem, anywhere = pl.BlockSpec(memory_space=pltpu.VMEM), pl.BlockSpec(memory_space=pl.ANY)
    outs = [
        (width, per_project), (width, per_output), (width, per_up), (per_up, width), (per_up, width), (per_up, width),
        (40, 128), (table.shape[0], per_output), (per_slots, width), (per_slots, width),
    ]

    def held(*shape, dtype=low):
        return pltpu.VMEM(shape, dtype)

    return pl.pallas_call(
        functools.partial(cross_kernel, grid, sizes),
        in_specs=[vmem] * 4 + [anywhere] * 5 + [vmem] * 4,
        out_specs=[vmem] * len(outs),
        out_shape=[jax.ShapeDtypeStruct(s, full) for s in outs],
        scratch_shapes=[
            held(slots, 3 * width), held(slots, hidden_units), held(slots, width), held(slots, width), held(slots, width),
            held(slots, hidden_units), held(slots, width), held(slots, hidden_units), held(slots, 3 * width),
            held(*mixed1.shape), held(3 * width, width), held(width, width), held(hidden_units, width), held(hidden_units, width),
            held(hidden_units, width), held(hidden_units, width), held(slots, hidden_units), held(slots, width),
            held(slots, hidden_units), held(slots, width), held(slots, hidden_units), held(slots, width, dtype=full),
            pltpu.SemaphoreType.DMA((5,)),
        ],
        compiler_params=pltpu.CompilerParams(vmem_limit_bytes=62 * 2**20),
        name="cross_block",
    )(firsts, grads, placement[None, :], placement[:, None], mixed1, flat(up1), flat(down1), flat(up0), flat(down0), *smalls, table)


def segment_backward_kernel(tile, qkv, d_first, cls_grad, seg_low, cls_out, project, output, d_qkv, d_branch, d_x, layer_out, sums_qkv, sums_out, d_mixed):
    width = d_first.shape[1]
    place = lax.broadcasted_iota(jnp.int32, (tile, 1), 0)
    grad, out = d_first[...], seg_low[...].astype(jnp.float32)
    step = pl.program_id(0)
    for s in range(tile // SEG_LEN):
        here = pl.ds(step * (tile // SEG_LEN) + s, 1)
        grad = jnp.where(place == s * SEG_LEN, cls_grad[here, :], grad)
        out = jnp.where(place == s * SEG_LEN, cls_out[here, :], out)
    layer_out[...] = out.astype(jnp.bfloat16)
    branch = grad.astype(jnp.bfloat16)
    d_branch[...] = branch
    d_mixed[...] = dot_nn(branch, output[...]).astype(jnp.bfloat16)
    attend_back(qkv, d_mixed, d_qkv, tile, SEG_LEN, width, None)
    d_x[...] = grad + dot_nn(d_qkv[...], project[...])

    @pl.when(step == 0)
    def _():
        sums_qkv[...] = jnp.zeros_like(sums_qkv)
        sums_out[...] = jnp.zeros_like(sums_out)

    sums_qkv[...] += jnp.broadcast_to(row_sums(d_qkv[...]), sums_qkv.shape)
    sums_out[...] += jnp.broadcast_to(row_sums(branch), sums_out.shape)


def segment_backward(qkv, d_first, cls_grad, seg_low, cls_out, project, output):
    rows, width = d_first.shape
    tile = 2 * SEG_LEN
    low, full = jnp.bfloat16, jnp.float32

    def cut(columns):
        return pl.BlockSpec((tile, columns), lambda i: (i, 0))

    return pl.pallas_call(
        functools.partial(segment_backward_kernel, tile),
        grid=(rows // tile,),
        in_specs=[
            cut(3 * width), cut(width), whole(cls_grad.shape), cut(width), whole(cls_out.shape), whole(project.shape), whole(output.shape),
        ],
        out_specs=[
            cut(3 * width), cut(width), cut(width), cut(width),
            pl.BlockSpec((8, 3 * width), lambda i: (0, 0)), pl.BlockSpec((8, width), lambda i: (0, 0)),
        ],
        out_shape=[
            jax.ShapeDtypeStruct((rows, 3 * width), low), jax.ShapeDtypeStruct((rows, width), low),
            jax.ShapeDtypeStruct((rows, width), full), jax.ShapeDtypeStruct((rows, width), low),
            jax.ShapeDtypeStruct((8, 3 * width), full), jax.ShapeDtypeStruct((8, width), full),
        ],
        scratch_shapes=[pltpu.VMEM((tile, width), jnp.bfloat16)],
        compiler_params=pltpu.CompilerParams(vmem_limit_bytes=60 * 2**20),
        name="segment_backward",
    )(qkv, d_first, cls_grad, seg_low, cls_out, project, output)


def sum_kernel(grid, chunk_list, nparts, *refs):
    given, outs = refs[:nparts], refs[nparts : 2 * nparts]
    held = refs[2 * nparts : 3 * nparts]
    lands = refs[3 * nparts : -3]
    send_sem, recv_sem, load_sem = refs[-3:]
    ndims = len(grid.dims)
    coords = grid.coords()
    loads = [pltpu.make_async_copy(given[a], held[a], load_sem.at[a]) for a in range(nparts)]
    for load in loads:
        load.start()
    grid.greet(coords)
    chunks, groups = [], {}
    for k, (a, first, count, colour) in enumerate(chunk_list):
        groups.setdefault(a, []).append(k)
        chunks.append((held[a], lands[k * ndims : (k + 1) * ndims], outs[a], first, count, colour))
    scatter = Scatter(grid, coords, chunks, send_sem, recv_sem)
    for tick in range(nparts + ndims):
        for a in range(nparts):
            stage = tick - a
            if not 0 <= stage <= ndims:
                continue
            if stage == 0:
                loads[a].wait()
            for k in groups[a]:
                if stage >= 1:
                    scatter.add(k, stage - 1)
                if stage < ndims:
                    scatter.start(k, stage)
    for k in range(len(chunks)):
        scatter.sent(k)


def sum_to_owners(grid, parts, cid):
    chunk_list = [(a, *h) for a, p in enumerate(parts) for h in halves(p.shape[1], p.dtype)]
    nparts = len(parts)
    shaped = [p.reshape(tuple(grid.dims) + p.shape[1:]) for p in parts]
    lands = []
    for a, first, count, colour in chunk_list:
        lands += Scatter.landing(grid, count, parts[a].shape[2], parts[a].dtype, colour)
    return pl.pallas_call(
        functools.partial(sum_kernel, grid, chunk_list, nparts),
        out_shape=[jax.ShapeDtypeStruct(p.shape[1:], jnp.float32) for p in parts],
        in_specs=[pl.BlockSpec(memory_space=pl.ANY)] * nparts,
        out_specs=[pl.BlockSpec(memory_space=pltpu.VMEM)] * nparts,
        scratch_shapes=[pltpu.VMEM(s.shape, s.dtype) for s in shaped] + lands + grid.sems(len(chunk_list)) + [pltpu.SemaphoreType.DMA((nparts,))],
        compiler_params=pltpu.CompilerParams(collective_id=cid, has_side_effects=True, vmem_limit_bytes=56 * 2**20),
        name="sum_to_owners",
    )(*shaped)


class Held:
    def __init__(self, value):
        self.value = value

    @property
    def shape(self):
        return self.value.shape

    @property
    def dtype(self):
        return self.value.dtype

    @staticmethod
    def plain(where):
        where = where if isinstance(where, tuple) else (where,)
        return tuple(slice(w.start, w.start + w.size) if isinstance(w, pl.Slice) else w for w in where)

    def __getitem__(self, where):
        return self.value[self.plain(where)]

    def __setitem__(self, where, value):
        self.value = self.value.at[self.plain(where)].set(value)


def cross_plain(grid, firsts, grads, placement, mixed1, up1, down1, up0, down0, smalls, table, sizes):
    slots, width = firsts.shape
    per_project, per_output, per_up, per_pair = sizes
    hidden_units = per_up * grid.n
    me = grid.flat()
    vec, vec_pair, vec_up = smalls

    def weights(b, up, down):
        return {
            "project_b": vec_pair[b], "output_b": vec[b, 0:1, :], "up_b": vec_up[b], "down_b": vec[b, 1:2, :],
            "gains": vec[b, 2:4, :], "shifts": vec[b, 4:6, :],
            "up": up.reshape(hidden_units, width), "down": down.reshape(hidden_units, width),
        }

    def blank(columns):
        return Held(jnp.zeros((slots, columns), jnp.bfloat16))

    def store():
        made = {k: blank(width) for k in ("mixed", "normed", "d_down", "d_mixed")}
        made.update({k: blank(hidden_units) for k in ("hidden", "slope", "d_inner")})
        made.update(qkv=blank(3 * width), d_qkv=blank(3 * width))
        return made

    def cut(matrix, size, axis=1):
        return lax.dynamic_slice_in_dim(matrix, me * size, size, axis)

    w0, w, r0, r = weights(0, up0, down0), weights(1, up1, down1), store(), store()
    parts = mixed1.reshape(grid.n, -1, width)
    w["project"] = parts[:, :per_project].reshape(3 * width, width)
    w["output"] = parts[:, per_project:].reshape(width, width)
    kept0 = feed_forward(firsts, w0, r0)
    seg_first = kept0[2] * w0["gains"][1:2, :] + w0["shifts"][1:2, :]
    doc, place = document_of(placement, slots // 2)
    picker = jnp.where(place[:, None] == jnp.arange(table.shape[0], dtype=jnp.int32)[None, :], 1.0, 0.0)
    x = seg_first + dot_nn(picker.astype(jnp.bfloat16), table)
    x_low = x.astype(jnp.bfloat16)
    allowed = doc[:, None] == doc[None, :]
    allowed = jnp.concatenate([allowed, allowed], 0)
    kept = forward_rows(x_low, x, w, r, slots, slots, allowed)
    out = kept[2] * w["gains"][1:2, :] + w["shifts"][1:2, :]
    d_first, sums = mlp_back(grads, *kept, w, r)
    branch = d_first.astype(jnp.bfloat16)
    r["d_mixed"][...] = dot_nn(branch, w["output"]).astype(jnp.bfloat16)
    attend_back(r["qkv"], r["d_mixed"], r["d_qkv"], slots, slots, width, allowed)
    d_x = d_first + dot_nn(r["d_qkv"][...], w["project"])
    d_first0, sums0 = mlp_back(d_x, *kept0, w0, r0)
    qkv_sums = row_sums(r["d_qkv"][...])
    pair = jnp.concatenate([qkv_sums[:, :width], qkv_sums[:, 2 * width :]], 1)

    def laid(rows, size):
        rows = cut(rows, size)
        return jnp.pad(rows, ((0, 8 - rows.shape[0]), (0, 128 - size)))

    own_small = jnp.concatenate(
        [
            laid(jnp.concatenate(list(sums[:5]) + [row_sums(branch)], 0), per_output), laid(sums[5], per_up), laid(pair, per_pair),
            laid(jnp.concatenate(list(sums0[:5]), 0), per_output), laid(sums0[5], per_up),
        ],
        0,
    )
    g_table = lax.dot_general(picker, cut(d_x, per_output), (((0,), (0,)), ((), ())), precision=highest)
    per_slots = slots // grid.n
    return (
        dot_tn(x_low, cut(r["d_qkv"][...], per_project)), dot_tn(r["mixed"][...], cut(branch, per_output)),
        dot_tn(r["normed"][...], cut(r["d_inner"][...], per_up)), dot_tn(cut(r["hidden"][...], per_up), r["d_down"][...]),
        dot_tn(cut(r0["d_inner"][...], per_up), r0["normed"][...]), dot_tn(cut(r0["hidden"][...], per_up), r0["d_down"][...]),
        own_small, g_table, cut(out, per_slots, 0), cut(d_first0, per_slots, 0),
    )


def shards(
    grid,
    tokens,
    cotangent,
    placement,
    project_weight,
    project_bias,
    output_weight,
    output_bias,
    up_weight,
    up_bias,
    down_weight,
    down_bias,
    norm_gain,
    norm_bias,
    position_table,
):
    n = grid.n
    seg_count, seg_len, width = tokens.shape
    slots, rows = placement.shape[0], seg_count * seg_len
    per_project, per_output = project_weight.shape[2], output_weight.shape[2]
    per_pair, per_up = project_bias.shape[1], up_bias.shape[1]
    sizes = (per_project, per_output, per_up, per_pair)
    low_tokens = tokens.reshape(rows, width)

    mixed0, up0, down0, *lines, vec, vec_pair, vec_up, table = gather_weights(
        grid,
        [project_weight, output_weight, up_weight, down_weight, project_bias, output_bias, up_bias, down_bias,
         norm_gain, norm_bias, position_table, cotangent],
        0,
    )
    smalls = [vec, vec_pair, vec_up]
    (qkv, mixed, normed, hidden, d_down, d_inner, d_first, seg_low, norm_sums, up_sums, project, output, all_first,
     mixed1, up1, down1, all_cot) = segment_forward(
        grid, low_tokens, cotangent.reshape(rows, width), mixed0, up0, down0, smalls, lines, per_project, 1
    )
    g_project, g_output, g_up, g_down, z_up, z_down, own_small, g_table, cross_own, cls_grad = (cross_block if slots <= 256 else cross_plain)(
        grid, all_first.reshape(slots, width), all_cot.reshape(slots, width), placement, mixed1, up1, down1, up0, down0,
        smalls, table, sizes,
    )
    d_qkv, d_branch, d_x, layer_out, sums_qkv, sums_out = segment_backward(
        qkv, d_first, cls_grad, seg_low, cross_own, project, output
    )
    grad_project, grad_output, grad_up, grad_down = [
        dot_tn(left, right).astype(jnp.bfloat16).reshape(n, -1, width)
        for left, right in ((d_qkv, low_tokens), (d_branch, mixed), (d_inner, normed), (hidden, d_down))
    ]

    def per_device(vector):
        return vector.reshape(vector.shape[:-1] + (n, -1))

    seg_small = jnp.concatenate(
        [
            per_device(jnp.concatenate([sums_qkv[0, :width], sums_qkv[0, 2 * width :]])), per_device(sums_out[0]),
            per_device(up_sums[0]), per_device(norm_sums[4]),
            per_device(norm_sums[:4]).transpose(1, 0, 2).reshape(n, -1),
        ],
        1,
    )
    small_size = seg_small.shape[1]
    small_width = -(-small_size // 128) * 128
    seg_small = jnp.pad(seg_small[:, None], ((0, 0), (0, 7), (0, small_width - small_size)))
    down_sum, up_sum, mixed_sum, small_sum = sum_to_owners(
        grid, [grad_down, grad_up, jnp.concatenate([grad_project, grad_output], 1), seg_small], 2
    )
    down_sum += z_down
    up_sum += z_up
    cuts, at = [], 0
    for size in (per_pair, per_output, per_up, per_output, 4 * per_output):
        cuts.append(small_sum[0, at : at + size])
        at += size
    pair_g = jnp.stack([cuts[0], own_small[16, :per_pair]])
    out_g = jnp.stack([cuts[1], own_small[5, :per_output]])
    up_g = jnp.stack([cuts[2] + own_small[32, :per_up], own_small[8, :per_up]])
    down_g = jnp.stack([cuts[3] + own_small[28, :per_output], own_small[4, :per_output]])
    norm_g = jnp.stack([cuts[4].reshape(4, per_output) + own_small[24:28, :per_output], own_small[0:4, :per_output]])
    return (
        layer_out.reshape(tokens.shape),
        d_x.reshape(tokens.shape),
        jnp.stack([mixed_sum[:per_project].T, g_project]),
        pair_g,
        jnp.stack([mixed_sum[per_project:].T, g_output]),
        out_g,
        jnp.stack([up_sum.T, g_up]),
        up_g,
        jnp.stack([down_sum, g_down]),
        down_g,
        norm_g[:, :2],
        norm_g[:, 2:],
        g_table,
    )


def solution(mesh):
    grid = Grid(mesh)
    rows, cols, last = P(AXES, None, None), P(None, AXES), P(None, None, AXES)
    middle = P(None, AXES, None)
    return jax.shard_map(
        functools.partial(shards, grid),
        mesh=mesh,
        in_specs=(
            rows, rows, P(), last, cols, last, cols, last, cols, middle, cols, last, last, cols,
        ),
        out_specs=(rows, rows, last, cols, last, cols, last, cols, middle, cols, last, last, cols),
        check_vma=False,
    )
```

time: 2100 us -> 404 us (0.19)
  waiting for transfers between devices: 1060 us -> 0 us
  blocking collectives: 643 us -> 0 us
  Pallas kernels: 0 us -> 350 us
  matrix products: 176 us -> 21.5 us
  local copies, waits for them, and re-layouts: 117 us -> 14.4 us
  other arithmetic: 74.2 us -> 11.8 us
    all_gather x9 -> x0, blocking collectives: 602 us -> none  [the longest x1 71.6 us: shards(): lax.all_gather(norm_bias, ('dp', 'fsdp'), axis=2, tiled=True)]
    reduce_scatter x4 -> x0, waiting for transfers between devices: 562 us -> none  [the longest x1 212 us: shards(): lax.psum_scatter(stacked[6], ('dp', 'fsdp'), scatter_dimension=1, tiled=T...]
    unnamed x16 -> x0, waiting for transfers between devices: 499 us -> none
    pallas_call x0 -> x5, Pallas kernels: none -> 350 us  [the longest x1 94.7 us: gather_weights(): pl.pallas_call(functools.partial(weights_kernel, grid, (width, per_projec...]
    dot_general x38 -> x4, matrix products: 176 us -> 21.5 us  [dot_tn(): lax.dot_general(left, right, (((0,), (0,)), ((), ())), preferred_element_...]
    another operation x12 -> x6, local copies, waits for them, and re-layouts: 50.5 us -> 0.34 us  [the longest x3 0.23 us: per_device(): return vector.reshape(vector.shape[:-1] + (n, -1))]
    unnamed x1 -> x0, blocking collectives: 40.8 us -> none
    another operation x16 -> x10, other arithmetic: 35.9 us -> 7.33 us  [the longest x2 1.98 us: shards(): jnp.stack([down_sum, g_down])]
  transfers between devices with their start and end apart: 12 -> 0, of which waited for: 7 -> 0; matrix products, arithmetic and copies ran while one was open for 11% -> 0% of each run, Pallas kernels for 0% -> 0%
where the time goes in v2:
time: 404 us; the launch traced here: 399 us
  Pallas kernels  350 us (87%)
  matrix products  21.5 us (5%)
  local copies, waits for them, and re-layouts  14.4 us (4%)
  other arithmetic  11.8 us (3%)
    pallas_call x1, Pallas kernels, gather_weights(): pl.pallas_call(functools.partial(weights_kernel, grid, (width, per_projec...  94.7 us
    pallas_call x1, Pallas kernels, segment_forward(): pl.pallas_call(functools.partial(segment_forward_kernel, grid, tile, step...  93.1 us
    pallas_call x1, Pallas kernels, sum_to_owners(): pl.pallas_call(functools.partial(sum_kernel, grid, chunk_list, nparts), o...  86.5 us
    pallas_call x1, Pallas kernels, cross_block(): pl.pallas_call(functools.partial(cross_kernel, grid, sizes), in_specs=[vm...  38.4 us
    pallas_call x1, Pallas kernels, segment_backward(): pl.pallas_call(functools.partial(segment_backward_kernel, tile), grid=(ro...  37.1 us
    dot_general x4, matrix products, dot_tn(): lax.dot_general(left, right, (((0,), (0,)), ((), ())), preferred_element_...  21.5 us

profile of v2, /device:TPU:0, one launch (start us, length us, event | category | flops | bytes accessed | tf_op | source)
XLA Modules:
  0.0 398.9 jit_solution(14458180616441878172)
XLA Ops:
  0.6 1.9 copy.36.refs_0_
  2.5 1.8 copy.37.refs_1_
  4.3 1.9 copy.38.refs_2_
  6.2 1.4 copy.39.refs_10_
  7.6 94.7 %gather_weights.1 = (bf16[2,2,2,4,96,768]{5,4,3,2,1,0:T(8,128)(2,1)}, bf16[2,2,2,4,96,768]{5,4,3,2,1,0:T(8,128)(2,1)}, bf16[2,2,2,4,96,768]{5,4,3,2,1,0:T(8,128)...) custom-call(bf16[2,768,72]{2,1,0:T(8,128)(2,1)} %copy.36.refs_0_, ...), custom_call_target="tpu_custom_call" | custom-call | tf_op jit(solution)/shard_map/gather_weights/pallas_call | solution.py:507
  102.3 93.1 %segment_forward.1 = (bf16[1024,2304]{1,0:T(8,128)(2,1)}, bf16[1024,768]{1,0:T(8,128)(2,1)}, bf16[1024,768]{1,0:T(8,128)(2,1)}, bf16[1024,3072]{1,0:T(8,128)(2,1...) custom-call(bf16[1024,768]{1,0:T(8,128)(2,1)} %bitcast.59, ...), custom_call_target="tpu_custom_call" | custom-call | tf_op jit(solution)/shard_map/segment_forward/pallas_call | solution.py:779
  195.4 0.8 copy.40.refs_3_
  196.2 38.4 %cross_block.1 = (f32[768,72]{1,0:T(8,128)}, f32[768,24]{1,0:T(8,128)}, f32[768,96]{1,0:T(8,128)}, f32[96,768]{1,0:T(8,128)}, f32[96,768]{1,0:T(8,128)}, /*index...) custom-call(f32[256,768]{1,0:T(8,128)} %bitcast.65, ...), custom_call_target="tpu_custom_call" | custom-call | tf_op jit(solution)/shard_map/cross_block/pallas_call | solution.py:929
  234.6 37.1 %segment_backward.1 = (bf16[1024,2304]{1,0:T(8,128)(2,1)}, bf16[1024,768]{1,0:T(8,128)(2,1)}, f32[1024,768]{1,0:T(8,128)}, bf16[1024,768]{1,0:T(8,128)(2,1)}, f32[8,2304]{1,0:T(8,128)}, /*index=5*/f32[8,768]{1,0:T(8,128)}) custom-call(bf16[1024,2304]{1,0:T(8,128)(2,1)} %get-tuple-element.71.qkv, f32[1024,768]{1,0:T(8,128)} %get-tuple-element.72.d_first, ...), custom_call_target="tpu_custom_call" | custom-call | tf_op jit(solution)/shard_map/segment_backward/pallas_call | solution.py:980
  271.7 0.8 slice_reduce_fusion.4
  272.5 0.1 concatenate.22
  272.6 0.1 concatenate.23
  272.6 0.8 slice_reduce_fusion.2
  273.4 0.1 reshape_squeeze.12
  273.5 0.1 reshape.89
  273.7 0.1 reshape.90
  273.8 0.1 reshape_squeeze.14
  273.9 0.9 slice_reduce_fusion
  274.8 0.1 reshape_squeeze.13
  274.9 0.1 concatenate.25
  275.0 0.1 copy.47
  275.0 0.8 pad.4.clone
  275.8 3.4 convolution_convert_fusion.3
  279.2 4.2 %convolution_convert_fusion.2 = bf16[2304,768]{1,0:T(8,128)(2,1)S(1)} fusion(bf16[1024,2304]{1,0:T(8,128)(2,1)S(1)} %copy-done.11, bf16[1024,768]{1,0:T(8,128)(2,1)S(1)} %bitcast.60), kind=kOutput, calls=%fused_computation.2 | convolution fusion | flops 3625648128 | bytes 9830400 | tf_op jit(solution)/shard_map/dot_general | solution.py:224
  283.4 2.7 pad_maximum_fusion.refs_2_
  286.2 7.0 %convolution_convert_fusion = bf16[3072,768]{1,0:T(8,128)(2,1)} fusion(bf16[1024,3072]{1,0:T(8,128)(2,1)S(1)} %bitcast.76, bf16[1024,768]{1,0:T(8,128)(2,1)S(1)} %copy-done.13), kind=kOutput, calls=%fused_computation | convolution fusion | flops 4834197504 | bytes 12582912 | tf_op jit(solution)/shard_map/dot_general | solution.py:224
  293.2 6.9 %convolution_convert_fusion.1 = bf16[3072,768]{1,0:T(8,128)(2,1)} fusion(bf16[1024,3072]{1,0:T(8,128)(2,1)S(1)} %bitcast.74, bf16[1024,768]{1,0:T(8,128)(2,1)S(1)} %copy-done.12), kind=kOutput, calls=%fused_computation.1 | convolution fusion | flops 4834197504 | bytes 12582912 | tf_op jit(solution)/shard_map/dot_general | solution.py:224
  300.2 86.5 %sum_to_owners.1 = (f32[96,768]{1,0:T(8,128)}, f32[96,768]{1,0:T(8,128)}, f32[96,768]{1,0:T(8,128)}, f32[8,384]{1,0:T(8,128)}) custom-call(bf16[2,2,2,4,96,768]{5,4,3,2,1,0:T(8,128)(2,1)} %bitcast.55, bf16[2,2,2,4,96,768]{5,4,3,2,1,0:T(8,128)(2,1)} %bitcast.54, bf16[2,2,2,4,96,768]{5,4,3,2,1,0:T(8,128)(2,1)} %pad_maximum_fusion.refs_2_, ...), custom_call_target="tpu_custom_call" | custom-call | tf_op jit(solution)/shard_map/sum_to_owners/pallas_call | solution.py:1040
  386.7 0.0 copy-start.1
  386.8 0.9 slice_add_fusion.1
  387.6 0.1 reshape_squeeze.15
  387.7 0.7 slice_bitcast_fusion.2
  388.4 0.6 pad_maximum_fusion.6
  389.0 1.1 add_bitcast_fusion
  390.2 0.9 pad_maximum_fusion.2
  391.0 0.6 pad_maximum_fusion.9
  391.6 0.2 copy.45
  391.7 0.9 pad_maximum_fusion.1
  392.6 0.8 slice_add_fusion
  393.4 0.6 pad_maximum_fusion.8
  394.0 0.1 copy.44
  394.2 0.7 pad_maximum_fusion.4
  394.8 0.7 slice.76
  395.5 0.7 slice.77
  396.2 0.6 pad_maximum_fusion.7
  396.8 0.1 copy.43
  397.0 0.8 pad_maximum_fusion.3
  397.8 0.7 copy.46
  (45 shorter events, 0.2 us)
Async XLA Ops:
  102.3 93.1 %copy-start.10 = (s32[256]{0:T(256)S(1)}, s32[256]{0:T(256)}, u32[]{:S(2)}) copy-start(s32[256]{0:T(256)} %param.16) | copy-start | bytes 3076
  234.6 38.9 %copy-start.9 = (f32[8,768]{1,0:T(8,128)S(1)}, f32[8,768]{1,0:T(8,128)}, u32[]{:S(2)}) copy-start(f32[8,768]{1,0:T(8,128)} %get-tuple-element.96) | copy-start | bytes 73732
  234.6 41.2 %copy-start.14 = (bf16[1024,768]{1,0:T(8,128)(2,1)S(1)}, bf16[1024,768]{1,0:T(8,128)(2,1)}, u32[]{:S(2)}) copy-start(bf16[1024,768]{1,0:T(8,128)(2,1)} %get-tuple-element.92) | copy-start | bytes 4718596
  275.0 4.2 %copy-start.11 = (bf16[1024,2304]{1,0:T(8,128)(2,1)S(1)}, bf16[1024,2304]{1,0:T(8,128)(2,1)}, u32[]{:S(2)}) copy-start(bf16[1024,2304]{1,0:T(8,128)(2,1)} %get-tuple-element.90) | copy-start | bytes 14155780
  275.8 3.4 copy-start
  275.8 10.4 %slice-start.2 = ((s8[6291456]{0:T(1024)(128)(4,1)}), s8[4194304]{0:T(1024)(128)(4,1)S(1)}, s32[]{:S(2)}) async-start(s8[6291456]{0:T(1024)(128)(4,1)} %bitcast.75), calls=%async_computation.2 | async-start | bytes 8388608
  279.2 7.0 %slice-start.3 = ((s8[6291456]{0:T(1024)(128)(4,1)}), s8[2097152]{0:T(1024)(128)(4,1)S(1)}, s32[]{:S(2)}) async-start(s8[6291456]{0:T(1024)(128)(4,1)} %bitcast.75), calls=%async_computation.3 | async-start | bytes 4194304
  283.4 2.8 copy-start.13
  283.4 9.8 %slice-start = ((s8[6291456]{0:T(1024)(128)(4,1)}), s8[2097152]{0:T(1024)(128)(4,1)S(1)}, s32[]{:S(2)}) async-start(s8[6291456]{0:T(1024)(128)(4,1)} %bitcast.73), calls=%async_computation | async-start | bytes 4194304
  286.2 7.0 %slice-start.1 = ((s8[6291456]{0:T(1024)(128)(4,1)}), s8[4194304]{0:T(1024)(128)(4,1)S(1)}, s32[]{:S(2)}) async-start(s8[6291456]{0:T(1024)(128)(4,1)} %bitcast.73), calls=%async_computation.1 | async-start | bytes 8388608
  286.2 7.0 %copy-start.12 = (bf16[1024,768]{1,0:T(8,128)(2,1)S(1)}, bf16[1024,768]{1,0:T(8,128)(2,1)}, u32[]{:S(2)}) copy-start(bf16[1024,768]{1,0:T(8,128)(2,1)} %get-tuple-element.87) | copy-start | bytes 4718596
  300.2 88.9 %copy-start.4 = (f32[96,768]{1,0:T(8,128)S(1)}, f32[96,768]{1,0:T(8,128)}, u32[]{:S(2)}) copy-start(f32[96,768]{1,0:T(8,128)} %get-tuple-element.103) | copy-start | bytes 884740
  300.2 88.9 %copy-start.5 = (f32[96,768]{1,0:T(8,128)S(1)}, f32[96,768]{1,0:T(8,128)}, u32[]{:S(2)}) copy-start(f32[96,768]{1,0:T(8,128)} %get-tuple-element.106) | copy-start | bytes 884740
  300.2 90.0 %copy-start.7 = (f32[96,768]{1,0:T(8,128)S(1)}, f32[96,768]{1,0:T(8,128)}, u32[]{:S(2)}) copy-start(f32[96,768]{1,0:T(8,128)} %get-tuple-element.107) | copy-start | bytes 884740
  300.2 91.4 %copy-start.3 = (f32[768,96]{1,0:T(8,128)S(1)}, f32[768,96]{1,0:T(8,128)}, u32[]{:S(2)}) copy-start(f32[768,96]{1,0:T(8,128)} %get-tuple-element.104) | copy-start | bytes 884740
  386.7 7.3 %copy-start.6 = (f32[96,768]{1,0:T(8,128)S(1)}, f32[96,768]{1,0:T(8,128)}, u32[]{:S(2)}) copy-start(f32[96,768]{1,0:T(8,128)} %get-tuple-element.97) | copy-start | bytes 884740
  386.7 7.3 %copy-start.2 = (f32[768,24]{1,0:T(8,128)S(1)}, f32[768,24]{1,0:T(8,128)}, u32[]{:S(2)}) copy-start(f32[768,24]{1,0:T(8,128)} %get-tuple-element.101) | copy-start | bytes 221188
  386.7 10.0 %copy-start.1 = (f32[768,72]{1,0:T(8,128)S(1)}, f32[768,72]{1,0:T(8,128)}, u32[]{:S(2)}) copy-start(f32[768,72]{1,0:T(8,128)} %get-tuple-element.98) | copy-start | bytes 663556
  389.0 8.8 %copy-start.8 = (f32[64,24]{1,0:T(8,128)S(1)}, f32[64,24]{1,0:T(8,128)}, u32[]{:S(2)}) copy-start(f32[64,24]{1,0:T(8,128)} %get-tuple-element.134) | copy-start | bytes 18436

commit v3 on v2

--- a/solution.py
+++ b/solution.py
@@ -52,6 +52,9 @@
         return (dp, other[-1]), other[dim]
 
     def greet(self, coords):
+        self.meet(self.call(coords))
+
+    def call(self, coords):
         barrier = pltpu.get_barrier_semaphore()
         count = 0
         for dim, size in enumerate(self.dims):
@@ -59,7 +62,10 @@
                 where, unused = self.peer(coords, dim, step)
                 pl.semaphore_signal(barrier, inc=1, device_id=where, device_id_type=MESH)
                 count += 1
-        pl.semaphore_wait(barrier, count)
+        return count
+
+    def meet(self, count):
+        pl.semaphore_wait(pltpu.get_barrier_semaphore(), count)
 
     def sems(self, chunks):
         shape = (chunks, len(self.dims), self.most)
@@ -172,35 +178,18 @@
         held, lands, out, first, rows, colour = self.chunks[k]
         grid, coords = self.grid, self.coords
         order = grid.orders[colour][::-1]
-        free = [d for d in range(len(order)) if d in order[stage + 1 :]]
-        sizes = [grid.dims[d] for d in free]
+        land = lands[stage]
+        where = index_of(coords, order[stage + 1 :], len(order)) + (pl.ds(first, rows),)
+        total = held[where]
         final = stage == self.stages - 1
-        land = lands[stage]
-
-        def body(i, unused):
-            there = list(coords)
-            rest = i
-            inner = [None] * len(free)
-            for pos in range(len(free) - 1, -1, -1):
-                inner[pos] = rest % sizes[pos]
-                rest = rest // sizes[pos]
-                there[free[pos]] = inner[pos]
-            where = tuple(there) + (pl.ds(first, rows),)
-            total = held[where]
-            if final:
-                total = total.astype(jnp.float32)
-            for step in range(grid.dims[order[stage]] - 1):
-                total += land[(step,) + tuple(inner)].astype(total.dtype)
-            if final:
-                out[pl.ds(first, rows)] = total
-            else:
-                held[where] = total
-            return unused
-
-        if free:
-            lax.fori_loop(0, math.prod(sizes), body, 0)
+        if final:
+            total = total.astype(jnp.float32)
+        for step in range(grid.dims[order[stage]] - 1):
+            total += land[step].astype(total.dtype)
+        if final:
+            out[pl.ds(first, rows)] = total
         else:
-            body(0, 0)
+            held[where] = total
 
     def sent(self, k):
         for stage in range(self.stages):
@@ -338,13 +327,17 @@
 SMALL_ROWS = 16
 
 
+def misc_rows(per_output):
+    return SMALL_ROWS + -(-per_output // 16) * 16
+
+
 def weights_kernel(grid, sizes, *refs):
     width, per_project, per_output, per_up, per_pair, places_n = sizes
     n, ndims = grid.n, len(grid.dims)
     pw, ow, uw, dw, pb, ob, ub, db, ng, nb, pt, cot = refs[:12]
     mixed0, up0, down0, mixed1, up1, cot1, own_down1, vec, vec_pair, vec_up, table = refs[12:23]
-    own_mixed, own_up, own_down, own_misc, misc_f, misc_all, own_cot, cot_head = refs[23:31]
-    send_sem, recv_sem, local_sem = refs[31:]
+    own_mixed, own_misc, misc_f, misc_all, own_cot, cot_head = refs[23:29]
+    send_sem, recv_sem, local_sem = refs[29:]
     coords = grid.coords()
     me_line = coords[-1]
     cot_copy = pltpu.make_async_copy(cot.at[:, pl.ds(0, 8)], cot_head, local_sem.at[0])
@@ -359,13 +352,13 @@
         for b in range(2):
             misc_f[pl.ds(at, 2), pl.ds(0, per_output)] = ref[b].astype(jnp.float32)
             at += 2
-    misc_f[pl.ds(SMALL_ROWS, places_n), pl.ds(0, per_output)] = pt[...].astype(jnp.float32)
+    misc_f[pl.ds(SMALL_ROWS, per_output), pl.ds(0, places_n)] = pt[...].astype(jnp.float32)
     own_misc[...] = misc_f[...].astype(jnp.bfloat16)
 
     def pack(b):
         rows = per_project + per_output
         own_mixed[b] = (
-            dot_nt(place_rows(rows, per_project, 0), pw[b]) + dot_nt(place_rows(rows, per_output, per_project), ow[b])
+            dot_nn(place_rows(rows, per_project, 0), pw[b]) + dot_nn(place_rows(rows, per_output, per_project), ow[b])
         ).astype(jnp.bfloat16)
 
     def place_rows(rows, size, first):
@@ -385,13 +378,13 @@
 
     mixed_rows = per_project + per_output
     units += [add(own_mixed.at[0], None, mixed0, u) for u in pairs(mixed_rows)]
-    units[0] += add(own_misc, None, misc_all, [(0, SMALL_ROWS + places_n, 0)])
+    units[0] += add(own_misc, None, misc_all, [(0, misc_rows(per_output), 0)])
     up_units = len(units)
-    units += [add(own_up.at[0], None, up0, u) for u in pairs(per_up)]
+    units += [add(uw.at[0], None, up0, u) for u in pairs(per_up)]
     down_units = len(units)
-    units += [add(own_down.at[0], None, down0, u) for u in pairs(per_up)]
+    units += [add(dw.at[0], None, down0, u) for u in pairs(per_up)]
     line_units = [add(own_mixed.at[1], mixed1, None, [h]) for h in halves(mixed_rows, jnp.bfloat16)]
-    line_units += [add(own_up.at[1], up1, None, [h]) for h in halves(per_up, jnp.bfloat16)]
+    line_units += [add(uw.at[1], up1, None, [h]) for h in halves(per_up, jnp.bfloat16)]
     line_units[0] += add(own_cot, cot1, None, [(0, own_cot.shape[0], 0)])
     gather = Gather(grid, coords, chunks, send_sem, recv_sem)
 
@@ -400,21 +393,17 @@
             gather.start(k, stage)
 
     start(units[0], 0)
-    own_up[0] = dot_nt(place_rows(per_up, per_up, 0), uw[0]).astype(jnp.bfloat16)
-    own_down[0] = dw[0]
     pack(1)
-    own_up[1] = dot_nt(place_rows(per_up, per_up, 0), uw[1]).astype(jnp.bfloat16)
-    own_down[1] = dw[1]
     cot_copy.wait()
     for s in range(own_cot.shape[0]):
         own_cot[pl.ds(s, 1), :] = cot_head[s, 0:1, :]
     locals_ = [
         pltpu.make_async_copy(own_mixed.at[0], mixed0.at[coords], local_sem.at[0]),
-        pltpu.make_async_copy(own_up.at[0], up0.at[coords], local_sem.at[1]),
-        pltpu.make_async_copy(own_down.at[0], down0.at[coords], local_sem.at[2]),
+        pltpu.make_async_copy(uw.at[0], up0.at[coords], local_sem.at[1]),
+        pltpu.make_async_copy(dw.at[0], down0.at[coords], local_sem.at[2]),
         pltpu.make_async_copy(own_mixed.at[1], mixed1.at[me_line], local_sem.at[3]),
-        pltpu.make_async_copy(own_up.at[1], up1.at[me_line], local_sem.at[4]),
-        pltpu.make_async_copy(own_down.at[1], own_down1, local_sem.at[5]),
+        pltpu.make_async_copy(uw.at[1], up1.at[me_line], local_sem.at[4]),
+        pltpu.make_async_copy(dw.at[1], own_down1, local_sem.at[5]),
         pltpu.make_async_copy(own_cot, cot1.at[me_line], local_sem.at[6]),
     ]
     for copy in locals_:
@@ -438,20 +427,13 @@
             vec_pair[b, :, width : 2 * width] = jnp.zeros((1, width), jnp.float32)
             vec_pair[b, :, 2 * width : 3 * width] = pairs[b : b + 1, width:]
             vec_up[b] = ups[4 + b : 5 + b]
-        lead = grid.dims[0]
-        total = jnp.zeros((places_n, width), jnp.float32)
-        per = n // lead
-        lane = lax.broadcasted_iota(jnp.int32, (128, 1), 0)
-        column = lax.broadcasted_iota(jnp.int32, (1, width), 1)
-        ones = jnp.where(column % per_output == lane, 1.0, 0.0).astype(jnp.bfloat16)
-        owner = column // per_output
-        for i in range(lead):
-            rows = misc_all[i, ..., SMALL_ROWS : SMALL_ROWS + places_n, :].reshape(per * places_n, 128)
-            laid = dot_nn(rows, ones)
-            slot = lax.broadcasted_iota(jnp.int32, (per * places_n, 1), 0) // places_n + i * per
-            kept = jnp.where(slot == owner, laid, 0.0)
-            total += jnp.sum(kept.reshape(per, places_n, width), 0)
-        table[...] = total.astype(jnp.bfloat16)
+        for d in range(n):
+            where, rest = [], d
+            for extent in grid.dims[::-1]:
+                where.append(rest % extent)
+                rest //= extent
+            rows = misc_all[tuple(where[::-1]) + (pl.ds(SMALL_ROWS, misc_rows(per_output) - SMALL_ROWS),)].astype(jnp.float32)
+            table[pl.ds(d * per_output, per_output), :] = rows[:per_output]
 
     count = len(units)
     line_ticks = {count - 6: line_units[:1], count - 4: line_units[1:2], count - 1: line_units[2:]} if count >= 7 else {0: line_units}
@@ -488,15 +470,15 @@
 
 def gather_weights(grid, arrays, cid):
     project_weight, output_weight, up_weight, down_weight, project_bias = arrays[:5]
-    width = project_weight.shape[1]
-    per_project, per_output, per_up = project_weight.shape[2], output_weight.shape[2], up_weight.shape[2]
+    per_project, per_output, per_up = project_weight.shape[1], output_weight.shape[1], up_weight.shape[1]
+    width = project_weight.shape[2]
     per_pair = project_bias.shape[1]
-    places_n = arrays[10].shape[0]
+    places_n = arrays[10].shape[1]
     segs = arrays[11].shape[0]
     n = grid.n
     low, full = jnp.bfloat16, jnp.float32
     mixed_rows = per_project + per_output
-    misc_rows = SMALL_ROWS + places_n
+    small_rows = misc_rows(per_output)
     fs = grid.fsdp
     count = 2 + sum(len(u) for r in (mixed_rows, per_up, per_up) for u in pairs(r)) + sum(len(halves(r, low)) for r in (mixed_rows, per_up))
     vmem, anywhere = pl.BlockSpec(memory_space=pltpu.VMEM), pl.BlockSpec(memory_space=pl.ANY)
@@ -511,11 +493,11 @@
         out_shape=[
             shape((*grid.dims, mixed_rows, width), low), shape((*grid.dims, per_up, width), low), shape((*grid.dims, per_up, width), low),
             shape((fs, mixed_rows, width), low), shape((fs, per_up, width), low), shape((fs, segs, width), full), shape((per_up, width), low),
-            shape((2, 8, width), full), shape((2, 1, 3 * width), full), shape((2, 1, n * per_up), full), shape((places_n, width), low),
+            shape((2, 8, width), full), shape((2, 1, 3 * width), full), shape((2, 1, n * per_up), full), shape((width, 128), full),
         ],
         scratch_shapes=[
-            pltpu.VMEM((2, mixed_rows, width), low), pltpu.VMEM((2, per_up, width), low), pltpu.VMEM((2, per_up, width), low),
-            pltpu.VMEM((misc_rows, 128), low), pltpu.VMEM((misc_rows, 128), full), pltpu.VMEM((*grid.dims, misc_rows, 128), low),
+            pltpu.VMEM((2, mixed_rows, width), low),
+            pltpu.VMEM((small_rows, 128), low), pltpu.VMEM((small_rows, 128), full), pltpu.VMEM((*grid.dims, small_rows, 128), low),
             pltpu.VMEM((segs, width), full), pltpu.VMEM((segs, 8, width), full),
         ]
         + grid.sems(count)
@@ -606,11 +588,12 @@
 
 def segment_forward_kernel(grid, tile, steps, per_project, *refs):
     (tokens, grads, mixed0, up0, down0, vec, vec_pair, vec_up, line_mixed, line_up, line_cot, own_down) = refs[:12]
-    names = ("qkv", "mixed", "normed", "hidden", "d_down", "d_inner", "d_first", "seg_low", "norm_sums", "up_sums")
-    r = dict(zip(names, refs[12:22]))
-    project_out, output_out, all_first, mixed1, up1, down1, all_cot = refs[22:29]
-    r["slope"], held_mixed, project, output, up, down, own_first = refs[29:36]
-    send_sem, recv_sem, local_sem = refs[36:]
+    names = ("qkv", "mixed", "d_first", "seg_low", "norm_sums", "up_sums")
+    r = dict(zip(names, refs[12:18]))
+    project_out, output_out, all_first, mixed1, up1, down1, all_cot, partial_up, partial_down = refs[18:27]
+    r.update(zip(("slope", "normed", "hidden", "d_down", "d_inner"), refs[27:32]))
+    held_mixed, project, output, up, down, own_first, sum_up, sum_down = refs[32:40]
+    send_sem, recv_sem, local_sem = refs[40:]
     w = small_of(vec, vec_pair, vec_up, 0)
     w.update(project=project, output=output, up=up, down=down)
     width = tokens.shape[1]
@@ -641,26 +624,26 @@
     chunks.append((own_first, None, all_first, 0, own_first.shape[0], 0))
     gather = Gather(grid, coords, chunks, send_sem, recv_sem)
 
-    ticks = ndims - 1 + len(groups)
+    ticks = ndims + 1
 
     def go(tick):
         if tick == 1:
             for copy in lines:
                 copy.wait()
-        for g in range(len(groups) - 1, -1, -1):
-            stage = tick - g + 1
-            late = chunks[groups[g][0]][1] is None
-            for k in groups[g]:
-                if late and tick == 0:
-                    gather.start(k, 0)
-                if (late and stage == 1) or 1 < stage <= ndims:
+        for group in groups:
+            late = chunks[group[0]][1] is None
+            stage = tick if late else tick + 1
+            for k in group:
+                if stage > (0 if late else 1) and stage <= ndims:
                     gather.landed(k, stage - 1)
-                if 1 <= stage < ndims:
+                if stage < ndims:
                     gather.start(k, stage)
 
     plan = {}
     for tick in range(1, ticks - 1):
-        at = min(2 * steps - 1, round(2 * steps * (tick - 0.65) / (ticks - 3)) - 1)
+        at = round((2 * steps - 1) * tick / (ticks - 2))
+        if ndims == 4 and steps == 4:
+            at = (1, 5, 7)[tick - 1]
         plan.setdefault(at, []).append(tick)
 
     def at_point(which):
@@ -739,21 +722,30 @@
     def _():
         r["norm_sums"][...] = jnp.zeros_like(r["norm_sums"])
         r["up_sums"][...] = jnp.zeros_like(r["up_sums"])
+        sum_up[...] = jnp.zeros_like(sum_up)
+        sum_down[...] = jnp.zeros_like(sum_down)
 
     r["norm_sums"][...] += gathered
     r["up_sums"][...] += jnp.broadcast_to(sums[5], r["up_sums"].shape)
-
+    for left, right, total in (("hidden", "d_down", sum_down), ("d_inner", "normed", sum_up)):
+        for c in range(0, total.shape[0], width):
+            total[pl.ds(c, width), :] += dot_tn(r[left][:, pl.ds(c, width)], r[right][...])
     at_point(1)
 
     @pl.when(step == last)
     def _():
+        down[...] = sum_down[...].astype(jnp.bfloat16)
+        up[...] = sum_up[...].astype(jnp.bfloat16)
+        out = [pltpu.make_async_copy(*p, local_sem.at[i]) for i, p in enumerate(((down, partial_down), (up, partial_up)))]
+        for copy in out:
+            copy.start()
         go(ticks - 1)
         for g in range(len(groups)):
             for k in groups[g]:
                 gather.sent(k, 1 if chunks[k][1] is not None else 0, ndims)
         gather.landed(first_chunk, ndims - 1)
         gather.sent(first_chunk, 0, ndims)
-        for copy in stores:
+        for copy in stores + out:
             copy.wait()
 
 
@@ -781,24 +773,26 @@
         grid=(steps,),
         in_specs=[cut(width), cut(width)] + [anywhere] * 3 + [whole(s.shape) for s in (*smalls, *lines)],
         out_specs=[
-            cut(3 * width), cut(width), cut(width), cut(hidden_units), cut(width), cut(hidden_units), cut(width), cut(width),
+            cut(3 * width), cut(width), cut(width), cut(width),
             pl.BlockSpec((8, width), lambda i: (0, 0)), pl.BlockSpec((8, hidden_units), lambda i: (0, 0)),
         ]
-        + [anywhere] * 7,
+        + [anywhere] * 9,
         out_shape=[
-            shape(3 * width, low), shape(width, low), shape(width, low), shape(hidden_units, low), shape(width, low),
-            shape(hidden_units, low), shape(width, full), shape(width, low),
+            shape(3 * width, low), shape(width, low), shape(width, full), shape(width, low),
             jax.ShapeDtypeStruct((8, width), full), jax.ShapeDtypeStruct((8, hidden_units), full),
             jax.ShapeDtypeStruct((3 * width, width), low), jax.ShapeDtypeStruct((width, width), low),
             jax.ShapeDtypeStruct((*grid.dims, segs, width), full),
             jax.ShapeDtypeStruct((*grid.dims, mixed_rows, width), low),
             jax.ShapeDtypeStruct((*grid.dims, per_up, width), low), jax.ShapeDtypeStruct((*grid.dims, per_up, width), low),
             jax.ShapeDtypeStruct((*grid.dims, segs, width), full),
+            jax.ShapeDtypeStruct((hidden_units, width), low), jax.ShapeDtypeStruct((hidden_units, width), low),
         ],
         scratch_shapes=[
-            pltpu.VMEM((tile, hidden_units), low), pltpu.VMEM((*grid.dims, mixed_rows, width), low),
+            pltpu.VMEM((tile, hidden_units), low), pltpu.VMEM((tile, width), low), pltpu.VMEM((tile, hidden_units), low),
+            pltpu.VMEM((tile, width), low), pltpu.VMEM((tile, hidden_units), low), pltpu.VMEM((*grid.dims, mixed_rows, width), low),
             pltpu.VMEM((3 * width, width), low), pltpu.VMEM((width, width), low),
             pltpu.VMEM((hidden_units, width), low), pltpu.VMEM((hidden_units, width), low), pltpu.VMEM((segs, width), full),
+            pltpu.VMEM((hidden_units, width), full), pltpu.VMEM((hidden_units, width), full),
         ]
         + grid.sems(count)
         + [pltpu.SemaphoreType.DMA((10,))],
@@ -828,18 +822,23 @@
 
 def cross_kernel(grid, sizes, *refs):
     per_project, per_output, per_up, per_pair = sizes
-    (firsts, grads, placed_row, placed_col, mixed1, up1, down1, up0, down0, vec, vec_pair, vec_up, table) = refs[:13]
-    g_project, g_output, g_up, g_down, z_up, z_down, smalls, g_table, cross_own, d_first_own = refs[13:23]
+    (firsts, grads, placed_row, placed_col, mixed1, up1, down1, up0, down0, vec, vec_pair, vec_up, table, partial) = refs[:14]
+    g_project, g_output, g_up, g_down, z_up, down_sum, smalls, g_table, cross_own, d_first_own = refs[14:24]
     names = ("qkv", "slope", "d_mixed", "mixed", "normed", "hidden", "d_down", "d_inner", "d_qkv")
-    r = dict(zip(names, refs[23:32]))
-    held_mixed, project, output, up, down, z_up_w, z_down_w, z_slope, z_normed, z_hidden, z_d_down, z_d_inner, rows_f = refs[32:45]
-    local_sem = refs[45]
+    r = dict(zip(names, refs[24:33]))
+    held_mixed, project, output, up, down, z_up_w, z_down_w, z_slope, z_normed, z_hidden, z_d_down, z_d_inner, rows_f = refs[33:46]
+    held, *lands, send_sem, recv_sem, local_sem = refs[46:]
+    coords = grid.coords()
+    reduce, ticks = summing(grid, coords, held, lands, down_sum, send_sem, recv_sem)
+    load_partial = pltpu.make_async_copy(partial, held, local_sem.at[5])
+    load_partial.start()
     loads = [pltpu.make_async_copy(*p, local_sem.at[i]) for i, p in enumerate(
         ((up0, z_up_w), (down0, z_down_w), (mixed1, held_mixed), (up1, up), (down1, down)))]
     for copy in loads:
         copy.start()
+    expected = grid.call(coords)
     slots, width = firsts.shape
-    places_n = table.shape[0]
+    places_n = LONG_SEGS
     me = grid.flat()
     per_slots = slots // grid.n
 
@@ -850,6 +849,9 @@
     def hook0(name):
         if name == "down":
             loads[1].wait()
+            load_partial.wait()
+            grid.meet(expected)
+            reduce(0)
 
     loads[0].wait()
     kept0 = feed_forward(firsts[...], w0, r0, hook0)
@@ -858,7 +860,7 @@
     doc_col, place_col = document_of(placed_col[...], slots // 2)
     picker = place_col == lax.broadcasted_iota(jnp.int32, (slots, places_n), 1)
     picker_f = jnp.where(picker, 1.0, 0.0)
-    x = seg_first + dot_nn(picker_f.astype(jnp.bfloat16), table[...])
+    x = seg_first + dot_nt(picker_f.astype(jnp.bfloat16), table[:, 0:places_n].astype(jnp.bfloat16))
 
     w = small_of(vec, vec_pair, vec_up, 1)
     w.update(project=project, output=output, up=up, down=down)
@@ -867,10 +869,12 @@
     x_low = x.astype(jnp.bfloat16)
     allowed = doc_col == doc_row
     allowed = jnp.concatenate([allowed, allowed], 0)
+    reduce(1)
 
     def hook(name):
         if name == "first":
             loads[3].wait()
+            reduce(2)
         if name == "down":
             loads[4].wait()
 
@@ -878,15 +882,18 @@
     mine = pl.ds(pl.multiple_of(me * per_slots, per_slots), per_slots)
     rows_f[...] = kept[2] * w["gains"][1:2, :] + w["shifts"][1:2, :]
     cross_own[...] = rows_f[mine, :]
+    reduce(3)
     d_first, sums = mlp_back(grads[...], *kept, w, r)
+    reduce(4)
     branch = d_first.astype(jnp.bfloat16)
     r["d_mixed"][...] = dot_nn(branch, output[...]).astype(jnp.bfloat16)
     attend_back(r["qkv"], r["d_mixed"], r["d_qkv"], slots, slots, width, allowed)
     d_x = d_first + dot_nn(r["d_qkv"][...], project[...])
-
-    g_project[...] = dot_tn(x_low, own_columns(r["d_qkv"][...], me * per_project, per_project))
-    g_output[...] = dot_tn(r["mixed"][...], own_columns(branch, me * per_output, per_output))
-    g_up[...] = dot_tn(r["normed"][...], own_columns(r["d_inner"][...], me * per_up, per_up))
+    reduce(5)
+
+    g_project[...] = dot_tn(own_columns(r["d_qkv"][...], me * per_project, per_project), x_low)
+    g_output[...] = dot_tn(own_columns(branch, me * per_output, per_output), r["mixed"][...])
+    g_up[...] = dot_tn(own_columns(r["d_inner"][...], me * per_up, per_up), r["normed"][...])
     g_down[...] = dot_tn(own_columns(r["hidden"][...], me * per_up, per_up), r["d_down"][...])
     smalls[...] = jnp.zeros_like(smalls)
     norm_rows = jnp.concatenate(list(sums[:5]) + [row_sums(branch), jnp.zeros((2, width), jnp.float32)], 0)
@@ -896,7 +903,7 @@
     pair = jnp.concatenate([qkv_sums[:, :width], qkv_sums[:, 2 * width :]], 1)
     smalls[16:24, 0:per_pair] = own_sums(jnp.broadcast_to(pair, (8, 2 * width)), me * per_pair, per_pair)
     g_table[...] = lax.dot_general(
-        picker_f, own_sums(d_x, me * per_output, per_output), (((0,), (0,)), ((), ())),
+        own_sums(d_x, me * per_output, per_output), picker_f, (((0,), (0,)), ((), ())),
         precision=highest, preferred_element_type=jnp.float32,
     )
 
@@ -904,13 +911,50 @@
     rows_f[...] = d_first0
     d_first_own[...] = rows_f[mine, :]
     z_up[...] = dot_tn(own_columns(z_d_inner[...], me * per_up, per_up), z_normed[...])
-    z_down[...] = dot_tn(own_columns(z_hidden[...], me * per_up, per_up), z_d_down[...])
+    z_down = dot_tn(own_columns(z_hidden[...], me * per_up, per_up), z_d_down[...])
     norm_rows = jnp.concatenate(list(sums[:5]) + [jnp.zeros((3, width), jnp.float32)], 0)
     smalls[24:32, 0:per_output] = own_sums(norm_rows, me * per_output, per_output)
     smalls[32:40, 0:per_up] = own_sums(jnp.broadcast_to(sums[5], (8, sums[5].shape[1])), me * per_up, per_up)
-
-
-def cross_block(grid, firsts, grads, placement, mixed1, up1, down1, up0, down0, smalls, table, sizes):
+    for tick in range(6, ticks):
+        reduce(tick)
+    down_sum[...] += z_down
+    reduce(None)
+
+
+def summing(grid, coords, held, lands, out, send_sem, recv_sem):
+    ndims = len(grid.dims)
+    units = pairs(held.shape[-2])
+    cuts = [cut for unit in units for cut in unit]
+    chunks = [(held, lands[k * ndims : (k + 1) * ndims], out, *cut) for k, cut in enumerate(cuts)]
+    scatter = Scatter(grid, coords, chunks, send_sem, recv_sem)
+    per = len(units[0])
+
+    def reduce(tick):
+        if tick is None:
+            for k in range(len(chunks)):
+                scatter.sent(k)
+            return
+        for stage in range(ndims + 1):
+            u = tick - stage
+            if not 0 <= u < len(units):
+                continue
+            for k in range(u * per, (u + 1) * per):
+                if stage > 0:
+                    scatter.add(k, stage - 1)
+                if stage < ndims:
+                    scatter.start(k, stage)
+
+    return reduce, len(units) + ndims
+
+
+def summing_scratch(grid, rows, width):
+    low = jnp.bfloat16
+    cuts = [cut for unit in pairs(rows) for cut in unit]
+    lands = [land for cut in cuts for land in Scatter.landing(grid, cut[1], width, low, cut[2])]
+    return [pltpu.VMEM((*grid.dims, rows, width), low)] + lands + grid.sems(len(cuts))
+
+
+def cross_block(grid, firsts, grads, placement, mixed1, up1, down1, up0, down0, smalls, table, sizes, partial, cid):
     slots, width = firsts.shape
     per_project, per_output, per_up, per_pair = sizes
     hidden_units = per_up * grid.n
@@ -919,8 +963,8 @@
     flat = lambda ref: ref.reshape(hidden_units, width)
     vmem, anywhere = pl.BlockSpec(memory_space=pltpu.VMEM), pl.BlockSpec(memory_space=pl.ANY)
     outs = [
-        (width, per_project), (width, per_output), (width, per_up), (per_up, width), (per_up, width), (per_up, width),
-        (40, 128), (table.shape[0], per_output), (per_slots, width), (per_slots, width),
+        (per_project, width), (per_output, width), (per_up, width), (per_up, width), (per_up, width), (per_up, width),
+        (40, 128), (per_output, LONG_SEGS), (per_slots, width), (per_slots, width),
     ]
 
     def held(*shape, dtype=low):
@@ -928,7 +972,7 @@
 
     return pl.pallas_call(
         functools.partial(cross_kernel, grid, sizes),
-        in_specs=[vmem] * 4 + [anywhere] * 5 + [vmem] * 4,
+        in_specs=[vmem] * 4 + [anywhere] * 5 + [vmem] * 4 + [anywhere],
         out_specs=[vmem] * len(outs),
         out_shape=[jax.ShapeDtypeStruct(s, full) for s in outs],
         scratch_shapes=[
@@ -937,18 +981,49 @@
             held(*mixed1.shape), held(3 * width, width), held(width, width), held(hidden_units, width), held(hidden_units, width),
             held(hidden_units, width), held(hidden_units, width), held(slots, hidden_units), held(slots, width),
             held(slots, hidden_units), held(slots, width), held(slots, hidden_units), held(slots, width, dtype=full),
-            pltpu.SemaphoreType.DMA((5,)),
+            *summing_scratch(grid, per_up, width),
+            pltpu.SemaphoreType.DMA((6,)),
         ],
-        compiler_params=pltpu.CompilerParams(vmem_limit_bytes=62 * 2**20),
+        compiler_params=pltpu.CompilerParams(collective_id=cid, has_side_effects=True, vmem_limit_bytes=63 * 2**20),
         name="cross_block",
-    )(firsts, grads, placement[None, :], placement[:, None], mixed1, flat(up1), flat(down1), flat(up0), flat(down0), *smalls, table)
-
-
-def segment_backward_kernel(tile, qkv, d_first, cls_grad, seg_low, cls_out, project, output, d_qkv, d_branch, d_x, layer_out, sums_qkv, sums_out, d_mixed):
+    )(firsts, grads, placement[None, :], placement[:, None], mixed1, flat(up1), flat(down1), flat(up0), flat(down0), *smalls, table, partial)
+
+
+def segment_backward_kernel(grid, tile, steps, *refs):
+    qkv, d_first, cls_grad, seg_low, cls_out, project, output, partial, cls_part = refs[:9]
+    d_qkv, d_branch, d_x, layer_out, sums_qkv, sums_out, up_sum, d_mixed, held = refs[9:18]
+    *lands, send_sem, recv_sem, local_sem = refs[18:]
     width = d_first.shape[1]
+    step = pl.program_id(0)
+    coords = grid.coords()
+    reduce, ticks = summing(grid, coords, held, lands, up_sum, send_sem, recv_sem)
+    plan = {}
+    for tick in range(ticks - 1):
+        plan.setdefault(min(2 * steps - 1, tick + 1), []).append(tick)
+
+    def at_point(which):
+        for at, stages in plan.items():
+            if at % 2 == which:
+
+                @pl.when(step == at // 2)
+                def _(stages=stages):
+                    for stage in stages:
+                        if stage == 0:
+                            load.wait()
+                        reduce(stage)
+
+    load = pltpu.make_async_copy(partial, held, local_sem.at[0])
+
+    @pl.when(step == 0)
+    def _():
+        load.start()
+        grid.greet(coords)
+        sums_qkv[...] = jnp.zeros_like(sums_qkv)
+        sums_out[...] = jnp.zeros_like(sums_out)
+
+    at_point(0)
     place = lax.broadcasted_iota(jnp.int32, (tile, 1), 0)
     grad, out = d_first[...], seg_low[...].astype(jnp.float32)
-    step = pl.program_id(0)
     for s in range(tile // SEG_LEN):
         here = pl.ds(step * (tile // SEG_LEN) + s, 1)
         grad = jnp.where(place == s * SEG_LEN, cls_grad[here, :], grad)
@@ -958,44 +1033,51 @@
     d_branch[...] = branch
     d_mixed[...] = dot_nn(branch, output[...]).astype(jnp.bfloat16)
     attend_back(qkv, d_mixed, d_qkv, tile, SEG_LEN, width, None)
+    at_point(1)
     d_x[...] = grad + dot_nn(d_qkv[...], project[...])
-
-    @pl.when(step == 0)
-    def _():
-        sums_qkv[...] = jnp.zeros_like(sums_qkv)
-        sums_out[...] = jnp.zeros_like(sums_out)
-
     sums_qkv[...] += jnp.broadcast_to(row_sums(d_qkv[...]), sums_qkv.shape)
     sums_out[...] += jnp.broadcast_to(row_sums(branch), sums_out.shape)
 
-
-def segment_backward(qkv, d_first, cls_grad, seg_low, cls_out, project, output):
+    @pl.when(step == steps - 1)
+    def _():
+        reduce(ticks - 1)
+        up_sum[...] += cls_part[...]
+        reduce(None)
+
+
+def segment_backward(grid, qkv, d_first, cls_grad, seg_low, cls_out, project, output, partial, cls_part, cid):
     rows, width = d_first.shape
     tile = 2 * SEG_LEN
     low, full = jnp.bfloat16, jnp.float32
+    per_up = partial.shape[-2]
 
     def cut(columns):
         return pl.BlockSpec((tile, columns), lambda i: (i, 0))
 
     return pl.pallas_call(
-        functools.partial(segment_backward_kernel, tile),
+        functools.partial(segment_backward_kernel, grid, tile, rows // tile),
         grid=(rows // tile,),
         in_specs=[
             cut(3 * width), cut(width), whole(cls_grad.shape), cut(width), whole(cls_out.shape), whole(project.shape), whole(output.shape),
+            pl.BlockSpec(memory_space=pl.ANY), whole(cls_part.shape),
         ],
         out_specs=[
             cut(3 * width), cut(width), cut(width), cut(width),
             pl.BlockSpec((8, 3 * width), lambda i: (0, 0)), pl.BlockSpec((8, width), lambda i: (0, 0)),
+            pl.BlockSpec((per_up, width), lambda i: (0, 0)),
         ],
         out_shape=[
             jax.ShapeDtypeStruct((rows, 3 * width), low), jax.ShapeDtypeStruct((rows, width), low),
             jax.ShapeDtypeStruct((rows, width), full), jax.ShapeDtypeStruct((rows, width), low),
             jax.ShapeDtypeStruct((8, 3 * width), full), jax.ShapeDtypeStruct((8, width), full),
+            jax.ShapeDtypeStruct((per_up, width), full),
         ],
-        scratch_shapes=[pltpu.VMEM((tile, width), jnp.bfloat16)],
-        compiler_params=pltpu.CompilerParams(vmem_limit_bytes=60 * 2**20),
+        scratch_shapes=[
+            pltpu.VMEM((tile, width), jnp.bfloat16), *summing_scratch(grid, per_up, width), pltpu.SemaphoreType.DMA((1,)),
+        ],
+        compiler_params=pltpu.CompilerParams(collective_id=cid, has_side_effects=True, vmem_limit_bytes=60 * 2**20),
         name="segment_backward",
-    )(qkv, d_first, cls_grad, seg_low, cls_out, project, output)
+    )(qkv, d_first, cls_grad, seg_low, cls_out, project, output, partial, cls_part)
 
 
 def sum_kernel(grid, chunk_list, nparts, *refs):
@@ -1009,19 +1091,24 @@
     for load in loads:
         load.start()
     grid.greet(coords)
-    chunks, groups = [], {}
-    for k, (a, first, count, colour) in enumerate(chunk_list):
-        groups.setdefault(a, []).append(k)
-        chunks.append((held[a], lands[k * ndims : (k + 1) * ndims], outs[a], first, count, colour))
+    chunks = [
+        (held[a], lands[k * ndims : (k + 1) * ndims], outs[a], first, count, colour)
+        for k, (a, first, count, colour, unit) in enumerate(chunk_list)
+    ]
     scatter = Scatter(grid, coords, chunks, send_sem, recv_sem)
-    for tick in range(nparts + ndims):
-        for a in range(nparts):
-            stage = tick - a
-            if not 0 <= stage <= ndims:
+    loaded = set()
+    units = sorted({c[4] for c in chunk_list})
+    for tick in range(len(units) + ndims):
+        for stage in range(ndims + 1):
+            u = tick - stage
+            if not 0 <= u < len(units):
                 continue
-            if stage == 0:
-                loads[a].wait()
-            for k in groups[a]:
+            for k, (a, first, count, colour, unit) in enumerate(chunk_list):
+                if unit != units[u]:
+                    continue
+                if a not in loaded:
+                    loaded.add(a)
+                    loads[a].wait()
                 if stage >= 1:
                     scatter.add(k, stage - 1)
                 if stage < ndims:
@@ -1031,11 +1118,14 @@
 
 
 def sum_to_owners(grid, parts, cid):
-    chunk_list = [(a, *h) for a, p in enumerate(parts) for h in halves(p.shape[1], p.dtype)]
+    chunk_list = []
+    for a, p in enumerate(parts):
+        for unit, cuts in enumerate(pairs(p.shape[1]) if p.dtype == jnp.bfloat16 else [halves(p.shape[1], p.dtype)]):
+            chunk_list += [(a, *cut, unit) for cut in cuts]
     nparts = len(parts)
     shaped = [p.reshape(tuple(grid.dims) + p.shape[1:]) for p in parts]
     lands = []
-    for a, first, count, colour in chunk_list:
+    for a, first, count, colour, unit in chunk_list:
         lands += Scatter.landing(grid, count, parts[a].shape[2], parts[a].dtype, colour)
     return pl.pallas_call(
         functools.partial(sum_kernel, grid, chunk_list, nparts),
@@ -1072,7 +1162,7 @@
         self.value = self.value.at[self.plain(where)].set(value)
 
 
-def cross_plain(grid, firsts, grads, placement, mixed1, up1, down1, up0, down0, smalls, table, sizes):
+def cross_plain(grid, firsts, grads, placement, mixed1, up1, down1, up0, down0, smalls, table, sizes, partial, cid):
     slots, width = firsts.shape
     per_project, per_output, per_up, per_pair = sizes
     hidden_units = per_up * grid.n
@@ -1105,8 +1195,8 @@
     kept0 = feed_forward(firsts, w0, r0)
     seg_first = kept0[2] * w0["gains"][1:2, :] + w0["shifts"][1:2, :]
     doc, place = document_of(placement, slots // 2)
-    picker = jnp.where(place[:, None] == jnp.arange(table.shape[0], dtype=jnp.int32)[None, :], 1.0, 0.0)
-    x = seg_first + dot_nn(picker.astype(jnp.bfloat16), table)
+    picker = jnp.where(place[:, None] == jnp.arange(LONG_SEGS, dtype=jnp.int32)[None, :], 1.0, 0.0)
+    x = seg_first + dot_nt(picker.astype(jnp.bfloat16), table[:, :LONG_SEGS].astype(jnp.bfloat16))
     x_low = x.astype(jnp.bfloat16)
     allowed = doc[:, None] == doc[None, :]
     allowed = jnp.concatenate([allowed, allowed], 0)
@@ -1132,12 +1222,12 @@
         ],
         0,
     )
-    g_table = lax.dot_general(picker, cut(d_x, per_output), (((0,), (0,)), ((), ())), precision=highest)
+    g_table = lax.dot_general(cut(d_x, per_output), picker, (((0,), (0,)), ((), ())), precision=highest)
     per_slots = slots // grid.n
     return (
-        dot_tn(x_low, cut(r["d_qkv"][...], per_project)), dot_tn(r["mixed"][...], cut(branch, per_output)),
-        dot_tn(r["normed"][...], cut(r["d_inner"][...], per_up)), dot_tn(cut(r["hidden"][...], per_up), r["d_down"][...]),
-        dot_tn(cut(r0["d_inner"][...], per_up), r0["normed"][...]), dot_tn(cut(r0["hidden"][...], per_up), r0["d_down"][...]),
+        dot_tn(cut(r["d_qkv"][...], per_project), x_low), dot_tn(cut(branch, per_output), r["mixed"][...]),
+        dot_tn(cut(r["d_inner"][...], per_up), r["normed"][...]), dot_tn(cut(r["hidden"][...], per_up), r["d_down"][...]),
+        dot_tn(cut(r0["d_inner"][...], per_up), r0["normed"][...]), dot_tn(cut(r0["hidden"][...], per_up), r0["d_down"][...]) + sum_to_owners(grid, [partial.reshape(grid.n, per_up, width)], cid)[0],
         own_small, g_table, cut(out, per_slots, 0), cut(d_first0, per_slots, 0),
     )
 
@@ -1169,25 +1259,26 @@
 
     mixed0, up0, down0, *lines, vec, vec_pair, vec_up, table = gather_weights(
         grid,
-        [project_weight, output_weight, up_weight, down_weight, project_bias, output_bias, up_bias, down_bias,
-         norm_gain, norm_bias, position_table, cotangent],
+        [*(jnp.swapaxes(w, 1, 2) for w in (project_weight, output_weight, up_weight)), down_weight,
+         project_bias, output_bias, up_bias, down_bias, norm_gain, norm_bias, position_table.T, cotangent],
         0,
     )
     smalls = [vec, vec_pair, vec_up]
-    (qkv, mixed, normed, hidden, d_down, d_inner, d_first, seg_low, norm_sums, up_sums, project, output, all_first,
-     mixed1, up1, down1, all_cot) = segment_forward(
+    (qkv, mixed, d_first, seg_low, norm_sums, up_sums, project, output, all_first,
+     mixed1, up1, down1, all_cot, partial_up, partial_down) = segment_forward(
         grid, low_tokens, cotangent.reshape(rows, width), mixed0, up0, down0, smalls, lines, per_project, 1
     )
-    g_project, g_output, g_up, g_down, z_up, z_down, own_small, g_table, cross_own, cls_grad = (cross_block if slots <= 256 else cross_plain)(
+    partial_up, partial_down = [p.reshape(*grid.dims, per_up, width) for p in (partial_up, partial_down)]
+    g_project, g_output, g_up, g_down, z_up, down_sum, own_small, g_table, cross_own, cls_grad = (cross_block if slots <= 256 else cross_plain)(
         grid, all_first.reshape(slots, width), all_cot.reshape(slots, width), placement, mixed1, up1, down1, up0, down0,
-        smalls, table, sizes,
+        smalls, table, sizes, partial_down, 2,
     )
-    d_qkv, d_branch, d_x, layer_out, sums_qkv, sums_out = segment_backward(
-        qkv, d_first, cls_grad, seg_low, cross_own, project, output
+    d_qkv, d_branch, d_x, layer_out, sums_qkv, sums_out, up_sum = segment_backward(
+        grid, qkv, d_first, cls_grad, seg_low, cross_own, project, output, partial_up, z_up, 3
     )
-    grad_project, grad_output, grad_up, grad_down = [
+    grad_project, grad_output = [
         dot_tn(left, right).astype(jnp.bfloat16).reshape(n, -1, width)
-        for left, right in ((d_qkv, low_tokens), (d_branch, mixed), (d_inner, normed), (hidden, d_down))
+        for left, right in ((d_qkv, low_tokens), (d_branch, mixed))
     ]
 
     def per_device(vector):
@@ -1204,11 +1295,7 @@
     small_size = seg_small.shape[1]
     small_width = -(-small_size // 128) * 128
     seg_small = jnp.pad(seg_small[:, None], ((0, 0), (0, 7), (0, small_width - small_size)))
-    down_sum, up_sum, mixed_sum, small_sum = sum_to_owners(
-        grid, [grad_down, grad_up, jnp.concatenate([grad_project, grad_output], 1), seg_small], 2
-    )
-    down_sum += z_down
-    up_sum += z_up
+    mixed_sum, small_sum = sum_to_owners(grid, [jnp.concatenate([grad_project, grad_output], 1), seg_small], 4)
     cuts, at = [], 0
     for size in (per_pair, per_output, per_up, per_output, 4 * per_output):
         cuts.append(small_sum[0, at : at + size])
@@ -1221,17 +1308,17 @@
     return (
         layer_out.reshape(tokens.shape),
         d_x.reshape(tokens.shape),
-        jnp.stack([mixed_sum[:per_project].T, g_project]),
+        jnp.swapaxes(jnp.stack([mixed_sum[:per_project], g_project]), 1, 2),
         pair_g,
-        jnp.stack([mixed_sum[per_project:].T, g_output]),
+        jnp.swapaxes(jnp.stack([mixed_sum[per_project:], g_output]), 1, 2),
         out_g,
-        jnp.stack([up_sum.T, g_up]),
+        jnp.swapaxes(jnp.stack([up_sum, g_up]), 1, 2),
         up_g,
         jnp.stack([down_sum, g_down]),
         down_g,
         norm_g[:, :2],
         norm_g[:, 2:],
-        g_table,
+        g_table.T,
     )
 
 

time: 404 us -> 366 us (0.906)
  Pallas kernels: 350 us -> 331 us
  matrix products: 21.5 us -> 7.17 us
    pallas_call x1, Pallas kernels: 86.5 us -> 34 us  [sum_to_owners(): pl.pallas_call(functools.partial(sum_kernel, grid, chunk_list, nparts), o...]
    pallas_call x1, Pallas kernels: 37.1 us -> 56 us  [segment_backward(): pl.pallas_call(functools.partial(segment_backward_kernel, grid, tile, row...]
    pallas_call x1, Pallas kernels: 38.4 us -> 53.4 us  [cross_block(): pl.pallas_call(functools.partial(cross_kernel, grid, sizes), in_specs=[vm...]
    dot_general x4 -> x2, matrix products: 21.5 us -> 7.17 us  [dot_tn(): lax.dot_general(left, right, (((0,), (0,)), ((), ())), preferred_element_...]
    pallas_call x1, Pallas kernels: 93.1 us -> 99.5 us  [segment_forward(): pl.pallas_call(functools.partial(segment_forward_kernel, grid, tile, step...]
    pallas_call x1, Pallas kernels: 94.7 us -> 88.4 us  [gather_weights(): pl.pallas_call(functools.partial(weights_kernel, grid, (width, per_projec...]
where the time goes in v3:
time: 366 us; the launch traced here: 361 us
  Pallas kernels  331 us (90%)
  local copies, waits for them, and re-layouts  11.1 us (3%)
  other arithmetic  10.5 us (3%)
  matrix products  7.17 us (2%)
    pallas_call x1, Pallas kernels, segment_forward(): pl.pallas_call(functools.partial(segment_forward_kernel, grid, tile, step...  99.5 us
    pallas_call x1, Pallas kernels, gather_weights(): pl.pallas_call(functools.partial(weights_kernel, grid, (width, per_projec...  88.4 us
    pallas_call x1, Pallas kernels, segment_backward(): pl.pallas_call(functools.partial(segment_backward_kernel, grid, tile, row...  56 us
    pallas_call x1, Pallas kernels, cross_block(): pl.pallas_call(functools.partial(cross_kernel, grid, sizes), in_specs=[vm...  53.4 us
    pallas_call x1, Pallas kernels, sum_to_owners(): pl.pallas_call(functools.partial(sum_kernel, grid, chunk_list, nparts), o...  34 us

profile of v3, /device:TPU:0, one launch (start us, length us, event | category | flops | bytes accessed | tf_op | source)
XLA Modules:
  0.0 361.5 jit_solution(9221440983965364888)
XLA Ops:
  0.6 88.4 %gather_weights.1 = (bf16[2,2,2,4,96,768]{5,4,3,2,1,0:T(8,128)(2,1)}, bf16[2,2,2,4,96,768]{5,4,3,2,1,0:T(8,128)(2,1)}, bf16[2,2,2,4,96,768]{5,4,3,2,1,0:T(8,128)...) custom-call(bf16[2,72,768]{2,1,0:T(8,128)(2,1)} %bitcast.73, ...), custom_call_target="tpu_custom_call" | custom-call | tf_op jit(solution)/shard_map/gather_weights/pallas_call | solution.py:489
  89.0 0.0 copy-start.11
  89.0 99.5 %segment_forward.1 = (bf16[1024,2304]{1,0:T(8,128)(2,1)}, bf16[1024,768]{1,0:T(8,128)(2,1)}, f32[1024,768]{1,0:T(8,128)}, bf16[1024,768]{1,0:T(8,128)(2,1)}, f32...) custom-call(bf16[1024,768]{1,0:T(8,128)(2,1)} %bitcast.59, ...), custom_call_target="tpu_custom_call" | custom-call | tf_op jit(solution)/shard_map/segment_forward/pallas_call | solution.py:771
  188.6 0.8 copy.28.refs_3_
  189.4 53.4 %cross_block.1 = (f32[72,768]{1,0:T(8,128)}, f32[24,768]{1,0:T(8,128)}, f32[96,768]{1,0:T(8,128)}, f32[96,768]{1,0:T(8,128)}, f32[96,768]{1,0:T(8,128)}, /*index...) custom-call(f32[256,768]{1,0:T(8,128)} %bitcast.64, ...), custom_call_target="tpu_custom_call" | custom-call | tf_op jit(solution)/shard_map/cross_block/pallas_call | solution.py:973
  242.8 0.0 copy-start.10
  242.8 0.0 copy-start.13
  242.9 56.0 %segment_backward.1 = (bf16[1024,2304]{1,0:T(8,128)(2,1)}, bf16[1024,768]{1,0:T(8,128)(2,1)}, f32[1024,768]{1,0:T(8,128)}, bf16[1024,768]{1,0:T(8,128)(2,1)}, f3...) custom-call(bf16[1024,2304]{1,0:T(8,128)(2,1)} %get-tuple-element.68.refs_0_, ...), custom_call_target="tpu_custom_call" | custom-call | tf_op jit(solution)/shard_map/segment_backward/pallas_call | solution.py:1057
  298.9 0.8 slice_reduce_fusion.4
  299.7 0.1 concatenate.22
  299.8 0.1 concatenate.23
  299.9 0.1 reshape_squeeze.12
  300.0 0.1 reshape.97
  300.1 0.1 reshape.98
  300.2 0.1 reshape_squeeze.14
  300.3 0.9 slice_reduce_fusion
  301.3 0.1 reshape_squeeze.13
  301.3 0.1 concatenate.25
  301.4 0.1 copy.31
  301.5 0.8 pad.4.clone
  302.3 3.0 convolution_convert_fusion.1
  305.3 0.0 copy-done.1
  305.3 0.3 copy-done.12
  305.6 4.2 %convolution_convert_fusion = bf16[2304,768]{1,0:T(8,128)(2,1)S(1)} fusion(bf16[1024,2304]{1,0:T(8,128)(2,1)S(1)} %copy-done.12, bf16[1024,768]{1,0:T(8,128)(2,1)S(1)} %bitcast.60), kind=kOutput, calls=%fused_computation | convolution fusion | flops 3625648128 | bytes 9830400 | tf_op jit(solution)/shard_map/dot_general | solution.py:213
  309.7 2.7 pad_maximum_fusion.refs_0_
  312.5 34.0 %sum_to_owners.1 = (f32[96,768]{1,0:T(8,128)}, f32[8,384]{1,0:T(8,128)}) custom-call(bf16[2,2,2,4,96,768]{5,4,3,2,1,0:T(8,128)(2,1)} %pad_maximum_fusion.refs_0_, f32[2,2,2,4,8,384]{5,4,3,2,1,0:T(8,128)} %bitcast.62), custom_call_target="tpu_custom_call" | custom-call | tf_op jit(solution)/shard_map/sum_to_owners/pallas_call | solution.py:1130
  346.5 0.9 slice_add_fusion.1
  347.4 0.1 reshape_squeeze.15
  347.4 0.7 slice_bitcast_fusion.2
  348.1 0.6 pad_maximum_fusion.3
  348.7 0.8 slice_add_fusion
  349.5 0.6 pad_maximum_fusion.7
  350.1 0.6 pad_maximum_fusion.6
  350.7 0.0 copy-done.6
  350.7 0.0 copy-start
  350.7 1.1 maximum_bitcast_fusion
  351.8 0.6 pad_maximum_fusion.5
  352.4 0.9 slice_bitcast_fusion.1
  353.3 0.7 maximum_bitcast_fusion.2
  353.9 0.7 slice.76
  354.6 0.7 slice.77
  355.3 0.6 pad_maximum_fusion.4
  355.9 0.9 slice_bitcast_fusion
  356.8 0.0 copy-done.7
  356.8 0.8 maximum_bitcast_fusion.1
  357.6 1.1 copy.35
  358.8 1.7 copy.36
  360.4 0.6 copy.37
  (24 shorter events, 0.1 us)
Async XLA Ops:
  89.0 99.6 %copy-start.11 = (s32[256]{0:T(256)S(1)}, s32[256]{0:T(256)}, u32[]{:S(2)}) copy-start(s32[256]{0:T(256)} %param.16) | copy-start | bytes 3076
  242.8 57.1 %copy-start.10 = (f32[8,768]{1,0:T(8,128)S(1)}, f32[8,768]{1,0:T(8,128)}, u32[]{:S(2)}) copy-start(f32[8,768]{1,0:T(8,128)} %get-tuple-element.92) | copy-start | bytes 73732
  242.8 59.4 %copy-start.13 = (bf16[1024,768]{1,0:T(8,128)(2,1)S(1)}, bf16[1024,768]{1,0:T(8,128)(2,1)}, u32[]{:S(2)}) copy-start(bf16[1024,768]{1,0:T(8,128)(2,1)} %get-tuple-element.88) | copy-start | bytes 4718596
  302.3 3.0 copy-start.1
  302.3 3.3 copy-start.12
  312.5 38.2 %copy-start.3 = (f32[96,768]{1,0:T(8,128)S(1)}, f32[96,768]{1,0:T(8,128)}, u32[]{:S(2)}) copy-start(f32[96,768]{1,0:T(8,128)} %get-tuple-element.99) | copy-start | bytes 884740
  312.5 38.2 %copy-start.4 = (f32[96,768]{1,0:T(8,128)S(1)}, f32[96,768]{1,0:T(8,128)}, u32[]{:S(2)}) copy-start(f32[96,768]{1,0:T(8,128)} %get-tuple-element.101) | copy-start | bytes 884740
  312.5 38.2 %copy-start.5 = (f32[96,768]{1,0:T(8,128)S(1)}, f32[96,768]{1,0:T(8,128)}, u32[]{:S(2)}) copy-start(f32[96,768]{1,0:T(8,128)} %get-tuple-element.100) | copy-start | bytes 884740
  312.5 38.2 %copy-start.6 = (f32[96,768]{1,0:T(8,128)S(1)}, f32[96,768]{1,0:T(8,128)}, u32[]{:S(2)}) copy-start(f32[96,768]{1,0:T(8,128)} %get-tuple-element.98) | copy-start | bytes 884740
  312.5 40.8 %copy-start.8 = (f32[24,768]{1,0:T(8,128)S(1)}, f32[24,768]{1,0:T(8,128)}, u32[]{:S(2)}) copy-start(f32[24,768]{1,0:T(8,128)} %get-tuple-element.97) | copy-start | bytes 221188
  312.5 44.4 %copy-start.7 = (f32[72,768]{1,0:T(8,128)S(1)}, f32[72,768]{1,0:T(8,128)}, u32[]{:S(2)}) copy-start(f32[72,768]{1,0:T(8,128)} %get-tuple-element.94) | copy-start | bytes 663556
  312.5 45.1 %copy-start.2 = (bf16[1024,768]{1,0:T(8,128)(2,1)S(1)}, bf16[1024,768]{1,0:T(8,128)(2,1)}, u32[]{:S(2)}) copy-start(bf16[1024,768]{1,0:T(8,128)(2,1)} %get-tuple-element.84) | copy-start | bytes 4718596
  350.7 8.1 %copy-start = (f32[1024,768]{1,0:T(8,128)S(1)}, f32[1024,768]{1,0:T(8,128)}, u32[]{:S(2)}) copy-start(f32[1024,768]{1,0:T(8,128)} %get-tuple-element.85) | copy-start | bytes 9437188
  358.8 1.7 copy-start.9

commit v4 on v3

--- a/solution.py
+++ b/solution.py
@@ -655,7 +655,7 @@
                     for tick in some:
                         go(tick)
 
-    first_points = ["first", "down", "back", "up"]
+    first_points = ["first", "back", "tail", "end"]
     first_events = [[] for unused in first_points]
     stages = list(range(ndims))
     for i, stage in enumerate(stages):
@@ -696,10 +696,6 @@
                     copy.wait()
 
             at_point(0)
-        if name == "down":
-            first_point("down")
-        if name == "up":
-            first_point("up")
 
     def take_first(first):
         for s in range(tile // SEG_LEN):
@@ -727,9 +723,11 @@
 
     r["norm_sums"][...] += gathered
     r["up_sums"][...] += jnp.broadcast_to(sums[5], r["up_sums"].shape)
+    first_point("tail")
     for left, right, total in (("hidden", "d_down", sum_down), ("d_inner", "normed", sum_up)):
         for c in range(0, total.shape[0], width):
             total[pl.ds(c, width), :] += dot_tn(r[left][:, pl.ds(c, width)], r[right][...])
+    first_point("end")
     at_point(1)
 
     @pl.when(step == last)
@@ -874,7 +872,6 @@
     def hook(name):
         if name == "first":
             loads[3].wait()
-            reduce(2)
         if name == "down":
             loads[4].wait()
 
@@ -882,14 +879,13 @@
     mine = pl.ds(pl.multiple_of(me * per_slots, per_slots), per_slots)
     rows_f[...] = kept[2] * w["gains"][1:2, :] + w["shifts"][1:2, :]
     cross_own[...] = rows_f[mine, :]
-    reduce(3)
     d_first, sums = mlp_back(grads[...], *kept, w, r)
-    reduce(4)
+    reduce(2)
     branch = d_first.astype(jnp.bfloat16)
     r["d_mixed"][...] = dot_nn(branch, output[...]).astype(jnp.bfloat16)
     attend_back(r["qkv"], r["d_mixed"], r["d_qkv"], slots, slots, width, allowed)
     d_x = d_first + dot_nn(r["d_qkv"][...], project[...])
-    reduce(5)
+    reduce(3)
 
     g_project[...] = dot_tn(own_columns(r["d_qkv"][...], me * per_project, per_project), x_low)
     g_output[...] = dot_tn(own_columns(branch, me * per_output, per_output), r["mixed"][...])
@@ -898,10 +894,11 @@
     smalls[...] = jnp.zeros_like(smalls)
     norm_rows = jnp.concatenate(list(sums[:5]) + [row_sums(branch), jnp.zeros((2, width), jnp.float32)], 0)
     smalls[0:8, 0:per_output] = own_sums(norm_rows, me * per_output, per_output)
-    smalls[8:16, 0:per_up] = own_sums(jnp.broadcast_to(sums[5], (8, sums[5].shape[1])), me * per_up, per_up)
+    up_rows = jnp.broadcast_to(sums[5], (8, sums[5].shape[1]))
+    smalls[6:7, 0:per_up] = own_sums(up_rows, me * per_up, per_up)[0:1]
     qkv_sums = row_sums(r["d_qkv"][...])
     pair = jnp.concatenate([qkv_sums[:, :width], qkv_sums[:, 2 * width :]], 1)
-    smalls[16:24, 0:per_pair] = own_sums(jnp.broadcast_to(pair, (8, 2 * width)), me * per_pair, per_pair)
+    smalls[7:8, 0:per_pair] = own_sums(jnp.broadcast_to(pair, (8, 2 * width)), me * per_pair, per_pair)[0:1]
     g_table[...] = lax.dot_general(
         own_sums(d_x, me * per_output, per_output), picker_f, (((0,), (0,)), ((), ())),
         precision=highest, preferred_element_type=jnp.float32,
@@ -913,9 +910,10 @@
     z_up[...] = dot_tn(own_columns(z_d_inner[...], me * per_up, per_up), z_normed[...])
     z_down = dot_tn(own_columns(z_hidden[...], me * per_up, per_up), z_d_down[...])
     norm_rows = jnp.concatenate(list(sums[:5]) + [jnp.zeros((3, width), jnp.float32)], 0)
-    smalls[24:32, 0:per_output] = own_sums(norm_rows, me * per_output, per_output)
-    smalls[32:40, 0:per_up] = own_sums(jnp.broadcast_to(sums[5], (8, sums[5].shape[1])), me * per_up, per_up)
-    for tick in range(6, ticks):
+    smalls[8:16, 0:per_output] = own_sums(norm_rows, me * per_output, per_output)
+    up_rows = jnp.broadcast_to(sums[5], (8, sums[5].shape[1]))
+    smalls[14:15, 0:per_up] = own_sums(up_rows, me * per_up, per_up)[0:1]
+    for tick in range(4, ticks):
         reduce(tick)
     down_sum[...] += z_down
     reduce(None)
@@ -923,7 +921,7 @@
 
 def summing(grid, coords, held, lands, out, send_sem, recv_sem):
     ndims = len(grid.dims)
-    units = pairs(held.shape[-2])
+    units = [halves(held.shape[-2], held.dtype)]
     cuts = [cut for unit in units for cut in unit]
     chunks = [(held, lands[k * ndims : (k + 1) * ndims], out, *cut) for k, cut in enumerate(cuts)]
     scatter = Scatter(grid, coords, chunks, send_sem, recv_sem)
@@ -949,7 +947,7 @@
 
 def summing_scratch(grid, rows, width):
     low = jnp.bfloat16
-    cuts = [cut for unit in pairs(rows) for cut in unit]
+    cuts = halves(rows, low)
     lands = [land for cut in cuts for land in Scatter.landing(grid, cut[1], width, low, cut[2])]
     return [pltpu.VMEM((*grid.dims, rows, width), low)] + lands + grid.sems(len(cuts))
 
@@ -964,7 +962,7 @@
     vmem, anywhere = pl.BlockSpec(memory_space=pltpu.VMEM), pl.BlockSpec(memory_space=pl.ANY)
     outs = [
         (per_project, width), (per_output, width), (per_up, width), (per_up, width), (per_up, width), (per_up, width),
-        (40, 128), (per_output, LONG_SEGS), (per_slots, width), (per_slots, width),
+        (16, 128), (per_output, LONG_SEGS), (per_slots, width), (per_slots, width),
     ]
 
     def held(*shape, dtype=low):
@@ -989,37 +987,39 @@
     )(firsts, grads, placement[None, :], placement[:, None], mixed1, flat(up1), flat(down1), flat(up0), flat(down0), *smalls, table, partial)
 
 
-def segment_backward_kernel(grid, tile, steps, *refs):
-    qkv, d_first, cls_grad, seg_low, cls_out, project, output, partial, cls_part = refs[:9]
-    d_qkv, d_branch, d_x, layer_out, sums_qkv, sums_out, up_sum, d_mixed, held = refs[9:18]
-    *lands, send_sem, recv_sem, local_sem = refs[18:]
+def segment_backward_kernel(grid, tile, steps, per_project, *refs):
+    qkv, d_first, cls_grad, seg_low, cls_out, mixed, tokens, project, output, partial, cls_part = refs[:11]
+    d_x, layer_out, sums_qkv, sums_out, up_sum, partial_mixed = refs[11:17]
+    d_mixed, d_qkv, d_branch, sum_project, sum_output, packed, held = refs[17:24]
+    *lands, send_sem, recv_sem, local_sem = refs[24:]
     width = d_first.shape[1]
+    per_output = packed.shape[-2] - per_project
     step = pl.program_id(0)
     coords = grid.coords()
     reduce, ticks = summing(grid, coords, held, lands, up_sum, send_sem, recv_sem)
     plan = {}
-    for tick in range(ticks - 1):
-        plan.setdefault(min(2 * steps - 1, tick + 1), []).append(tick)
+    for tick in range(1, ticks - 1):
+        at = (2, 5, 6)[tick - 1] if ticks == 5 and steps == 4 else min(2 * steps - 1, tick + 1)
+        plan.setdefault(at, []).append(tick)
 
     def at_point(which):
-        for at, stages in plan.items():
+        for at, some in plan.items():
             if at % 2 == which:
 
                 @pl.when(step == at // 2)
-                def _(stages=stages):
-                    for stage in stages:
-                        if stage == 0:
-                            load.wait()
-                        reduce(stage)
-
-    load = pltpu.make_async_copy(partial, held, local_sem.at[0])
+                def _(some=some):
+                    for tick in some:
+                        reduce(tick)
 
     @pl.when(step == 0)
     def _():
+        load = pltpu.make_async_copy(partial, held, local_sem.at[0])
         load.start()
+        for total in (sums_qkv, sums_out, sum_project, sum_output):
+            total[...] = jnp.zeros_like(total)
         grid.greet(coords)
-        sums_qkv[...] = jnp.zeros_like(sums_qkv)
-        sums_out[...] = jnp.zeros_like(sums_out)
+        load.wait()
+        reduce(0)
 
     at_point(0)
     place = lax.broadcasted_iota(jnp.int32, (tile, 1), 0)
@@ -1037,47 +1037,62 @@
     d_x[...] = grad + dot_nn(d_qkv[...], project[...])
     sums_qkv[...] += jnp.broadcast_to(row_sums(d_qkv[...]), sums_qkv.shape)
     sums_out[...] += jnp.broadcast_to(row_sums(branch), sums_out.shape)
+    sum_output[...] += dot_tn(d_branch[...], mixed[...])
+    for c in range(0, 3 * width, width):
+        sum_project[pl.ds(c, width), :] += dot_tn(d_qkv[:, pl.ds(c, width)], tokens[...])
 
     @pl.when(step == steps - 1)
     def _():
+        for d in range(grid.n):
+            where, rest = [], d
+            for size in grid.dims[::-1]:
+                where.append(rest % size)
+                rest //= size
+            rows = [sum_project[pl.ds(d * per_project, per_project), :], sum_output[pl.ds(d * per_output, per_output), :]]
+            packed[tuple(where[::-1])] = jnp.concatenate(rows, 0).astype(jnp.bfloat16)
+        store = pltpu.make_async_copy(packed, partial_mixed, local_sem.at[0])
+        store.start()
         reduce(ticks - 1)
         up_sum[...] += cls_part[...]
         reduce(None)
-
-
-def segment_backward(grid, qkv, d_first, cls_grad, seg_low, cls_out, project, output, partial, cls_part, cid):
+        store.wait()
+
+
+def segment_backward(grid, qkv, d_first, cls_grad, seg_low, cls_out, mixed, tokens, project, output, partial, cls_part, per_project, cid):
     rows, width = d_first.shape
     tile = 2 * SEG_LEN
     low, full = jnp.bfloat16, jnp.float32
     per_up = partial.shape[-2]
+    mixed_rows = 4 * width // grid.n
+    anywhere = pl.BlockSpec(memory_space=pl.ANY)
 
     def cut(columns):
         return pl.BlockSpec((tile, columns), lambda i: (i, 0))
 
     return pl.pallas_call(
-        functools.partial(segment_backward_kernel, grid, tile, rows // tile),
+        functools.partial(segment_backward_kernel, grid, tile, rows // tile, per_project),
         grid=(rows // tile,),
         in_specs=[
-            cut(3 * width), cut(width), whole(cls_grad.shape), cut(width), whole(cls_out.shape), whole(project.shape), whole(output.shape),
-            pl.BlockSpec(memory_space=pl.ANY), whole(cls_part.shape),
+            cut(3 * width), cut(width), whole(cls_grad.shape), cut(width), whole(cls_out.shape), cut(width), cut(width),
+            whole(project.shape), whole(output.shape), anywhere, whole(cls_part.shape),
         ],
         out_specs=[
-            cut(3 * width), cut(width), cut(width), cut(width),
-            pl.BlockSpec((8, 3 * width), lambda i: (0, 0)), pl.BlockSpec((8, width), lambda i: (0, 0)),
-            pl.BlockSpec((per_up, width), lambda i: (0, 0)),
+            cut(width), cut(width), pl.BlockSpec((8, 3 * width), lambda i: (0, 0)), pl.BlockSpec((8, width), lambda i: (0, 0)),
+            pl.BlockSpec((per_up, width), lambda i: (0, 0)), anywhere,
         ],
         out_shape=[
-            jax.ShapeDtypeStruct((rows, 3 * width), low), jax.ShapeDtypeStruct((rows, width), low),
             jax.ShapeDtypeStruct((rows, width), full), jax.ShapeDtypeStruct((rows, width), low),
             jax.ShapeDtypeStruct((8, 3 * width), full), jax.ShapeDtypeStruct((8, width), full),
-            jax.ShapeDtypeStruct((per_up, width), full),
+            jax.ShapeDtypeStruct((per_up, width), full), jax.ShapeDtypeStruct((*grid.dims, mixed_rows, width), low),
         ],
         scratch_shapes=[
-            pltpu.VMEM((tile, width), jnp.bfloat16), *summing_scratch(grid, per_up, width), pltpu.SemaphoreType.DMA((1,)),
+            pltpu.VMEM((tile, width), low), pltpu.VMEM((tile, 3 * width), low), pltpu.VMEM((tile, width), low),
+            pltpu.VMEM((3 * width, width), full), pltpu.VMEM((width, width), full), pltpu.VMEM((*grid.dims, mixed_rows, width), low),
+            *summing_scratch(grid, per_up, width), pltpu.SemaphoreType.DMA((1,)),
         ],
         compiler_params=pltpu.CompilerParams(collective_id=cid, has_side_effects=True, vmem_limit_bytes=60 * 2**20),
         name="segment_backward",
-    )(qkv, d_first, cls_grad, seg_low, cls_out, project, output, partial, cls_part)
+    )(qkv, d_first, cls_grad, seg_low, cls_out, mixed, tokens, project, output, partial, cls_part)
 
 
 def sum_kernel(grid, chunk_list, nparts, *refs):
@@ -1212,13 +1227,13 @@
     pair = jnp.concatenate([qkv_sums[:, :width], qkv_sums[:, 2 * width :]], 1)
 
     def laid(rows, size):
-        rows = cut(rows, size)
-        return jnp.pad(rows, ((0, 8 - rows.shape[0]), (0, 128 - size)))
-
+        return jnp.pad(cut(rows, size), ((0, 0), (0, 128 - size)))
+
+    none = jnp.zeros((1, 128), jnp.float32)
     own_small = jnp.concatenate(
         [
             laid(jnp.concatenate(list(sums[:5]) + [row_sums(branch)], 0), per_output), laid(sums[5], per_up), laid(pair, per_pair),
-            laid(jnp.concatenate(list(sums0[:5]), 0), per_output), laid(sums0[5], per_up),
+            laid(jnp.concatenate(list(sums0[:5]), 0), per_output), none, laid(sums0[5], per_up), none,
         ],
         0,
     )
@@ -1273,51 +1288,36 @@
         grid, all_first.reshape(slots, width), all_cot.reshape(slots, width), placement, mixed1, up1, down1, up0, down0,
         smalls, table, sizes, partial_down, 2,
     )
-    d_qkv, d_branch, d_x, layer_out, sums_qkv, sums_out, up_sum = segment_backward(
-        grid, qkv, d_first, cls_grad, seg_low, cross_own, project, output, partial_up, z_up, 3
+    d_x, layer_out, sums_qkv, sums_out, up_sum, partial_mixed = segment_backward(
+        grid, qkv, d_first, cls_grad, seg_low, cross_own, mixed, low_tokens, project, output, partial_up, z_up, per_project, 3
     )
-    grad_project, grad_output = [
-        dot_tn(left, right).astype(jnp.bfloat16).reshape(n, -1, width)
-        for left, right in ((d_qkv, low_tokens), (d_branch, mixed))
-    ]
-
-    def per_device(vector):
-        return vector.reshape(vector.shape[:-1] + (n, -1))
+
+    def per_device(rows):
+        cut = rows.reshape(rows.shape[0], n, -1).transpose(1, 0, 2)
+        return jnp.pad(cut, ((0, 0), (0, 0), (0, 128 - cut.shape[2])))
 
     seg_small = jnp.concatenate(
         [
-            per_device(jnp.concatenate([sums_qkv[0, :width], sums_qkv[0, 2 * width :]])), per_device(sums_out[0]),
-            per_device(up_sums[0]), per_device(norm_sums[4]),
-            per_device(norm_sums[:4]).transpose(1, 0, 2).reshape(n, -1),
+            per_device(jnp.concatenate([norm_sums[:5], sums_out[:1]], 0)), per_device(up_sums[:1]),
+            per_device(jnp.concatenate([sums_qkv[:1, :width], sums_qkv[:1, 2 * width :]], 1)),
         ],
         1,
     )
-    small_size = seg_small.shape[1]
-    small_width = -(-small_size // 128) * 128
-    seg_small = jnp.pad(seg_small[:, None], ((0, 0), (0, 7), (0, small_width - small_size)))
-    mixed_sum, small_sum = sum_to_owners(grid, [jnp.concatenate([grad_project, grad_output], 1), seg_small], 4)
-    cuts, at = [], 0
-    for size in (per_pair, per_output, per_up, per_output, 4 * per_output):
-        cuts.append(small_sum[0, at : at + size])
-        at += size
-    pair_g = jnp.stack([cuts[0], own_small[16, :per_pair]])
-    out_g = jnp.stack([cuts[1], own_small[5, :per_output]])
-    up_g = jnp.stack([cuts[2] + own_small[32, :per_up], own_small[8, :per_up]])
-    down_g = jnp.stack([cuts[3] + own_small[28, :per_output], own_small[4, :per_output]])
-    norm_g = jnp.stack([cuts[4].reshape(4, per_output) + own_small[24:28, :per_output], own_small[0:4, :per_output]])
+    mixed_sum, small_sum = sum_to_owners(grid, [partial_mixed.reshape(n, -1, width), seg_small], 4)
+    both = jnp.stack([small_sum + own_small[8:], own_small[:8]])
     return (
         layer_out.reshape(tokens.shape),
         d_x.reshape(tokens.shape),
         jnp.swapaxes(jnp.stack([mixed_sum[:per_project], g_project]), 1, 2),
-        pair_g,
+        both[:, 7, :per_pair],
         jnp.swapaxes(jnp.stack([mixed_sum[per_project:], g_output]), 1, 2),
-        out_g,
+        both[:, 5, :per_output],
         jnp.swapaxes(jnp.stack([up_sum, g_up]), 1, 2),
-        up_g,
+        both[:, 6, :per_up],
         jnp.stack([down_sum, g_down]),
-        down_g,
-        norm_g[:, :2],
-        norm_g[:, 2:],
+        both[:, 4, :per_output],
+        both[:, 0:2, :per_output],
+        both[:, 2:4, :per_output],
         g_table.T,
     )
 

time: 366 us -> 340 us (0.929)
  Pallas kernels: 331 us -> 319 us
  matrix products: 7.17 us -> 0 us
  other arithmetic: 10.5 us -> 5.57 us
    dot_general x2 -> x0, matrix products: 7.17 us -> none  [dot_tn(): lax.dot_general(left, right, (((0,), (0,)), ((), ())), preferred_element_...]
    pallas_call x1, Pallas kernels: 99.5 us -> 93.7 us  [segment_forward(): pl.pallas_call(functools.partial(segment_forward_kernel, grid, tile, step...]
    pallas_call x1, Pallas kernels: 56 us -> 51 us  [segment_backward(): pl.pallas_call(functools.partial(segment_backward_kernel, grid, tile, row...]
where the time goes in v4:
time: 340 us; the launch traced here: 335 us
  Pallas kernels  319 us (94%)
  local copies, waits for them, and re-layouts  9.6 us (3%)
  other arithmetic  5.57 us (2%)
    pallas_call x1, Pallas kernels, segment_forward(): pl.pallas_call(functools.partial(segment_forward_kernel, grid, tile, step...  93.7 us
    pallas_call x1, Pallas kernels, gather_weights(): pl.pallas_call(functools.partial(weights_kernel, grid, (width, per_projec...  88.5 us
    pallas_call x1, Pallas kernels, cross_block(): pl.pallas_call(functools.partial(cross_kernel, grid, sizes), in_specs=[vm...  51.3 us
    pallas_call x1, Pallas kernels, segment_backward(): pl.pallas_call(functools.partial(segment_backward_kernel, grid, tile, row...  51 us
    pallas_call x1, Pallas kernels, sum_to_owners(): pl.pallas_call(functools.partial(sum_kernel, grid, chunk_list, nparts), o...  34.2 us

profile of v4, /device:TPU:0, one launch (start us, length us, event | category | flops | bytes accessed | tf_op | source)
XLA Modules:
  0.0 334.9 jit_solution(9308760983537592442)
XLA Ops:
  0.6 88.5 %gather_weights.1 = (bf16[2,2,2,4,96,768]{5,4,3,2,1,0:T(8,128)(2,1)}, bf16[2,2,2,4,96,768]{5,4,3,2,1,0:T(8,128)(2,1)}, bf16[2,2,2,4,96,768]{5,4,3,2,1,0:T(8,128)...) custom-call(bf16[2,72,768]{2,1,0:T(8,128)(2,1)} %bitcast.69, ...), custom_call_target="tpu_custom_call" | custom-call | tf_op jit(solution)/shard_map/gather_weights/pallas_call | solution.py:489
  89.2 0.0 copy-start.11
  89.2 93.7 %segment_forward.1 = (bf16[1024,2304]{1,0:T(8,128)(2,1)}, bf16[1024,768]{1,0:T(8,128)(2,1)}, f32[1024,768]{1,0:T(8,128)}, bf16[1024,768]{1,0:T(8,128)(2,1)}, f32...) custom-call(bf16[1024,768]{1,0:T(8,128)(2,1)} %bitcast.51, ...), custom_call_target="tpu_custom_call" | custom-call | tf_op jit(solution)/shard_map/segment_forward/pallas_call | solution.py:769
  182.9 0.0 copy-done.11
  182.9 0.8 copy.30.refs_3_
  183.7 51.3 %cross_block.1 = (f32[72,768]{1,0:T(8,128)}, f32[24,768]{1,0:T(8,128)}, f32[96,768]{1,0:T(8,128)}, f32[96,768]{1,0:T(8,128)}, f32[96,768]{1,0:T(8,128)}, /*index...) custom-call(f32[256,768]{1,0:T(8,128)} %bitcast.59, ...), custom_call_target="tpu_custom_call" | custom-call | tf_op jit(solution)/shard_map/cross_block/pallas_call | solution.py:971
  235.0 0.0 copy-start.8
  235.0 51.0 %segment_backward.1 = (f32[1024,768]{1,0:T(8,128)}, bf16[1024,768]{1,0:T(8,128)(2,1)}, f32[8,2304]{1,0:T(8,128)}, f32[8,768]{1,0:T(8,128)}, f32[96,768]{1,0:T(8,128)}, /*index=5*/bf16[2,2,2,4,96,768]{5,4,3,2,1,0:T(8,128)(2,1)}) custom-call(bf16[1024,2304]{1,0:T(8,128)(2,1)} %get-tuple-element.67.refs_0_, f32[1024,768]{1,0:T(8,128)} %get-tuple-element.68.refs_1_, ...), custom_call_target="tpu_custom_call" | custom-call | tf_op jit(solution)/shard_map/segment_backward/pallas_call | solution.py:1072
  286.0 0.0 copy-start.10
  286.0 0.0 copy-start.2
  286.0 0.0 copy-start.3
  286.0 0.0 copy-start.4
  286.0 0.0 copy-start.5
  286.0 0.8 slice.46
  286.9 0.0 copy-done.8
  286.9 0.1 reshape.82
  287.0 0.8 fusion.1
  287.8 0.1 transpose_reshape.7
  287.9 0.9 slice_reduce_fusion
  288.8 0.1 transpose_reshape.6
  288.9 0.7 copy.31
  289.6 0.0 copy-start.7
  289.6 0.0 copy-start.6
  289.6 34.2 %sum_to_owners.1 = (f32[96,768]{1,0:T(8,128)}, f32[8,128]{1,0:T(8,128)}) custom-call(bf16[2,2,2,4,96,768]{5,4,3,2,1,0:T(8,128)(2,1)} %get-tuple-element.86.refs_0_, f32[2,2,2,4,8,128]{5,4,3,2,1,0:T(8,128)} %bitcast.61), custom_call_target="tpu_custom_call" | custom-call | tf_op jit(solution)/shard_map/sum_to_owners/pallas_call | solution.py:1145
  323.8 0.0 copy-done.10
  323.8 0.7 add_bitcast_fusion
  324.5 0.6 pad_maximum_fusion.2
  325.1 0.6 pad_maximum_fusion.5
  325.6 0.0 copy-done.2
  325.6 0.0 copy-done.3
  325.6 0.0 copy-done.4
  325.6 0.0 copy-done.5
  325.6 0.0 copy-start
  325.7 1.1 maximum_bitcast_fusion
  326.7 0.6 pad_maximum_fusion.4
  327.3 0.9 slice_bitcast_fusion.1
  328.2 0.0 copy-done.7
  328.2 0.7 maximum_bitcast_fusion.2
  328.9 0.6 pad_maximum_fusion.7
  329.4 0.9 slice_bitcast_fusion
  330.4 0.0 copy-done.6
  330.4 0.8 maximum_bitcast_fusion.1
  331.2 0.0 copy-done.1
  331.2 1.1 copy.35
  332.3 0.0 copy-done
  332.4 1.7 copy.36
  334.0 0.0 copy-done.9
  334.0 0.6 copy.37
  (5 shorter events, 0.1 us)
Async XLA Ops:
  89.2 93.7 %copy-start.11 = (s32[256]{0:T(256)S(1)}, s32[256]{0:T(256)}, u32[]{:S(2)}) copy-start(s32[256]{0:T(256)} %param.16) | copy-start | bytes 3076
  235.0 51.9 %copy-start.8 = (f32[8,768]{1,0:T(8,128)S(1)}, f32[8,768]{1,0:T(8,128)}, u32[]{:S(2)}) copy-start(f32[8,768]{1,0:T(8,128)} %get-tuple-element.87) | copy-start | bytes 73732
  286.0 37.8 %copy-start.10 = (f32[16,128]{1,0:T(8,128)S(1)}, f32[16,128]{1,0:T(8,128)}, u32[]{:S(2)}) copy-start(f32[16,128]{1,0:T(8,128)} %get-tuple-element.94) | copy-start | bytes 24580
  286.0 39.6 %copy-start.2 = (f32[96,768]{1,0:T(8,128)S(1)}, f32[96,768]{1,0:T(8,128)}, u32[]{:S(2)}) copy-start(f32[96,768]{1,0:T(8,128)} %get-tuple-element.97) | copy-start | bytes 884740
  286.0 39.6 %copy-start.3 = (f32[96,768]{1,0:T(8,128)S(1)}, f32[96,768]{1,0:T(8,128)}, u32[]{:S(2)}) copy-start(f32[96,768]{1,0:T(8,128)} %get-tuple-element.99) | copy-start | bytes 884740
  286.0 39.6 %copy-start.4 = (f32[96,768]{1,0:T(8,128)S(1)}, f32[96,768]{1,0:T(8,128)}, u32[]{:S(2)}) copy-start(f32[96,768]{1,0:T(8,128)} %get-tuple-element.98) | copy-start | bytes 884740
  286.0 39.6 %copy-start.5 = (f32[96,768]{1,0:T(8,128)S(1)}, f32[96,768]{1,0:T(8,128)}, u32[]{:S(2)}) copy-start(f32[96,768]{1,0:T(8,128)} %get-tuple-element.96) | copy-start | bytes 884740
  289.6 38.6 %copy-start.7 = (f32[24,768]{1,0:T(8,128)S(1)}, f32[24,768]{1,0:T(8,128)}, u32[]{:S(2)}) copy-start(f32[24,768]{1,0:T(8,128)} %get-tuple-element.95) | copy-start | bytes 221188
  289.6 40.8 %copy-start.6 = (f32[72,768]{1,0:T(8,128)S(1)}, f32[72,768]{1,0:T(8,128)}, u32[]{:S(2)}) copy-start(f32[72,768]{1,0:T(8,128)} %get-tuple-element.92) | copy-start | bytes 663556
  289.6 41.6 %copy-start.1 = (bf16[1024,768]{1,0:T(8,128)(2,1)S(1)}, bf16[1024,768]{1,0:T(8,128)(2,1)}, u32[]{:S(2)}) copy-start(bf16[1024,768]{1,0:T(8,128)(2,1)} %get-tuple-element.84) | copy-start | bytes 4718596
  325.6 6.7 %copy-start = (f32[1024,768]{1,0:T(8,128)S(1)}, f32[1024,768]{1,0:T(8,128)}, u32[]{:S(2)}) copy-start(f32[1024,768]{1,0:T(8,128)} %get-tuple-element.85) | copy-start | bytes 9437188
  332.4 1.7 copy-start.9

commit v5 on v4

--- a/solution.py
+++ b/solution.py
@@ -191,8 +191,8 @@
         else:
             held[where] = total
 
-    def sent(self, k):
-        for stage in range(self.stages):
+    def sent(self, k, stages):
+        for stage in range(stages):
             for copy in self.copies(k, stage):
                 copy.wait_send()
 
@@ -821,13 +821,13 @@
 def cross_kernel(grid, sizes, *refs):
     per_project, per_output, per_up, per_pair = sizes
     (firsts, grads, placed_row, placed_col, mixed1, up1, down1, up0, down0, vec, vec_pair, vec_up, table, partial) = refs[:14]
-    g_project, g_output, g_up, g_down, z_up, down_sum, smalls, g_table, cross_own, d_first_own = refs[14:24]
+    g_project, g_output, g_up, g_down, z_up, z_down, smalls, g_table, cross_own, d_first_own, line_down = refs[14:25]
     names = ("qkv", "slope", "d_mixed", "mixed", "normed", "hidden", "d_down", "d_inner", "d_qkv")
-    r = dict(zip(names, refs[24:33]))
-    held_mixed, project, output, up, down, z_up_w, z_down_w, z_slope, z_normed, z_hidden, z_d_down, z_d_inner, rows_f = refs[33:46]
-    held, *lands, send_sem, recv_sem, local_sem = refs[46:]
+    r = dict(zip(names, refs[25:34]))
+    held_mixed, project, output, up, down, z_up_w, z_down_w, z_slope, z_normed, z_hidden, z_d_down, z_d_inner, rows_f = refs[34:47]
+    held, *lands, send_sem, recv_sem, local_sem = refs[47:]
     coords = grid.coords()
-    reduce, ticks = summing(grid, coords, held, lands, down_sum, send_sem, recv_sem)
+    reduce, ticks = summing(grid, coords, held, lands, None, send_sem, recv_sem, 1)
     load_partial = pltpu.make_async_copy(partial, held, local_sem.at[5])
     load_partial.start()
     loads = [pltpu.make_async_copy(*p, local_sem.at[i]) for i, p in enumerate(
@@ -885,7 +885,10 @@
     r["d_mixed"][...] = dot_nn(branch, output[...]).astype(jnp.bfloat16)
     attend_back(r["qkv"], r["d_mixed"], r["d_qkv"], slots, slots, width, allowed)
     d_x = d_first + dot_nn(r["d_qkv"][...], project[...])
-    reduce(3)
+    for tick in range(3, ticks):
+        reduce(tick)
+    store = pltpu.make_async_copy(held.at[coords[:-1]], line_down, local_sem.at[5])
+    store.start()
 
     g_project[...] = dot_tn(own_columns(r["d_qkv"][...], me * per_project, per_project), x_low)
     g_output[...] = dot_tn(own_columns(branch, me * per_output, per_output), r["mixed"][...])
@@ -908,29 +911,28 @@
     rows_f[...] = d_first0
     d_first_own[...] = rows_f[mine, :]
     z_up[...] = dot_tn(own_columns(z_d_inner[...], me * per_up, per_up), z_normed[...])
-    z_down = dot_tn(own_columns(z_hidden[...], me * per_up, per_up), z_d_down[...])
+    z_down[...] = dot_tn(own_columns(z_hidden[...], me * per_up, per_up), z_d_down[...])
     norm_rows = jnp.concatenate(list(sums[:5]) + [jnp.zeros((3, width), jnp.float32)], 0)
     smalls[8:16, 0:per_output] = own_sums(norm_rows, me * per_output, per_output)
     up_rows = jnp.broadcast_to(sums[5], (8, sums[5].shape[1]))
     smalls[14:15, 0:per_up] = own_sums(up_rows, me * per_up, per_up)[0:1]
-    for tick in range(4, ticks):
-        reduce(tick)
-    down_sum[...] += z_down
+    store.wait()
     reduce(None)
 
 
-def summing(grid, coords, held, lands, out, send_sem, recv_sem):
-    ndims = len(grid.dims)
+def summing(grid, coords, held, lands, out, send_sem, recv_sem, short=0):
+    ndims = len(grid.dims) - short
     units = [halves(held.shape[-2], held.dtype)]
     cuts = [cut for unit in units for cut in unit]
-    chunks = [(held, lands[k * ndims : (k + 1) * ndims], out, *cut) for k, cut in enumerate(cuts)]
+    whole_dims = len(grid.dims)
+    chunks = [(held, lands[k * whole_dims : (k + 1) * whole_dims], out, *cut) for k, cut in enumerate(cuts)]
     scatter = Scatter(grid, coords, chunks, send_sem, recv_sem)
     per = len(units[0])
 
     def reduce(tick):
         if tick is None:
             for k in range(len(chunks)):
-                scatter.sent(k)
+                scatter.sent(k, ndims)
             return
         for stage in range(ndims + 1):
             u = tick - stage
@@ -971,8 +973,8 @@
     return pl.pallas_call(
         functools.partial(cross_kernel, grid, sizes),
         in_specs=[vmem] * 4 + [anywhere] * 5 + [vmem] * 4 + [anywhere],
-        out_specs=[vmem] * len(outs),
-        out_shape=[jax.ShapeDtypeStruct(s, full) for s in outs],
+        out_specs=[vmem] * len(outs) + [anywhere],
+        out_shape=[jax.ShapeDtypeStruct(s, full) for s in outs] + [jax.ShapeDtypeStruct((grid.fsdp, per_up, width), low)],
         scratch_shapes=[
             held(slots, 3 * width), held(slots, hidden_units), held(slots, width), held(slots, width), held(slots, width),
             held(slots, hidden_units), held(slots, width), held(slots, hidden_units), held(slots, 3 * width),
@@ -988,18 +990,32 @@
 
 
 def segment_backward_kernel(grid, tile, steps, per_project, *refs):
-    qkv, d_first, cls_grad, seg_low, cls_out, mixed, tokens, project, output, partial, cls_part = refs[:11]
-    d_x, layer_out, sums_qkv, sums_out, up_sum, partial_mixed = refs[11:17]
-    d_mixed, d_qkv, d_branch, sum_project, sum_output, packed, held = refs[17:24]
-    *lands, send_sem, recv_sem, local_sem = refs[24:]
+    (qkv, d_first, cls_grad, seg_low, cls_out, mixed, tokens, project, output, partial, cls_up, cls_down, line_down, norm_sums, up_sums,
+     own_small) = refs[:16]
+    d_x, layer_out, up_sum, down_sum, mixed_sum, small_out = refs[16:22]
+    d_mixed, d_qkv, d_branch, sum_project, sum_output, packed, sums_qkv, sums_out, small_held, small_sum = refs[22:32]
+    first_sems = 32 + summing_length(grid, partial.shape[-2])
+    held, *lands, send_sem, recv_sem = refs[32:first_sems]
+    line_land, line_send, line_recv = refs[first_sems : first_sems + 3]
+    *last_lands, last_send, last_recv, local_sem = refs[first_sems + 3 :]
+    fs, ndims = grid.fsdp, len(grid.dims)
     width = d_first.shape[1]
     per_output = packed.shape[-2] - per_project
     step = pl.program_id(0)
     coords = grid.coords()
     reduce, ticks = summing(grid, coords, held, lands, up_sum, send_sem, recv_sem)
+    line = []
+    for ahead in range(1, fs):
+        target, value = grid.peer(coords, ndims - 1, ahead)
+        line.append(
+            pltpu.make_async_remote_copy(
+                line_down.at[value], line_land.at[ahead - 1], line_send.at[ahead - 1], line_recv.at[ahead - 1],
+                device_id=target, device_id_type=MESH,
+            )
+        )
     plan = {}
     for tick in range(1, ticks - 1):
-        at = (2, 5, 6)[tick - 1] if ticks == 5 and steps == 4 else min(2 * steps - 1, tick + 1)
+        at = (2, 5, 7)[tick - 1] if ticks == 5 and steps == 4 else min(2 * steps - 1, tick + 1)
         plan.setdefault(at, []).append(tick)
 
     def at_point(which):
@@ -1015,11 +1031,13 @@
     def _():
         load = pltpu.make_async_copy(partial, held, local_sem.at[0])
         load.start()
-        for total in (sums_qkv, sums_out, sum_project, sum_output):
+        for total in (sums_qkv, sums_out, sum_project, sum_output, small_held):
             total[...] = jnp.zeros_like(total)
         grid.greet(coords)
         load.wait()
         reduce(0)
+        for copy in line:
+            copy.start()
 
     at_point(0)
     place = lax.broadcasted_iota(jnp.int32, (tile, 1), 0)
@@ -1049,16 +1067,60 @@
                 where.append(rest % size)
                 rest //= size
             rows = [sum_project[pl.ds(d * per_project, per_project), :], sum_output[pl.ds(d * per_output, per_output), :]]
-            packed[tuple(where[::-1])] = jnp.concatenate(rows, 0).astype(jnp.bfloat16)
-        store = pltpu.make_async_copy(packed, partial_mixed, local_sem.at[0])
-        store.start()
-        reduce(ticks - 1)
-        up_sum[...] += cls_part[...]
+            where = tuple(where[::-1])
+            packed[where] = jnp.concatenate(rows, 0).astype(jnp.bfloat16)
+            per_pair = 2 * per_output
+            at = d * per_pair if d * per_pair < width else d * per_pair + width
+            for row, count, source, first, size in (
+                (0, 5, norm_sums[0:5, :], d * per_output, per_output), (5, 1, sums_out[0:1, :], d * per_output, per_output),
+                (6, 1, up_sums[0:1, :], d * 4 * per_output, 4 * per_output), (7, 1, sums_qkv[0:1, :], at, per_pair),
+            ):
+                small_held[where + (pl.ds(row, count), pl.ds(0, size))] = source[:, first : first + size]
+        units, cuts = [], []
+        for unit in pairs(packed.shape[-2]):
+            units.append(list(range(len(cuts), len(cuts) + len(unit))))
+            cuts += [(packed, mixed_sum, *cut) for cut in unit]
+        units[0].append(len(cuts))
+        cuts.append((small_held, small_sum, 0, 8, 0))
+        last = Scatter(
+            grid, coords, [(h, last_lands[k * ndims : (k + 1) * ndims], *rest) for k, (h, *rest) in enumerate(cuts)], last_send, last_recv
+        )
+        for tick in range(len(units) + ndims):
+            for stage in range(ndims + 1):
+                u = tick - stage
+                if not 0 <= u < len(units):
+                    continue
+                for k in units[u]:
+                    if stage > 0:
+                        last.add(k, stage - 1)
+                    if stage < ndims:
+                        last.start(k, stage)
+            if tick == 1:
+                total = line_down[coords[-1]].astype(jnp.float32) + cls_down[...]
+                for ahead, copy in enumerate(line):
+                    copy.wait_recv()
+                    total += line_land[ahead].astype(jnp.float32)
+                down_sum[...] = total
+            if tick == 2:
+                reduce(ticks - 1)
+                up_sum[...] += cls_up[...]
+        small_out[0] = small_sum[...] + own_small[8:16, :]
+        small_out[1] = own_small[0:8, :]
+        for copy in line:
+            copy.wait_send()
+        for k in range(len(cuts)):
+            last.sent(k, ndims)
         reduce(None)
-        store.wait()
-
-
-def segment_backward(grid, qkv, d_first, cls_grad, seg_low, cls_out, mixed, tokens, project, output, partial, cls_part, per_project, cid):
+
+
+def summing_length(grid, rows):
+    return 1 + len(halves(rows, jnp.bfloat16)) * len(grid.dims) + 2
+
+
+def segment_backward(
+    grid, qkv, d_first, cls_grad, seg_low, cls_out, mixed, tokens, project, output, partial, cls_up, cls_down, line_down, norm_sums,
+    up_sums, own_small, per_project, cid,
+):
     rows, width = d_first.shape
     tile = 2 * SEG_LEN
     low, full = jnp.bfloat16, jnp.float32
@@ -1069,88 +1131,44 @@
     def cut(columns):
         return pl.BlockSpec((tile, columns), lambda i: (i, 0))
 
+    def fixed(*shape):
+        return pl.BlockSpec(shape, lambda i: (0,) * len(shape))
+
+    last_lands, last_count = [], 0
+    for first, count, colour in [c for unit in pairs(mixed_rows) for c in unit]:
+        last_lands += Scatter.landing(grid, count, width, low, colour)
+        last_count += 1
+    last_lands += Scatter.landing(grid, 8, 128, full, 0)
     return pl.pallas_call(
         functools.partial(segment_backward_kernel, grid, tile, rows // tile, per_project),
         grid=(rows // tile,),
         in_specs=[
             cut(3 * width), cut(width), whole(cls_grad.shape), cut(width), whole(cls_out.shape), cut(width), cut(width),
-            whole(project.shape), whole(output.shape), anywhere, whole(cls_part.shape),
+            whole(project.shape), whole(output.shape), anywhere,
+            *[whole(a.shape) for a in (cls_up, cls_down, line_down, norm_sums, up_sums, own_small)],
         ],
         out_specs=[
-            cut(width), cut(width), pl.BlockSpec((8, 3 * width), lambda i: (0, 0)), pl.BlockSpec((8, width), lambda i: (0, 0)),
-            pl.BlockSpec((per_up, width), lambda i: (0, 0)), anywhere,
+            cut(width), cut(width), fixed(per_up, width), fixed(per_up, width), fixed(mixed_rows, width), fixed(2, 8, 128),
         ],
         out_shape=[
             jax.ShapeDtypeStruct((rows, width), full), jax.ShapeDtypeStruct((rows, width), low),
-            jax.ShapeDtypeStruct((8, 3 * width), full), jax.ShapeDtypeStruct((8, width), full),
-            jax.ShapeDtypeStruct((per_up, width), full), jax.ShapeDtypeStruct((*grid.dims, mixed_rows, width), low),
+            jax.ShapeDtypeStruct((per_up, width), full), jax.ShapeDtypeStruct((per_up, width), full),
+            jax.ShapeDtypeStruct((mixed_rows, width), full), jax.ShapeDtypeStruct((2, 8, 128), full),
         ],
         scratch_shapes=[
             pltpu.VMEM((tile, width), low), pltpu.VMEM((tile, 3 * width), low), pltpu.VMEM((tile, width), low),
             pltpu.VMEM((3 * width, width), full), pltpu.VMEM((width, width), full), pltpu.VMEM((*grid.dims, mixed_rows, width), low),
-            *summing_scratch(grid, per_up, width), pltpu.SemaphoreType.DMA((1,)),
+            pltpu.VMEM((8, 3 * width), full), pltpu.VMEM((8, width), full), pltpu.VMEM((*grid.dims, 8, 128), full), pltpu.VMEM((8, 128), full),
+            *summing_scratch(grid, per_up, width),
+            pltpu.VMEM((grid.fsdp - 1, per_up, width), low), pltpu.SemaphoreType.DMA((grid.fsdp - 1,)), pltpu.SemaphoreType.DMA((grid.fsdp - 1,)),
+            *last_lands, *grid.sems(last_count + 1), pltpu.SemaphoreType.DMA((1,)),
         ],
-        compiler_params=pltpu.CompilerParams(collective_id=cid, has_side_effects=True, vmem_limit_bytes=60 * 2**20),
+        compiler_params=pltpu.CompilerParams(collective_id=cid, has_side_effects=True, vmem_limit_bytes=61 * 2**20),
         name="segment_backward",
-    )(qkv, d_first, cls_grad, seg_low, cls_out, mixed, tokens, project, output, partial, cls_part)
-
-
-def sum_kernel(grid, chunk_list, nparts, *refs):
-    given, outs = refs[:nparts], refs[nparts : 2 * nparts]
-    held = refs[2 * nparts : 3 * nparts]
-    lands = refs[3 * nparts : -3]
-    send_sem, recv_sem, load_sem = refs[-3:]
-    ndims = len(grid.dims)
-    coords = grid.coords()
-    loads = [pltpu.make_async_copy(given[a], held[a], load_sem.at[a]) for a in range(nparts)]
-    for load in loads:
-        load.start()
-    grid.greet(coords)
-    chunks = [
-        (held[a], lands[k * ndims : (k + 1) * ndims], outs[a], first, count, colour)
-        for k, (a, first, count, colour, unit) in enumerate(chunk_list)
-    ]
-    scatter = Scatter(grid, coords, chunks, send_sem, recv_sem)
-    loaded = set()
-    units = sorted({c[4] for c in chunk_list})
-    for tick in range(len(units) + ndims):
-        for stage in range(ndims + 1):
-            u = tick - stage
-            if not 0 <= u < len(units):
-                continue
-            for k, (a, first, count, colour, unit) in enumerate(chunk_list):
-                if unit != units[u]:
-                    continue
-                if a not in loaded:
-                    loaded.add(a)
-                    loads[a].wait()
-                if stage >= 1:
-                    scatter.add(k, stage - 1)
-                if stage < ndims:
-                    scatter.start(k, stage)
-    for k in range(len(chunks)):
-        scatter.sent(k)
-
-
-def sum_to_owners(grid, parts, cid):
-    chunk_list = []
-    for a, p in enumerate(parts):
-        for unit, cuts in enumerate(pairs(p.shape[1]) if p.dtype == jnp.bfloat16 else [halves(p.shape[1], p.dtype)]):
-            chunk_list += [(a, *cut, unit) for cut in cuts]
-    nparts = len(parts)
-    shaped = [p.reshape(tuple(grid.dims) + p.shape[1:]) for p in parts]
-    lands = []
-    for a, first, count, colour, unit in chunk_list:
-        lands += Scatter.landing(grid, count, parts[a].shape[2], parts[a].dtype, colour)
-    return pl.pallas_call(
-        functools.partial(sum_kernel, grid, chunk_list, nparts),
-        out_shape=[jax.ShapeDtypeStruct(p.shape[1:], jnp.float32) for p in parts],
-        in_specs=[pl.BlockSpec(memory_space=pl.ANY)] * nparts,
-        out_specs=[pl.BlockSpec(memory_space=pltpu.VMEM)] * nparts,
-        scratch_shapes=[pltpu.VMEM(s.shape, s.dtype) for s in shaped] + lands + grid.sems(len(chunk_list)) + [pltpu.SemaphoreType.DMA((nparts,))],
-        compiler_params=pltpu.CompilerParams(collective_id=cid, has_side_effects=True, vmem_limit_bytes=56 * 2**20),
-        name="sum_to_owners",
-    )(*shaped)
+    )(
+        qkv, d_first, cls_grad, seg_low, cls_out, mixed, tokens, project, output, partial, cls_up, cls_down, line_down, norm_sums, up_sums,
+        own_small,
+    )
 
 
 class Held:
@@ -1175,6 +1193,12 @@
 
     def __setitem__(self, where, value):
         self.value = self.value.at[self.plain(where)].set(value)
+
+
+def sum_to_lines(partial):
+    rows, width = partial.shape[-2:]
+    fs = partial.shape[-3]
+    return lax.psum_scatter(partial.reshape(-1, fs, rows, width), "dp", scatter_dimension=0, tiled=True)[0]
 
 
 def cross_plain(grid, firsts, grads, placement, mixed1, up1, down1, up0, down0, smalls, table, sizes, partial, cid):
@@ -1242,8 +1266,8 @@
     return (
         dot_tn(cut(r["d_qkv"][...], per_project), x_low), dot_tn(cut(branch, per_output), r["mixed"][...]),
         dot_tn(cut(r["d_inner"][...], per_up), r["normed"][...]), dot_tn(cut(r["hidden"][...], per_up), r["d_down"][...]),
-        dot_tn(cut(r0["d_inner"][...], per_up), r0["normed"][...]), dot_tn(cut(r0["hidden"][...], per_up), r0["d_down"][...]) + sum_to_owners(grid, [partial.reshape(grid.n, per_up, width)], cid)[0],
-        own_small, g_table, cut(out, per_slots, 0), cut(d_first0, per_slots, 0),
+        dot_tn(cut(r0["d_inner"][...], per_up), r0["normed"][...]), dot_tn(cut(r0["hidden"][...], per_up), r0["d_down"][...]),
+        own_small, g_table, cut(out, per_slots, 0), cut(d_first0, per_slots, 0), sum_to_lines(partial),
     )
 
 
@@ -1284,27 +1308,14 @@
         grid, low_tokens, cotangent.reshape(rows, width), mixed0, up0, down0, smalls, lines, per_project, 1
     )
     partial_up, partial_down = [p.reshape(*grid.dims, per_up, width) for p in (partial_up, partial_down)]
-    g_project, g_output, g_up, g_down, z_up, down_sum, own_small, g_table, cross_own, cls_grad = (cross_block if slots <= 256 else cross_plain)(
+    g_project, g_output, g_up, g_down, z_up, z_down, own_small, g_table, cross_own, cls_grad, line_down = (cross_block if slots <= 256 else cross_plain)(
         grid, all_first.reshape(slots, width), all_cot.reshape(slots, width), placement, mixed1, up1, down1, up0, down0,
         smalls, table, sizes, partial_down, 2,
     )
-    d_x, layer_out, sums_qkv, sums_out, up_sum, partial_mixed = segment_backward(
-        grid, qkv, d_first, cls_grad, seg_low, cross_own, mixed, low_tokens, project, output, partial_up, z_up, per_project, 3
+    d_x, layer_out, up_sum, down_sum, mixed_sum, both = segment_backward(
+        grid, qkv, d_first, cls_grad, seg_low, cross_own, mixed, low_tokens, project, output, partial_up, z_up, z_down, line_down,
+        norm_sums, up_sums, own_small, per_project, 3,
     )
-
-    def per_device(rows):
-        cut = rows.reshape(rows.shape[0], n, -1).transpose(1, 0, 2)
-        return jnp.pad(cut, ((0, 0), (0, 0), (0, 128 - cut.shape[2])))
-
-    seg_small = jnp.concatenate(
-        [
-            per_device(jnp.concatenate([norm_sums[:5], sums_out[:1]], 0)), per_device(up_sums[:1]),
-            per_device(jnp.concatenate([sums_qkv[:1, :width], sums_qkv[:1, 2 * width :]], 1)),
-        ],
-        1,
-    )
-    mixed_sum, small_sum = sum_to_owners(grid, [partial_mixed.reshape(n, -1, width), seg_small], 4)
-    both = jnp.stack([small_sum + own_small[8:], own_small[:8]])
     return (
         layer_out.reshape(tokens.shape),
         d_x.reshape(tokens.shape),

time: 340 us -> 326 us (0.959)
  Pallas kernels: 319 us -> 309 us
    pallas_call x1 -> x0, Pallas kernels: 34.2 us -> none  [sum_to_owners(): pl.pallas_call(functools.partial(sum_kernel, grid, chunk_list, nparts), o...]
    pallas_call x1, Pallas kernels: 51 us -> 78.5 us  [segment_backward(): pl.pallas_call(functools.partial(segment_backward_kernel, grid, tile, row...]
where the time goes in v5:
time: 326 us; the launch traced here: 322 us
  Pallas kernels  309 us (95%)
  local copies, waits for them, and re-layouts  8.37 us (3%)
  other arithmetic  3.75 us (1%)
    pallas_call x1, Pallas kernels, segment_forward(): pl.pallas_call(functools.partial(segment_forward_kernel, grid, tile, step...  93.7 us
    pallas_call x1, Pallas kernels, gather_weights(): pl.pallas_call(functools.partial(weights_kernel, grid, (width, per_projec...  88.5 us
    pallas_call x1, Pallas kernels, segment_backward(): pl.pallas_call(functools.partial(segment_backward_kernel, grid, tile, row...  78.5 us
    pallas_call x1, Pallas kernels, cross_block(): pl.pallas_call(functools.partial(cross_kernel, grid, sizes), in_specs=[vm...  48.1 us

profile of v5, /device:TPU:0, one launch (start us, length us, event | category | flops | bytes accessed | tf_op | source)
XLA Modules:
  0.0 322.1 jit_solution(13786394637330880060)
XLA Ops:
  0.6 88.5 %gather_weights.1 = (bf16[2,2,2,4,96,768]{5,4,3,2,1,0:T(8,128)(2,1)}, bf16[2,2,2,4,96,768]{5,4,3,2,1,0:T(8,128)(2,1)}, bf16[2,2,2,4,96,768]{5,4,3,2,1,0:T(8,128)...) custom-call(bf16[2,72,768]{2,1,0:T(8,128)(2,1)} %bitcast.60, ...), custom_call_target="tpu_custom_call" | custom-call | tf_op jit(solution)/shard_map/gather_weights/pallas_call | solution.py:489
  89.1 0.0 copy-start.8
  89.2 93.7 %segment_forward.1 = (bf16[1024,2304]{1,0:T(8,128)(2,1)}, bf16[1024,768]{1,0:T(8,128)(2,1)}, f32[1024,768]{1,0:T(8,128)}, bf16[1024,768]{1,0:T(8,128)(2,1)}, f32...) custom-call(bf16[1024,768]{1,0:T(8,128)(2,1)} %bitcast.44, ...), custom_call_target="tpu_custom_call" | custom-call | tf_op jit(solution)/shard_map/segment_forward/pallas_call | solution.py:769
  182.9 0.0 copy-done.8
  182.9 0.8 copy.27.refs_3_
  183.7 48.1 %cross_block.1 = (f32[72,768]{1,0:T(8,128)}, f32[24,768]{1,0:T(8,128)}, f32[96,768]{1,0:T(8,128)}, f32[96,768]{1,0:T(8,128)}, f32[96,768]{1,0:T(8,128)}, /*index...) custom-call(f32[256,768]{1,0:T(8,128)} %bitcast.52, ...), custom_call_target="tpu_custom_call" | custom-call | tf_op jit(solution)/shard_map/cross_block/pallas_call | solution.py:973
  231.8 0.0 copy-start.2
  231.8 0.0 copy-start.3
  231.8 0.0 copy-start.5
  231.9 0.0 copy-start.4
  231.9 78.5 %segment_backward.1 = (f32[1024,768]{1,0:T(8,128)}, bf16[1024,768]{1,0:T(8,128)(2,1)}, f32[96,768]{1,0:T(8,128)}, f32[96,768]{1,0:T(8,128)}, f32[96,768]{1,0:T(8,128)}, /*index=5*/f32[2,8,128]{2,1,0:T(8,128)}) custom-call(bf16[1024,2304]{1,0:T(8,128)(2,1)} %get-tuple-element.66.refs_0_, f32[1024,768]{1,0:T(8,128)} %get-tuple-element.67.refs_1_, ...), custom_call_target="tpu_custom_call" | custom-call | tf_op jit(solution)/shard_map/segment_backward/pallas_call | solution.py:1142
  310.4 0.0 copy-start.7
  310.4 0.0 copy-start.1
  310.4 0.0 copy-done.2
  310.4 0.0 copy-done.3
  310.5 0.0 copy-start
  310.5 2.3 maximum_bitcast_fusion
  312.8 0.9 slice_bitcast_fusion.1
  313.6 0.0 copy-done.5
  313.6 0.7 maximum_bitcast_fusion.2
  314.3 0.9 slice_bitcast_fusion
  315.3 0.0 copy-done.4
  315.3 0.8 maximum_bitcast_fusion.1
  316.1 0.0 copy-done.7
  316.1 0.6 fusion
  316.7 0.6 fusion.1
  317.2 0.6 slice.25
  317.8 0.6 slice.28
  318.4 0.0 copy-done.1
  318.4 1.1 copy.31
  319.5 0.0 copy-done
  319.5 0.0 copy-start.6
  319.5 1.7 copy.32
  321.2 0.0 copy-done.6
  321.2 0.6 copy.33
Async XLA Ops:
  89.1 93.7 %copy-start.8 = (s32[256]{0:T(256)S(1)}, s32[256]{0:T(256)}, u32[]{:S(2)}) copy-start(s32[256]{0:T(256)} %param.16) | copy-start | bytes 3076
  231.8 78.6 %copy-start.2 = (f32[96,768]{1,0:T(8,128)S(1)}, f32[96,768]{1,0:T(8,128)}, u32[]{:S(2)}) copy-start(f32[96,768]{1,0:T(8,128)} %get-tuple-element.95) | copy-start | bytes 884740
  231.8 78.6 %copy-start.3 = (f32[96,768]{1,0:T(8,128)S(1)}, f32[96,768]{1,0:T(8,128)}, u32[]{:S(2)}) copy-start(f32[96,768]{1,0:T(8,128)} %get-tuple-element.97) | copy-start | bytes 884740
  231.8 81.8 %copy-start.5 = (f32[24,768]{1,0:T(8,128)S(1)}, f32[24,768]{1,0:T(8,128)}, u32[]{:S(2)}) copy-start(f32[24,768]{1,0:T(8,128)} %get-tuple-element.93) | copy-start | bytes 221188
  231.9 83.4 %copy-start.4 = (f32[72,768]{1,0:T(8,128)S(1)}, f32[72,768]{1,0:T(8,128)}, u32[]{:S(2)}) copy-start(f32[72,768]{1,0:T(8,128)} %get-tuple-element.91) | copy-start | bytes 663556
  310.4 5.7 %copy-start.7 = (f32[2,8,128]{2,1,0:T(8,128)S(1)}, f32[2,8,128]{2,1,0:T(8,128)}, u32[]{:S(2)}) copy-start(f32[2,8,128]{2,1,0:T(8,128)} %get-tuple-element.92) | copy-start | bytes 24580
  310.4 7.9 %copy-start.1 = (bf16[1024,768]{1,0:T(8,128)(2,1)S(1)}, bf16[1024,768]{1,0:T(8,128)(2,1)}, u32[]{:S(2)}) copy-start(bf16[1024,768]{1,0:T(8,128)(2,1)} %get-tuple-element.88) | copy-start | bytes 4718596
  310.5 9.1 %copy-start = (f32[1024,768]{1,0:T(8,128)S(1)}, f32[1024,768]{1,0:T(8,128)}, u32[]{:S(2)}) copy-start(f32[1024,768]{1,0:T(8,128)} %get-tuple-element.89) | copy-start | bytes 9437188
  319.5 1.7 copy-start.6

commit v6 on v5

--- a/solution.py
+++ b/solution.py
@@ -621,7 +621,8 @@
     groups[0].append(len(chunks))
     chunks.append((None, line_cot, all_cot, 0, line_cot.shape[1], 1))
     first_chunk = len(chunks)
-    chunks.append((own_first, None, all_first, 0, own_first.shape[0], 0))
+    first_chunks = [first_chunk, first_chunk + 1]
+    chunks += [(own_first, None, all_first, half, 1, half) for half in range(2)]
     gather = Gather(grid, coords, chunks, send_sem, recv_sem)
 
     ticks = ndims + 1
@@ -643,7 +644,7 @@
     for tick in range(1, ticks - 1):
         at = round((2 * steps - 1) * tick / (ticks - 2))
         if ndims == 4 and steps == 4:
-            at = (1, 5, 7)[tick - 1]
+            at = (1, 6, 7)[tick - 1]
         plan.setdefault(at, []).append(tick)
 
     def at_point(which):
@@ -667,11 +668,12 @@
             for stage in first_events[first_points.index(name)]:
                 if stage == 0:
                     keep_first.start()
-                else:
-                    gather.landed(first_chunk, stage - 1)
-                    if stage == 1:
+                for k in first_chunks:
+                    if stage > 0:
+                        gather.landed(k, stage - 1)
+                    if stage == 1 and k == first_chunk:
                         keep_first.wait()
-                gather.start(first_chunk, stage)
+                    gather.start(k, stage)
 
     @pl.when(step == 0)
     def _():
@@ -699,7 +701,9 @@
 
     def take_first(first):
         for s in range(tile // SEG_LEN):
-            own_first[pl.ds(step * (tile // SEG_LEN) + s, 1), :] = first[s * SEG_LEN : s * SEG_LEN + 1]
+            for half in range(2):
+                row = first[s * SEG_LEN : s * SEG_LEN + 1, half * (width // 2) : (half + 1) * (width // 2)]
+                own_first[half, pl.ds(step * (tile // SEG_LEN) + s, 1), :] = row
 
     r["first"] = take_first
     x_low = tokens[...]
@@ -741,8 +745,9 @@
         for g in range(len(groups)):
             for k in groups[g]:
                 gather.sent(k, 1 if chunks[k][1] is not None else 0, ndims)
-        gather.landed(first_chunk, ndims - 1)
-        gather.sent(first_chunk, 0, ndims)
+        for k in first_chunks:
+            gather.landed(k, ndims - 1)
+            gather.sent(k, 0, ndims)
         for copy in stores + out:
             copy.wait()
 
@@ -757,7 +762,7 @@
     segs = rows // SEG_LEN
     low, full = jnp.bfloat16, jnp.float32
     up0, down0 = up0.reshape(hidden_units, width), down0.reshape(hidden_units, width)
-    count = 2 + sum(len(halves(r, low)) for r in (mixed_rows, per_up, per_up))
+    count = 3 + sum(len(halves(r, low)) for r in (mixed_rows, per_up, per_up))
     vmem, anywhere = pl.BlockSpec(memory_space=pltpu.VMEM), pl.BlockSpec(memory_space=pl.ANY)
 
     def cut(columns):
@@ -779,7 +784,7 @@
             shape(3 * width, low), shape(width, low), shape(width, full), shape(width, low),
             jax.ShapeDtypeStruct((8, width), full), jax.ShapeDtypeStruct((8, hidden_units), full),
             jax.ShapeDtypeStruct((3 * width, width), low), jax.ShapeDtypeStruct((width, width), low),
-            jax.ShapeDtypeStruct((*grid.dims, segs, width), full),
+            jax.ShapeDtypeStruct((*grid.dims, 2, segs, width // 2), full),
             jax.ShapeDtypeStruct((*grid.dims, mixed_rows, width), low),
             jax.ShapeDtypeStruct((*grid.dims, per_up, width), low), jax.ShapeDtypeStruct((*grid.dims, per_up, width), low),
             jax.ShapeDtypeStruct((*grid.dims, segs, width), full),
@@ -789,7 +794,7 @@
             pltpu.VMEM((tile, hidden_units), low), pltpu.VMEM((tile, width), low), pltpu.VMEM((tile, hidden_units), low),
             pltpu.VMEM((tile, width), low), pltpu.VMEM((tile, hidden_units), low), pltpu.VMEM((*grid.dims, mixed_rows, width), low),
             pltpu.VMEM((3 * width, width), low), pltpu.VMEM((width, width), low),
-            pltpu.VMEM((hidden_units, width), low), pltpu.VMEM((hidden_units, width), low), pltpu.VMEM((segs, width), full),
+            pltpu.VMEM((hidden_units, width), low), pltpu.VMEM((hidden_units, width), low), pltpu.VMEM((2, segs, width // 2), full),
             pltpu.VMEM((hidden_units, width), full), pltpu.VMEM((hidden_units, width), full),
         ]
         + grid.sems(count)
@@ -1309,7 +1314,7 @@
     )
     partial_up, partial_down = [p.reshape(*grid.dims, per_up, width) for p in (partial_up, partial_down)]
     g_project, g_output, g_up, g_down, z_up, z_down, own_small, g_table, cross_own, cls_grad, line_down = (cross_block if slots <= 256 else cross_plain)(
-        grid, all_first.reshape(slots, width), all_cot.reshape(slots, width), placement, mixed1, up1, down1, up0, down0,
+        grid, all_first.reshape(n, 2, seg_count, width // 2).transpose(0, 2, 1, 3).reshape(slots, width), all_cot.reshape(slots, width), placement, mixed1, up1, down1, up0, down0,
         smalls, table, sizes, partial_down, 2,
     )
     d_x, layer_out, up_sum, down_sum, mixed_sum, both = segment_backward(

time: 326 us -> 324 us (level)
  no operation moved by 1% of the time
where the time goes in v6:
time: 324 us; the launch traced here: 320 us
  Pallas kernels  306 us (94%)
  local copies, waits for them, and re-layouts  8.37 us (3%)
  other arithmetic  3.75 us (1%)
    pallas_call x1, Pallas kernels, segment_forward(): pl.pallas_call(functools.partial(segment_forward_kernel, grid, tile, step...  90.9 us
    pallas_call x1, Pallas kernels, gather_weights(): pl.pallas_call(functools.partial(weights_kernel, grid, (width, per_projec...  88.5 us
    pallas_call x1, Pallas kernels, segment_backward(): pl.pallas_call(functools.partial(segment_backward_kernel, grid, tile, row...  77.6 us
    pallas_call x1, Pallas kernels, cross_block(): pl.pallas_call(functools.partial(cross_kernel, grid, sizes), in_specs=[vm...  49.5 us

profile of v6, /device:TPU:0, one launch (start us, length us, event | category | flops | bytes accessed | tf_op | source)
XLA Modules:
  0.0 319.6 jit_solution(10317618809053343486)
XLA Ops:
  0.6 88.5 %gather_weights.1 = (bf16[2,2,2,4,96,768]{5,4,3,2,1,0:T(8,128)(2,1)}, bf16[2,2,2,4,96,768]{5,4,3,2,1,0:T(8,128)(2,1)}, bf16[2,2,2,4,96,768]{5,4,3,2,1,0:T(8,128)...) custom-call(bf16[2,72,768]{2,1,0:T(8,128)(2,1)} %bitcast.64, ...), custom_call_target="tpu_custom_call" | custom-call | tf_op jit(solution)/shard_map/gather_weights/pallas_call | solution.py:489
  89.1 0.0 copy-start.8
  89.2 90.9 %segment_forward.1 = (bf16[1024,2304]{1,0:T(8,128)(2,1)}, bf16[1024,768]{1,0:T(8,128)(2,1)}, f32[1024,768]{1,0:T(8,128)}, bf16[1024,768]{1,0:T(8,128)(2,1)}, f32...) custom-call(bf16[1024,768]{1,0:T(8,128)(2,1)} %bitcast.48, ...), custom_call_target="tpu_custom_call" | custom-call | tf_op jit(solution)/shard_map/segment_forward/pallas_call | solution.py:774
  180.0 0.0 copy-done.8
  180.1 0.8 copy.27.refs_3_
  180.9 49.5 %cross_block.1 = (f32[72,768]{1,0:T(8,128)}, f32[24,768]{1,0:T(8,128)}, f32[96,768]{1,0:T(8,128)}, f32[96,768]{1,0:T(8,128)}, f32[96,768]{1,0:T(8,128)}, /*index...) custom-call(f32[256,768]{1,0:T(8,128)} %bitcast.56, ...), custom_call_target="tpu_custom_call" | custom-call | tf_op jit(solution)/shard_map/cross_block/pallas_call | solution.py:978
  230.4 0.0 copy-start.2
  230.4 0.0 copy-start.3
  230.4 0.0 copy-start.5
  230.4 0.0 copy-start.4
  230.4 77.6 %segment_backward.1 = (f32[1024,768]{1,0:T(8,128)}, bf16[1024,768]{1,0:T(8,128)(2,1)}, f32[96,768]{1,0:T(8,128)}, f32[96,768]{1,0:T(8,128)}, f32[96,768]{1,0:T(8,128)}, /*index=5*/f32[2,8,128]{2,1,0:T(8,128)}) custom-call(bf16[1024,2304]{1,0:T(8,128)(2,1)} %get-tuple-element.66.refs_0_, f32[1024,768]{1,0:T(8,128)} %get-tuple-element.67.refs_1_, ...), custom_call_target="tpu_custom_call" | custom-call | tf_op jit(solution)/shard_map/segment_backward/pallas_call | solution.py:1147
  308.0 0.0 copy-start.7
  308.0 0.0 copy-start.1
  308.0 0.0 copy-done.2
  308.0 0.0 copy-done.3
  308.0 0.0 copy-start
  308.1 2.3 maximum_bitcast_fusion
  310.3 0.9 slice_bitcast_fusion.1
  311.2 0.0 copy-done.5
  311.2 0.7 maximum_bitcast_fusion.2
  311.9 0.9 slice_bitcast_fusion
  312.9 0.0 copy-done.4
  312.9 0.8 maximum_bitcast_fusion.1
  313.7 0.0 copy-done.7
  313.7 0.6 fusion
  314.3 0.6 fusion.1
  314.8 0.6 slice.25
  315.4 0.6 slice.28
  316.0 0.0 copy-done.1
  316.0 1.1 copy.31
  317.1 0.0 copy-done
  317.1 0.0 copy-start.6
  317.1 1.7 copy.32
  318.8 0.0 copy-done.6
  318.8 0.6 copy.33
Async XLA Ops:
  89.1 90.9 %copy-start.8 = (s32[256]{0:T(256)S(1)}, s32[256]{0:T(256)}, u32[]{:S(2)}) copy-start(s32[256]{0:T(256)} %param.16) | copy-start | bytes 3076
  230.4 77.6 %copy-start.2 = (f32[96,768]{1,0:T(8,128)S(1)}, f32[96,768]{1,0:T(8,128)}, u32[]{:S(2)}) copy-start(f32[96,768]{1,0:T(8,128)} %get-tuple-element.95) | copy-start | bytes 884740
  230.4 77.6 %copy-start.3 = (f32[96,768]{1,0:T(8,128)S(1)}, f32[96,768]{1,0:T(8,128)}, u32[]{:S(2)}) copy-start(f32[96,768]{1,0:T(8,128)} %get-tuple-element.97) | copy-start | bytes 884740
  230.4 80.8 %copy-start.5 = (f32[24,768]{1,0:T(8,128)S(1)}, f32[24,768]{1,0:T(8,128)}, u32[]{:S(2)}) copy-start(f32[24,768]{1,0:T(8,128)} %get-tuple-element.93) | copy-start | bytes 221188
  230.4 82.4 %copy-start.4 = (f32[72,768]{1,0:T(8,128)S(1)}, f32[72,768]{1,0:T(8,128)}, u32[]{:S(2)}) copy-start(f32[72,768]{1,0:T(8,128)} %get-tuple-element.91) | copy-start | bytes 663556
  308.0 5.7 %copy-start.7 = (f32[2,8,128]{2,1,0:T(8,128)S(1)}, f32[2,8,128]{2,1,0:T(8,128)}, u32[]{:S(2)}) copy-start(f32[2,8,128]{2,1,0:T(8,128)} %get-tuple-element.92) | copy-start | bytes 24580
  308.0 7.9 %copy-start.1 = (bf16[1024,768]{1,0:T(8,128)(2,1)S(1)}, bf16[1024,768]{1,0:T(8,128)(2,1)}, u32[]{:S(2)}) copy-start(bf16[1024,768]{1,0:T(8,128)(2,1)} %get-tuple-element.88) | copy-start | bytes 4718596
  308.0 9.1 %copy-start = (f32[1024,768]{1,0:T(8,128)S(1)}, f32[1024,768]{1,0:T(8,128)}, u32[]{:S(2)}) copy-start(f32[1024,768]{1,0:T(8,128)} %get-tuple-element.89) | copy-start | bytes 9437188
  317.1 1.7 copy-start.6
